TPU v7x, 32 devices: a whole 2x2x4 slice. The times are simulated.
32 devices in a mesh: dp: 8 (over z, y), tensor: 4 (over x, core).
Axes of the slice: x: 2, y: 2, z: 4, core: 2. Of those that a mesh axis runs over, the one named last changes fastest.
Arguments:
- tokens: bfloat16 [24, 1024, 1024], P(None, 'dp', 'tensor'), may hold values from -6 to 6
- cotangent: bfloat16 [24, 1024, 1024], P(None, 'dp', 'tensor'), may hold values from -6 to 6
- lengths: int32 [24], replicated, may hold values from 512 to 1024, as said below
- packing: int32 [24], replicated, may hold values from 0 to 23, as said below
- pre_gain: bfloat16 [2, 1024], P(None, 'dp'), may hold values from 0.099609375 to 1.8984375
- w_z: bfloat16 [2, 1024, 2048], P(None, 'dp', 'tensor'), may hold values from -0.1875 to 0.1875
- w_x: bfloat16 [2, 1024, 2048], P(None, 'dp', 'tensor'), may hold values from -0.1875 to 0.1875
- w_bc: bfloat16 [2, 1024, 256], P(None, 'dp'), may hold values from -0.1875 to 0.1875
- w_dt: bfloat16 [2, 1024, 32], P(None, 'dp', 'tensor'), may hold values from -0.1875 to 0.1875
- conv_x: bfloat16 [2, 5, 2048], P(None, None, 'tensor'), may hold values from -3 to 3
- conv_bc: bfloat16 [2, 5, 256], replicated, may hold values from -3 to 3
- head_params: float32 [2, 3, 32], P(None, None, 'tensor'), may hold values from -6.9 to 2.77, as said below
- norm_gain: bfloat16 [2, 2048], P(None, 'tensor'), may hold values from 0.099609375 to 1.8984375
- w_out: bfloat16 [2, 2048, 1024], P(None, 'tensor', 'dp'), may hold values from -0.125 to 0.125
Outputs:
- activations: bfloat16 [24, 1024, 1024], P(None, 'dp', 'tensor')
- input_grad: bfloat16 [24, 1024, 1024], P(None, 'dp', 'tensor')
- grad_pre_gain: float32 [2, 1024], P(None, 'dp')
- grad_w_z: float32 [2, 1024, 2048], P(None, 'dp', 'tensor')
- grad_w_x: float32 [2, 1024, 2048], P(None, 'dp', 'tensor')
- grad_w_bc: float32 [2, 1024, 256], P(None, 'dp')
- grad_w_dt: float32 [2, 1024, 32], P(None, 'dp', 'tensor')
- grad_conv_x: float32 [2, 5, 2048], P(None, None, 'tensor')
- grad_conv_bc: float32 [2, 5, 256], replicated
- grad_head_params: float32 [2, 3, 32], P(None, None, 'tensor')
- grad_norm_gain: float32 [2, 2048], P(None, 'tensor')
- grad_w_out: float32 [2, 2048, 1024], P(None, 'tensor', 'dp')
Inputs may be any that keep to these rules, and one draw needn't show every extreme that they name: Each value is a whole number; in every bin the three lengths add up to 2048. `packing`: A permutation of the 24 sequences. `head_params`: row 0 lies in -6.9 to -2.3, row 1 in 0 to 2.77, row 2 in 0.5 to 1.5.
All inputs are finite; a program needn't handle non-finite values.
Results may differ from a plain program's by a relative error of at most 0.02.
Values may be sent and summed in bfloat16 or wider, within the bound.
A program may use at most 256 MiB of HBM per device.

v0:
```python
import jax
import jax.numpy as jnp
from jax import lax
from jax.sharding import PartitionSpec as P

INNER = 2048
HEADS = 32
STATE = 128
CONV = 4
SCAN_BLOCK = 256
LAYERS = 2
BIN = 2048


eps = 1e-05
high_precision = lax.Precision.HIGH


def causal_conv(values, conv_taps, segment):
    row_count = values.shape[0]
    running = jnp.broadcast_to(conv_taps[CONV], values.shape)
    for delay_step in range(CONV):
        shifted = jnp.pad(values, ((delay_step, 0), (0, 0)))[:row_count]
        earlier = jnp.pad(segment, (delay_step, 0), constant_values=-1)[:row_count]
        running = running + conv_taps[CONV - 1 - delay_step] * jnp.where(
            (earlier == segment)[:, None], shifted, 0.0
        )
    return running


def state_space(inputs, step_sizes, decay_rates, b_rows, c_rows, segment):
    row_count, heads_here, head_dim = inputs.shape
    blocks = row_count // SCAN_BLOCK
    log_decay = step_sizes * decay_rates[None, :]
    seg_blocks = segment.reshape(blocks, SCAN_BLOCK)
    previous = jnp.concatenate([jnp.full((1,), -1, jnp.int32), seg_blocks[:-1, -1]])

    def one_block(state, block_data):
        x_blk, dt_blk, a_blk, b_blk, c_blk, s_blk, prior_seg = block_data
        cumulative = jnp.cumsum(a_blk, axis=0)
        positions = jnp.arange(SCAN_BLOCK)
        allowed = (s_blk[:, None] == s_blk[None, :]) & (positions[:, None] >= positions[None, :])
        log_gaps = jnp.where(
            allowed[:, :, None], cumulative[:, None, :] - cumulative[None, :, :], 0.0
        )
        decays = jnp.where(allowed[:, :, None], jnp.exp(log_gaps), 0.0)
        scores = jnp.dot(c_blk, b_blk.T, precision=high_precision)
        coupling = decays * scores[:, :, None] * dt_blk[None, :, :]
        inside = jnp.einsum("pqh,qhd->phd", coupling, x_blk, precision=high_precision)
        entering = jnp.where((s_blk == prior_seg)[:, None], jnp.exp(cumulative), 0.0)
        carried = (
            jnp.einsum("pn,hdn->phd", c_blk, state, precision=high_precision) * entering[:, :, None]
        )
        final_log = cumulative[-1]
        tail_weight = (
            jnp.where((s_blk == s_blk[-1])[:, None], jnp.exp(final_log[None, :] - cumulative), 0.0)
            * dt_blk
        )
        retained = jnp.where(s_blk[-1] == prior_seg, jnp.exp(final_log), 0.0)
        new_state = state * retained[:, None, None] + jnp.einsum(
            "qh,qhd,qn->hdn", tail_weight, x_blk, b_blk, precision=high_precision
        )
        return (new_state, inside + carried)

    blocked = (
        inputs.reshape(blocks, SCAN_BLOCK, heads_here, head_dim),
        step_sizes.reshape(blocks, SCAN_BLOCK, heads_here),
        log_decay.reshape(blocks, SCAN_BLOCK, heads_here),
        b_rows.reshape(blocks, SCAN_BLOCK, -1),
        c_rows.reshape(blocks, SCAN_BLOCK, -1),
        seg_blocks,
        previous,
    )
    start_state = jnp.zeros((heads_here, head_dim, b_rows.shape[1]), jnp.float32)
    end_state, outputs = lax.scan(jax.checkpoint(one_block), start_state, blocked)
    return outputs.reshape(row_count, heads_here, head_dim)


def core_piece(inputs, b_rows, c_rows, gate_in, dt_raw, head_part, segment):
    row_count, inner_part = inputs.shape
    heads_here = head_part.shape[1]
    step_sizes = jax.nn.softplus(dt_raw + head_part[0])
    decay_rates = -jnp.exp(head_part[1])
    shaped = inputs.reshape(row_count, heads_here, inner_part // heads_here)
    mixed_out = (
        state_space(shaped, step_sizes, decay_rates, b_rows, c_rows, segment)
        + head_part[2][None, :, None] * shaped
    )
    return mixed_out.reshape(row_count, inner_part) * jax.nn.silu(gate_in)


def pre_norm(hidden, gain_full):
    return hidden * lax.rsqrt(jnp.mean(hidden * hidden, axis=-1, keepdims=True) + eps) * gain_full


def post_scale(gated_out, squares, gain_part):
    return gated_out * lax.rsqrt(squares / INNER + eps)[:, None] * gain_part


def rounded(values):
    return lax.optimization_barrier(values.astype(jnp.bfloat16)).astype(jnp.float32)


def contract_rows(left_side, right_side):
    return lax.dot_general(
        left_side, right_side, (((0,), (0,)), ((), ())), preferred_element_type=jnp.float32
    )


def contract_cols(left_side, right_side):
    return lax.dot_general(
        left_side, right_side, (((1,), (1,)), ((), ())), preferred_element_type=jnp.float32
    )


def on_device(
    tokens,
    cotangent,
    lengths,
    packing,
    pre_gain,
    w_z,
    w_x,
    w_bc,
    w_dt,
    conv_x,
    conv_bc,
    head_params,
    norm_gain,
    w_out,
):
    dp_count = lax.axis_size("dp")
    bin_index = lax.axis_index("dp")
    part_index = lax.axis_index("tensor")
    seq_total, pos_here, cols_here = tokens.shape
    inner_part = conv_x.shape[2]
    heads_here = head_params.shape[2]
    dp_rows = w_z.shape[1]
    conv_cols = 2 * inner_part + 2 * STATE
    triples = lengths[packing].reshape(dp_count, 3)
    offsets = jnp.cumsum(triples, axis=1) - triples
    my_offsets = offsets[bin_index]
    my_lengths = triples[bin_index]
    bin_rows = jnp.arange(BIN, dtype=jnp.int32)
    segment = (bin_rows >= my_offsets[1]).astype(jnp.int32) + (bin_rows >= my_offsets[2]).astype(
        jnp.int32
    )
    seg_start = jnp.where(
        segment == 0, my_offsets[0], jnp.where(segment == 1, my_offsets[1], my_offsets[2])
    )
    within = bin_rows - seg_start
    pick_rows = (within // pos_here * 3 + segment) * pos_here + within % pos_here
    groups = packing.reshape(dp_count, 3)
    arrived = (
        lax.all_to_all(tokens[groups], "dp", split_axis=0, concat_axis=0, tiled=True),
        lax.all_to_all(cotangent[groups], "dp", split_axis=0, concat_axis=0, tiled=True),
    )
    flat_tokens = arrived[0].reshape(-1, cols_here)[pick_rows]
    flat_cot = arrived[1].reshape(-1, cols_here)[pick_rows]
    row_tokens, row_cot = (
        lax.all_to_all(flat_tokens, "tensor", split_axis=0, concat_axis=1, tiled=True),
        lax.all_to_all(flat_cot, "tensor", split_axis=0, concat_axis=1, tiled=True),
    )

    def forward_layer(hidden, gathered, conv_part, conv_shared, head_part, gain_part):
        full_z, full_x, full_bc, full_dt, out_part, gain_full = gathered
        weights_cat = jnp.concatenate([full_z, full_x, full_bc, full_dt], axis=1)
        normed, norm_back = jax.vjp(pre_norm, hidden, gain_full.astype(jnp.float32))
        normed_low = normed.astype(jnp.bfloat16)
        shard_rows = lax.all_gather(normed_low, "tensor", axis=0, tiled=True)
        product = jnp.dot(shard_rows, weights_cat, preferred_element_type=jnp.float32)
        conv_taps = jnp.concatenate([conv_part, conv_shared], axis=1).astype(jnp.float32)

        def convolve(mixed_in, taps_in):
            return jax.nn.silu(causal_conv(mixed_in, taps_in, segment))

        conv_out, conv_back = jax.vjp(convolve, product[:, inner_part:conv_cols], conv_taps)
        inputs = rounded(conv_out[:, :inner_part])
        b_rows = rounded(conv_out[:, inner_part : inner_part + STATE])
        c_rows = rounded(conv_out[:, inner_part + STATE :])

        def mixing(inputs_in, b_in, c_in, gate_in, dt_raw, head_vals):
            return core_piece(inputs_in, b_in, c_in, gate_in, dt_raw, head_vals, segment)

        gated_out, core_back = jax.vjp(
            mixing,
            inputs,
            b_rows,
            c_rows,
            product[:, :inner_part],
            product[:, conv_cols:],
            head_part,
        )
        squares = lax.psum(jnp.sum(gated_out * gated_out, axis=-1), "tensor")
        scaled, post_back = jax.vjp(post_scale, gated_out, squares, gain_part.astype(jnp.float32))
        scaled_low = scaled.astype(jnp.bfloat16)
        branch = lax.psum_scatter(
            jnp.dot(scaled_low, out_part, preferred_element_type=jnp.float32).astype(jnp.bfloat16),
            "tensor",
            scatter_dimension=0,
            tiled=True,
        ).astype(jnp.float32)
        record = (norm_back, shard_rows, conv_back, gated_out, core_back, post_back, scaled_low)
        return (hidden + branch, record)

    hidden = row_tokens.astype(jnp.float32)
    records = []
    for layer_index in range(LAYERS):
        gathered = (
            lax.all_gather(w_z[layer_index], "dp", axis=0, tiled=True),
            lax.all_gather(w_x[layer_index], "dp", axis=0, tiled=True),
            lax.all_gather(w_bc[layer_index], "dp", axis=0, tiled=True),
            lax.all_gather(w_dt[layer_index], "dp", axis=0, tiled=True),
            lax.all_gather(w_out[layer_index], "dp", axis=1, tiled=True),
            lax.all_gather(pre_gain[layer_index], "dp", axis=0, tiled=True),
        )
        hidden, record = forward_layer(
            hidden,
            gathered,
            conv_x[layer_index],
            conv_bc[layer_index],
            head_params[layer_index],
            norm_gain[layer_index],
        )
        records.append((gathered, record))
    final_rows = hidden.astype(jnp.bfloat16)
    grad_hidden = row_cot.astype(jnp.float32)
    collected = [None] * LAYERS
    for layer_index in reversed(range(LAYERS)):
        gathered, record = records[layer_index]
        (
            backward_full_z,
            backward_full_x,
            backward_full_bc,
            backward_full_dt,
            backward_out_part,
            backward_gain_full,
        ) = gathered
        backward_weights_cat = jnp.concatenate(
            [backward_full_z, backward_full_x, backward_full_bc, backward_full_dt], axis=1
        )
        (
            backward_norm_back,
            backward_whole_rows,
            backward_conv_back,
            backward_gated_out,
            backward_core_back,
            backward_post_back,
            backward_scaled_low,
        ) = record
        grad_low = grad_hidden.astype(jnp.bfloat16)
        spread_shard_rows = lax.all_gather(grad_low, "tensor", axis=0, tiled=True)
        spread_product = contract_cols(spread_shard_rows, backward_out_part)
        wout_acc = contract_rows(backward_scaled_low, spread_shard_rows)
        grad_gated, grad_squares, grad_gain_part = backward_post_back(spread_product)
        total_squares = lax.psum(grad_squares, "tensor")
        grad_gated = grad_gated + 2.0 * backward_gated_out * total_squares[:, None]
        grad_inputs, grad_b, grad_c, grad_gate, grad_dt, grad_head = backward_core_back(grad_gated)
        grad_mixed, grad_taps = backward_conv_back(
            jnp.concatenate([grad_inputs, grad_b, grad_c], axis=1)
        )
        grad_proj = jnp.concatenate([grad_gate, grad_mixed, grad_dt], axis=1).astype(jnp.bfloat16)
        grad_cat = contract_rows(backward_whole_rows, grad_proj)
        grad_normed = lax.psum_scatter(
            contract_cols(grad_proj, backward_weights_cat).astype(jnp.bfloat16),
            "tensor",
            scatter_dimension=0,
            tiled=True,
        ).astype(jnp.float32)
        grad_before, grad_gain_full = backward_norm_back(grad_normed)
        grad_hidden, collected[layer_index] = (
            grad_hidden + grad_before,
            (grad_cat, wout_acc, grad_gain_full, grad_taps, grad_head, grad_gain_part),
        )
    grad_cat_all = jnp.stack([item[0] for item in collected])
    grad_out_all = jnp.stack([item[1] for item in collected])
    grad_pre_all = jnp.stack([item[2] for item in collected])
    grad_taps_all = jnp.stack([item[3] for item in collected])
    grad_head_all = jnp.stack([item[4] for item in collected])
    grad_norm_all = jnp.stack([item[5] for item in collected])
    shard_z, shard_x, shard_dt, shard_out = (
        lax.psum_scatter(grad_cat_all[:, :, :inner_part], "dp", scatter_dimension=1, tiled=True),
        lax.psum_scatter(
            grad_cat_all[:, :, inner_part : 2 * inner_part], "dp", scatter_dimension=1, tiled=True
        ),
        lax.psum_scatter(grad_cat_all[:, :, conv_cols:], "dp", scatter_dimension=1, tiled=True),
        lax.psum_scatter(grad_out_all, "dp", scatter_dimension=2, tiled=True),
    )
    conv_x_full = lax.dynamic_update_slice_in_dim(
        jnp.zeros((LAYERS, CONV + 1, INNER), jnp.float32),
        grad_taps_all[:, :, :inner_part],
        part_index * inner_part,
        2,
    )
    head_full = lax.dynamic_update_slice_in_dim(
        jnp.zeros((LAYERS, 3, HEADS), jnp.float32), grad_head_all, part_index * heads_here, 2
    )
    norm_full = lax.dynamic_update_slice_in_dim(
        jnp.zeros((LAYERS, INNER), jnp.float32), grad_norm_all, part_index * inner_part, 1
    )
    summed = lax.psum(
        (
            grad_cat_all[:, :, 2 * inner_part : conv_cols],
            grad_pre_all,
            conv_x_full,
            grad_taps_all[:, :, inner_part:],
            head_full,
            norm_full,
        ),
        ("dp", "tensor"),
    )
    shard_bc = lax.dynamic_slice_in_dim(summed[0], bin_index * dp_rows, dp_rows, 1)
    shard_pre = lax.dynamic_slice_in_dim(summed[1], bin_index * dp_rows, dp_rows, 1)
    shard_convx = lax.dynamic_slice_in_dim(summed[2], part_index * inner_part, inner_part, 2)
    shard_head = lax.dynamic_slice_in_dim(summed[4], part_index * heads_here, heads_here, 2)
    shard_norm = lax.dynamic_slice_in_dim(summed[5], part_index * inner_part, inner_part, 1)
    back_cols = (
        lax.all_to_all(final_rows, "tensor", split_axis=1, concat_axis=0, tiled=True),
        lax.all_to_all(
            grad_hidden.astype(jnp.bfloat16), "tensor", split_axis=1, concat_axis=0, tiled=True
        ),
    )
    dev_grid = jnp.arange(dp_count, dtype=jnp.int32)[:, None, None]
    pos_grid = jnp.arange(pos_here, dtype=jnp.int32)[None, None, :]
    seq_pos = dev_grid * pos_here + pos_grid
    live_slot = (seq_pos < my_lengths[None, :, None]).reshape(-1, 1)
    source = jnp.minimum(my_offsets[None, :, None] + seq_pos, BIN - 1).reshape(-1)
    slot_out = jnp.where(live_slot, back_cols[0][source], 0).reshape(
        dp_count, 3, pos_here, cols_here
    )
    slot_grad = jnp.where(live_slot, back_cols[1][source], 0).reshape(
        dp_count, 3, pos_here, cols_here
    )
    returned = (
        lax.all_to_all(slot_out, "dp", split_axis=0, concat_axis=0, tiled=True),
        lax.all_to_all(slot_grad, "dp", split_axis=0, concat_axis=0, tiled=True),
    )
    rank_of = jnp.zeros_like(packing).at[packing].set(jnp.arange(seq_total, dtype=jnp.int32))
    activations = returned[0].reshape(seq_total, pos_here, cols_here)[rank_of]
    input_grad = returned[1].reshape(seq_total, pos_here, cols_here)[rank_of]
    return (
        activations,
        input_grad,
        shard_pre,
        shard_z,
        shard_x,
        shard_bc,
        shard_dt,
        shard_convx,
        summed[3],
        shard_head,
        shard_norm,
        shard_out,
    )


def solution(mesh):
    placed = (
        P(None, "dp", "tensor"),
        P(None, "dp", "tensor"),
        P(),
        P(),
        P(None, "dp"),
        P(None, "dp", "tensor"),
        P(None, "dp", "tensor"),
        P(None, "dp", None),
        P(None, "dp", "tensor"),
        P(None, None, "tensor"),
        P(),
        P(None, None, "tensor"),
        P(None, "tensor"),
        P(None, "tensor", "dp"),
    )
    return jax.shard_map(
        on_device,
        mesh=mesh,
        in_specs=placed,
        out_specs=(
            P(None, "dp", "tensor"),
            P(None, "dp", "tensor"),
            P(None, "dp"),
            P(None, "dp", "tensor"),
            P(None, "dp", "tensor"),
            P(None, "dp", None),
            P(None, "dp", "tensor"),
            P(None, None, "tensor"),
            P(),
            P(None, None, "tensor"),
            P(None, "tensor"),
            P(None, "tensor", "dp"),
        ),
        check_vma=False,
    )
```

profile of v0, /device:TPU:1, one launch (start us, length us, event | category | flops | bytes accessed | tf_op | source)
XLA Modules:
  0.0 2296.0 jit_solution(12393447698526090900)
XLA Ops:
  23.2 42.7 %all-to-all-done = bf16[8,3,128,256]{3,2,1,0:T(8,128)(2,1)S(1)} async-done(((bf16[8,3,128,256]{3,2,1,0:T(8,128)(2,1)}), bf16[8,3,128,256]{3,2,1,0:T(8,128)(2,1)S(1)}, u32[]{:S(2)}, u32[]{:S(2)}) %all-to-all-start) | async-done | bytes 1572896 | tf_op jit(solution)/shard_map/all_to_all | solution.py:155
  81.8 14.8 all-gather
  103.1 26.0 %all-gather.3 = bf16[1,1024,256]{2,1,0:T(8,128)(2,1)S(1)} all-gather(bf16[1,128,256]{2,1,0:T(8,128)(2,1)S(1)} %get-tuple-element.1762), channel_id=5, replica_groups=mesh['dp'=8,'tensor'=4] {'dp'}, dimensions={1}, use_global_device_ids=true | all-gather | bytes 589824 | tf_op jit(solution)/shard_map/all_gather | solution.py:212
  129.2 21.4 all-gather.4
  186.7 205.8 %while.84 = (s32[]{:T(128)}, f32[8,64,128]{2,1,0:T(8,128)S(1)}, f32[8,256,8,64]{1,0,3,2:T(8,128)}, f32[8,8,64,128]{3,2,1,0:T(8,128)}, s32[8,256]{1,0:T(8,128)S(1...) while((s32[]{:T(128)}, f32[8,64,128]{2,1,0:T(8,128)S(1)}, ...), condition=%wide.region_5.7_spmd.clone, body=%wide.region_2.6_spmd.clone.sunk | while | flops 456794656 | bytes 7349639 | solution.py:75
  196.1 12.7 dynamic_update_slice.171
  221.8 12.7 dynamic_update_slice.171
  247.5 12.7 dynamic_update_slice.171
  403.1 19.3 psum.70
  443.7 28.1 %reduce-scatter.9.cloned.1.call-done = bf16[512,1024]{1,0:T(8,128)(2,1)} async-done(((bf16[2048,1024]{1,0:T(8,128)(2,1)}), bf16[512,1024]{1,0:T(8,128)(2,1)}) %reduce-scatter.9.cloned.1.call-update) | async-done | bytes 1048592 | tf_op jit(solution)/shard_map/reduce_scatter | solution.py:197
  485.2 46.8 %all-to-all-done.4 = bf16[8,3,128,256]{3,2,1,0:T(8,128)(2,1)S(1)} async-done(((bf16[8,3,128,256]{3,2,1,0:T(8,128)(2,1)}), bf16[8,3,128,256]{3,2,1,0:T(8,128)(2,1)S(1)}, u32[]{:S(2)}, u32[]{:S(2)}) %all-to-all-start.4) | async-done | bytes 1572896 | tf_op jit(solution)/shard_map/all_to_all | solution.py:156
  546.2 21.5 all-gather.10
  568.1 25.5 %all-gather.9 = bf16[1,1024,256]{2,1,0:T(8,128)(2,1)S(1)} all-gather(bf16[1,128,256]{2,1,0:T(8,128)(2,1)S(1)} %get-tuple-element.1761), channel_id=11, replica_groups=mesh['dp'=8,'tensor'=4] {'dp'}, dimensions={1}, use_global_device_ids=true | all-gather | bytes 589824 | tf_op jit(solution)/shard_map/all_gather | solution.py:212
  594.9 14.4 all-gather.25.cloned.1.call-done
  644.8 205.8 %while.85 = (s32[]{:T(128)}, f32[8,64,128]{2,1,0:T(8,128)S(1)}, f32[8,256,8,64]{1,0,3,2:T(8,128)}, f32[8,8,64,128]{3,2,1,0:T(8,128)}, s32[8,256]{1,0:T(8,128)S(1...) while((s32[]{:T(128)}, f32[8,64,128]{2,1,0:T(8,128)S(1)}, ...), condition=%wide.region_13.15_spmd.clone, body=%wide.region_10.14_spmd.clone.sunk | while | flops 456794656 | bytes 7349639 | solution.py:75
  654.2 12.8 dynamic_update_slice.173
  899.9 286.9 %while.86 = (s32[]{:T(128)}, f32[8,64,128]{2,1,0:T(8,128)S(1)}, f32[8,256,8,64]{1,0,3,2:T(8,128)}, f32[8,256,8]{1,2,0:T(8,128)S(1)}, f32[8,256,8]{1,2,0:T(8,128)...) while((s32[]{:T(128)}, f32[8,64,128]{2,1,0:T(8,128)S(1)}, ...), condition=%wide.region_32.34_spmd.clone, body=%wide.region_20.33_spmd.clone.sunk | while | flops 1069718016 | bytes 18498860 | solution.py:75
  1223.4 45.9 %reduce-scatter.13.cloned.1.call-done = bf16[512,1024]{1,0:T(8,128)(2,1)} async-done(((bf16[2048,1024]{1,0:T(8,128)(2,1)}), bf16[512,1024]{1,0:T(8,128)(2,1)}) %reduce-scatter.13.cloned.1.call-update) | async-done | bytes 1048592 | tf_op jit(solution)/shard_map/reduce_scatter | solution.py:264
  1274.1 35.0 %all-gather.29.cloned.1.call-done = bf16[2048,1024]{1,0:T(8,128)(2,1)} async-done(((bf16[512,1024]{1,0:T(8,128)(2,1)}), bf16[2048,1024]{1,0:T(8,128)(2,1)}) %all-gather.29.cloned.1.call-update) | async-done | bytes 4194320 | tf_op jit(solution)/shard_map/all_gather | solution.py:252
  1341.7 293.6 %while.87 = (s32[]{:T(128)}, f32[8,64,128]{2,1,0:T(8,128)S(1)}, f32[8,256,8,64]{1,0,3,2:T(8,128)}, f32[8,256,8]{1,2,0:T(8,128)S(1)}, f32[8,256,8]{1,2,0:T(8,128)...) while((s32[]{:T(128)}, f32[8,64,128]{2,1,0:T(8,128)S(1)}, ...), condition=%wide.region_49.51_spmd.clone, body=%wide.region_37.50_spmd.clone.sunk | while | flops 1069718016 | bytes 18498860 | solution.py:75
  1642.9 34.6 %multiply_reduce_fusion.13 = (f32[768]{0:T(1024)}, f32[768]{0:T(1024)}, f32[768]{0:T(1024)}, f32[768]{0:T(1024)}, f32[768]{0:T(1024)}, /*index=5*/f32[768]{0:T(1...) fusion(f32[2048,768]{0,1:T(8,128)} %copy-done.7, ...), kind=kLoop, calls=%fused_computation.325 | loop fusion | flops 55042560 | bytes 50368512 | tf_op jit(solution)/shard_map/transpose(jvp())/reduce_sum | solution.py:25
  1759.6 35.8 %reduce-scatter.11.cloned.1.call-done = bf16[512,1024]{1,0:T(8,128)(2,1)} async-done(((bf16[2048,1024]{1,0:T(8,128)(2,1)}), bf16[512,1024]{1,0:T(8,128)(2,1)}) %reduce-scatter.11.cloned.1.call-update) | async-done | bytes 1048592 | tf_op jit(solution)/shard_map/reduce_scatter | solution.py:197
  1806.6 16.0 all-to-all-done.2
  1827.1 13.0 gather_fusion.3
  1841.4 13.0 gather_fusion.7
  1857.5 42.8 %all_to_all.90 = bf16[8,3,128,256]{3,2,1,0:T(8,128)(2,1)} all-to-all(bf16[8,3,128,256]{3,2,1,0:T(8,128)(2,1)S(1)} %get-tuple-element.1770), channel_id=1, replica_groups=mesh['dp'=8,'tensor'=4] {'dp'}, dimensions={0} | all-to-all | bytes 3145728 | tf_op jit(solution)/shard_map/all_to_all | solution.py:336
  1907.3 48.5 %all-reduce.37.cloned.1.call-done = (f32[2,1024,256]{1,2,0:T(8,128)}, f32[2,5,2048]{2,0,1:T(2,128)}) async-done(((f32[2,1024,256]{1,2,0:T(8,128)}, f32[2,5,2048]{2,0,1:T(2,128)}), (f32[2,1024,256]{1,2,0:T(8,128)}, f32[2,5,2048]{2,0,1:T(2,128)})) %all-reduce.37.cloned.1.call-update) | async-done | bytes 2179088 | tf_op jit(solution)/shard_map/psum | solution.py:301
  1959.0 43.2 %all-reduce.33 = (f32[2,1024]{1,0:T(2,128)S(1)}, f32[2,5,256]{2,1,0:T(8,128)S(1)}, f32[2,3,32]{2,0,1:T(2,128)S(1)}, f32[2,2048]{1,0:T(2,128)S(1)}) all-reduce(f32[2,1024]{1,0:T(2,128)S(1)} %pad_maximum_fusion.17, f32[2,5,256]{2,1,0:T(8,128)S(1)} %pad_maximum_fusion.16, ...), channel_id=1, replica_groups=mesh['dp'=8,'tensor'=4] {'dp','tensor'}, use_global_device_ids=true, to_apply=%region_54.56 | all-reduce | flops 8896 | bytes 71168 | tf_op jit(solution)/shard_map/psum | solution.py:301
  2002.8 45.0 %reduce-scatter.17.cloned.1.call-done = f32[2,128,512]{1,2,0:T(8,128)} async-done(((f32[2,1024,512]{1,2,0:T(8,128)}), f32[2,128,512]{1,2,0:T(8,128)}) %reduce-scatter.17.cloned.1.call-update) | async-done | bytes 524304 | tf_op jit(solution)/shard_map/reduce_scatter | solution.py:282
  2049.8 89.7 %reduce-scatter.19.cloned.1.call-done = f32[2,128,512]{1,2,0:T(8,128)} async-done(((f32[2,1024,512]{1,2,0:T(8,128)}), f32[2,128,512]{1,2,0:T(8,128)}) %reduce-scatter.19.cloned.1.call-update) | async-done | bytes 524304 | tf_op jit(solution)/shard_map/reduce_scatter | solution.py:283
  2148.5 46.2 %reduce-scatter.21.cloned.1.call-done = f32[2,128,8]{1,2,0:T(8,128)} async-done(((f32[2,1024,8]{1,2,0:T(8,128)}), f32[2,128,8]{1,2,0:T(8,128)}) %reduce-scatter.21.cloned.1.call-update) | async-done | bytes 8208 | tf_op jit(solution)/shard_map/reduce_scatter | solution.py:286
  2194.6 94.4 %reduce-scatter.23.cloned.1.call-done = f32[2,512,128]{2,1,0:T(8,128)} async-done(((f32[2,512,1024]{2,1,0:T(8,128)}), f32[2,512,128]{2,1,0:T(8,128)}) %reduce-scatter.23.cloned.1.call-update) | async-done | bytes 524304 | tf_op jit(solution)/shard_map/reduce_scatter | solution.py:287
  (1538 shorter events, 1319.5 us)
Async XLA Ops:
  7.2 145.3 %all-gather.31.cloned.1.call-start = ((), (), s32[]{:S(2)}) async-start(), calls=%async_computation.28 | async-start | bytes 1179648 | tf_op jit(solution)/shard_map/all_gather | solution.py:210
  11.8 54.2 %all-to-all-start = ((bf16[8,3,128,256]{3,2,1,0:T(8,128)(2,1)}), bf16[8,3,128,256]{3,2,1,0:T(8,128)(2,1)S(1)}, u32[]{:S(2)}, u32[]{:S(2)}) async-start(bf16[8,3,128,256]{3,2,1,0:T(8,128)(2,1)} %bitcast.1), calls=%async_computation | async-start | bytes 3145728 | tf_op jit(solution)/shard_map/all_to_all | solution.py:155
  18.2 134.4 %all-gather.33.cloned.1.call-start = ((), (), s32[]{:S(2)}) async-start(), calls=%async_computation.29 | async-start | bytes 1179648 | tf_op jit(solution)/shard_map/all_gather | solution.py:211
  75.0 21.6 all-to-all-start.1
  81.3 71.3 %all-gather.23.cloned.1.call-start = ((), (), s32[]{:S(2)}) async-start(), calls=%async_computation.16 | async-start | bytes 5242880 | tf_op jit(solution)/shard_map/all_gather | solution.py:170
  97.1 376.3 %copy-start.3 = (f32[4,64,8,256]{3,2,0,1:T(8,128)}, f32[4,64,8,256]{3,2,0,1:T(8,128)S(1)}, u32[]{:S(2)}) copy-start(f32[4,64,8,256]{3,2,0,1:T(8,128)S(1)} %copy.346) | copy-start | bytes 6291460
  98.8 323.7 %all-gather.35.cloned.1.call-start = ((), (), s32[]{:S(2)}) async-start(), calls=%async_computation.30 | async-start | bytes 1179648 | tf_op jit(solution)/shard_map/all_gather | solution.py:214
  99.5 372.2 %reduce-scatter.9.cloned.1.call-start = ((), (), s32[]{:S(2)}) async-start(), calls=%async_computation.17 | async-start | bytes 5242880 | tf_op jit(solution)/shard_map/reduce_scatter | solution.py:197
  151.8 245.0 %copy-start.73 = (f32[512]{0:T(512)}, f32[512]{0:T(512)S(1)}, u32[]{:S(2)}) copy-start(f32[512]{0:T(512)S(1)} %mul.1213) | copy-start | bytes 6148
  151.8 270.7 %copy-start.92 = (f32[1,512]{1,0:T(1,128)}, f32[1,512]{1,0:T(1,128)S(1)}, u32[]{:S(2)}) copy-start(f32[1,512]{1,0:T(1,128)S(1)} %get-tuple-element.1783) | copy-start | bytes 6148
  151.8 729.7 %copy-start.95 = (f32[1,512]{1,0:T(1,128)}, f32[1,512]{1,0:T(1,128)S(1)}, u32[]{:S(2)}) copy-start(f32[1,512]{1,0:T(1,128)S(1)} %get-tuple-element.1782) | copy-start | bytes 6148
  429.6 165.3 %all-gather.37.cloned.1.call-start = ((), (), s32[]{:S(2)}) async-start(), calls=%async_computation.31 | async-start | bytes 1179648 | tf_op jit(solution)/shard_map/all_gather | solution.py:210
  430.2 164.7 %all-gather.39.cloned.1.call-start = ((), (), s32[]{:S(2)}) async-start(), calls=%async_computation.32 | async-start | bytes 1179648 | tf_op jit(solution)/shard_map/all_gather | solution.py:211
  430.9 178.4 %all-gather.25.cloned.1.call-start = ((), (), s32[]{:S(2)}) async-start(), calls=%async_computation.18 | async-start | bytes 5242880 | tf_op jit(solution)/shard_map/all_gather | solution.py:170
  479.2 52.8 %all-to-all-start.4 = ((bf16[8,3,128,256]{3,2,1,0:T(8,128)(2,1)}), bf16[8,3,128,256]{3,2,1,0:T(8,128)(2,1)S(1)}, u32[]{:S(2)}, u32[]{:S(2)}) async-start(bf16[8,3,128,256]{3,2,1,0:T(8,128)(2,1)} %bitcast.43), calls=%async_computation.6 | async-start | bytes 3145728 | tf_op jit(solution)/shard_map/all_to_all | solution.py:156
  484.4 382.0 %all-gather.41.cloned.1.call-start = ((), (), s32[]{:S(2)}) async-start(), calls=%async_computation.33 | async-start | bytes 1179648 | tf_op jit(solution)/shard_map/all_gather | solution.py:214
  541.0 52.6 %all-to-all-start.5 = ((bf16[4,512,256]{2,1,0:T(8,128)(2,1)}), bf16[4,512,256]{2,1,0:T(8,128)(2,1)S(1)}, u32[]{:S(2)}, u32[]{:S(2)}) async-start(bf16[4,512,256]{2,1,0:T(8,128)(2,1)} %bitcast.45), calls=%async_computation.7 | async-start | bytes 2097152 | tf_op jit(solution)/shard_map/all_to_all | solution.py:162
  546.2 320.2 %all-gather.27.cloned.1.call-start = ((), (), s32[]{:S(2)}) async-start(), calls=%async_computation.20 | async-start | bytes 5242880 | tf_op jit(solution)/shard_map/all_gather | solution.py:252
  594.8 674.5 %reduce-scatter.13.cloned.1.call-start = ((), (), s32[]{:S(2)}) async-start(), calls=%async_computation.21 | async-start | bytes 5242880 | tf_op jit(solution)/shard_map/reduce_scatter | solution.py:264
  1223.2 85.9 %all-gather.29.cloned.1.call-start = ((), (), s32[]{:S(2)}) async-start(), calls=%async_computation.22 | async-start | bytes 5242880 | tf_op jit(solution)/shard_map/all_gather | solution.py:252
  1274.0 481.7 %reduce-scatter.15.cloned.1.call-start = ((), (), s32[]{:S(2)}) async-start(), calls=%async_computation.23 | async-start | bytes 5242880 | tf_op jit(solution)/shard_map/reduce_scatter | solution.py:264
  1702.3 93.1 %reduce-scatter.11.cloned.1.call-start = ((), (), s32[]{:S(2)}) async-start(), calls=%async_computation.19 | async-start | bytes 5242880 | tf_op jit(solution)/shard_map/reduce_scatter | solution.py:197
  1710.3 245.4 %all-reduce.37.cloned.1.call-start = ((), (), s32[]{:S(2)}) async-start(), calls=%async_computation.34 | async-start | bytes 4358144 | tf_op jit(solution)/shard_map/psum | solution.py:301
  1732.0 315.7 %reduce-scatter.17.cloned.1.call-start = ((), (), s32[]{:S(2)}) async-start(), calls=%async_computation.24 | async-start | bytes 4718592 | tf_op jit(solution)/shard_map/reduce_scatter | solution.py:282
  1738.4 401.1 %reduce-scatter.19.cloned.1.call-start = ((), (), s32[]{:S(2)}) async-start(), calls=%async_computation.25 | async-start | bytes 4718592 | tf_op jit(solution)/shard_map/reduce_scatter | solution.py:283
  1739.0 455.6 %reduce-scatter.21.cloned.1.call-start = ((), (), s32[]{:S(2)}) async-start(), calls=%async_computation.26 | async-start | bytes 73728 | tf_op jit(solution)/shard_map/reduce_scatter | solution.py:286
  1747.2 541.8 %reduce-scatter.23.cloned.1.call-start = ((), (), s32[]{:S(2)}) async-start(), calls=%async_computation.27 | async-start | bytes 4718592 | tf_op jit(solution)/shard_map/reduce_scatter | solution.py:287
  1800.5 22.1 all-to-all-start.2
  1822.6 18.8 all-to-all-start.6
  1857.5 101.4 %copy-start.89 = (f32[1024]{0:T(1024)S(1)}, f32[1024]{0:T(1024)}, u32[]{:S(2)}) copy-start(f32[1024]{0:T(1024)} %get-tuple-element.1542) | copy-start | bytes 12292
  1900.3 246.3 %all-to-all-start.3 = ((bf16[8,3,128,256]{3,2,1,0:T(8,128)(2,1)}), bf16[8,3,128,256]{3,2,1,0:T(8,128)(2,1)S(1)}, u32[]{:S(2)}, u32[]{:S(2)}) async-start(bf16[8,3,128,256]{3,2,1,0:T(8,128)(2,1)} %get-tuple-element.1771), calls=%async_computation.5 | async-start | bytes 3145728 | tf_op jit(solution)/shard_map/all_to_all | solution.py:335
  2002.1 286.9 %copy-start.1 = (bf16[24,128,256]{2,1,0:T(8,128)(2,1)S(1)}, bf16[24,128,256]{2,1,0:T(8,128)(2,1)}, u32[]{:S(2)}) copy-start(bf16[24,128,256]{2,1,0:T(8,128)(2,1)} %param.23) | copy-start | bytes 4718596
  (121 other events, 2226.9 us)
Sparse Core Ops, SparseCore 0:
  10.8 58.4 all-gather.30
  71.9 37.6 all-gather.32
  111.8 34.1 all-gather.22
  148.4 36.6 all-gather.34
  429.7 42.0 reduce-scatter.8
  473.9 56.5 all-gather.36
  533.5 38.7 all-gather.38
  574.4 34.7 all-gather.24
  611.5 36.6 all-gather.40
  649.7 36.1 all-gather.26
  1223.3 45.9 reduce-scatter.12
  1274.1 34.8 all-gather.28
  1702.5 45.8 reduce-scatter.14
  1750.9 44.5 reduce-scatter.10
  1801.5 154.2 all-reduce.36
  1959.7 87.9 reduce-scatter.16
  2051.2 88.2 reduce-scatter.18
  2143.4 51.1 reduce-scatter.20
  2199.3 89.7 reduce-scatter.22
where the time goes:
time: 2320 us; the launch traced here: 2300 us
  local copies, waits for them, and re-layouts  729 us (31%)
  waiting for transfers between devices  592 us (26%)
  matrix products  343 us (15%)
  other arithmetic  288 us (12%)
  blocking collectives  244 us (11%)
  loops' own time  45.4 us (2%)
  starting transfers between devices  37.5 us (2%)
    dynamic_update_slice x64, local copies, waits for them, and re-layouts, state_space(): lax.scan(jax.checkpoint(one_block), start_state, blocked)  424 us
    dot_general x48, matrix products, one_block(): jnp.einsum('pqh,qhd->phd', coupling, x_blk, precision=high_precision)  104 us
    reduce_scatter x1, waiting for transfers between devices, on_device(): lax.psum_scatter(grad_out_all, 'dp', scatter_dimension=2, tiled=True)  94.4 us
    another operation x116, other arithmetic  90.2 us
    reduce_scatter x1, waiting for transfers between devices, on_device(): lax.psum_scatter(grad_cat_all[:, :, inner_part:2 * inner_part], 'dp', sca...  89.7 us
    reduce_scatter x2, waiting for transfers between devices, forward_layer(): lax.psum_scatter(jnp.dot(scaled_low, out_part, preferred_element_type=jnp...  63.9 us
    unnamed x272, local copies, waits for them, and re-layouts  62.8 us
    dynamic_slice x80, local copies, waits for them, and re-layouts, state_space(): lax.scan(jax.checkpoint(one_block), start_state, blocked)  60.2 us
  transfers between devices with their start and end apart: 26, of which 14 were waited for; matrix products, arithmetic and copies ran while one was open for 27% of the time, Pallas kernels for 0%

commit v1 on v0

v1 whole, which is shorter than its diff:
```python
import functools
import jax
import jax.numpy as jnp
from jax import lax
from jax.experimental import pallas as pl
from jax.experimental.pallas import tpu as pltpu
from jax.sharding import PartitionSpec as P

CONV = 4
INNER = 2048
LAYERS = 2
BIN = 2048
eps = 1e-05
STATE = 128
BLK = 256
LANES = 128
LOG2E = 1.4426950408889634
F32 = jnp.float32
BF16 = jnp.bfloat16


def dot_nn(left, right):
    return lax.dot_general(left, right, (((1,), (0,)), ((), ())), preferred_element_type=F32)


def dot_nt(left, right):
    return lax.dot_general(left, right, (((1,), (1,)), ((), ())), preferred_element_type=F32)


def dot_tn(left, right):
    return lax.dot_general(left, right, (((0,), (0,)), ((), ())), preferred_element_type=F32)


def split_two(values):
    high = values.astype(BF16)
    return high, (values - high.astype(F32)).astype(BF16)


def split_three(values):
    high = values.astype(BF16)
    rest = values - high.astype(F32)
    middle = rest.astype(BF16)
    return high, middle, (rest - middle.astype(F32)).astype(BF16)


def spread_heads(values, spread):
    high, low = split_two(values)
    return dot_nn(jnp.concatenate([high, low], axis=1), spread)


def gather_heads(values, spread):
    high, low = split_two(values)
    half = spread[:LANES]
    return dot_nt(high, half) + dot_nt(low, half)


def sigmoid(values):
    return 0.5 * jnp.tanh(0.5 * values) + 0.5


def softplus(values):
    return jnp.maximum(values, 0.0) + jnp.log1p(jnp.exp(-jnp.abs(values)))


def segment_of(rows, first, second):
    return (rows >= first).astype(jnp.int32) + (rows >= second).astype(jnp.int32)


def block_frame(block, first, second):
    row_col = block * BLK + lax.broadcasted_iota(jnp.int32, (BLK, 1), 0)
    row_row = block * BLK + lax.broadcasted_iota(jnp.int32, (1, BLK), 1)
    return row_col, row_row, segment_of(row_col, first, second), segment_of(row_row, first, second)


def decay_parts(block, dt_raw, head, seg_col, first, second):
    shifted = dt_raw + head[0:1]
    steps = softplus(shifted)
    log_decay = steps * head[1:2]
    above = lax.broadcasted_iota(jnp.int32, (BLK, BLK), 0)
    below = lax.broadcasted_iota(jnp.int32, (BLK, BLK), 1)
    lower = jnp.where(above >= below, 1.0, 0.0).astype(BF16)
    parts = dot_nn(lower, jnp.concatenate(split_three(log_decay), axis=1))
    cumulative = parts[:, :LANES] + parts[:, LANES : 2 * LANES] + parts[:, 2 * LANES :]
    cum2 = cumulative * LOG2E
    final2 = cum2[BLK - 1 : BLK]
    last_seg = segment_of(block * BLK + BLK - 1, first, second)
    prior_seg = jnp.where(block == 0, -1, segment_of(block * BLK - 1, first, second))
    entering = jnp.where(seg_col == prior_seg, jnp.exp2(cum2), 0.0)
    tail = jnp.where(seg_col == last_seg, jnp.exp2(final2 - cum2), 0.0)
    retained = jnp.where(last_seg == prior_seg, jnp.exp2(final2), 0.0)
    return shifted, steps, cum2, entering, tail, retained


def head_half(pair, head):
    lanes = lax.broadcasted_iota(jnp.int32, pair.shape, 1)
    keep = (lanes < LANES // 2) if head % 2 == 0 else (lanes >= LANES // 2)
    return jnp.where(keep, pair, jnp.zeros_like(pair))


def forward_kernel(
    off_ref, rows_ref, w_ref, taps_ref, head_ref, wide_ref, spread_ref,
    part_ref, sq_ref, z_ref, in_ref, pre_ref, dt_ref, y_ref, gg_ref, st_ref,
    state, padded,
):
    block = pl.program_id(0)
    inner = y_ref.shape[1]
    mixed = in_ref.shape[1]
    first, second = off_ref[0], off_ref[1]

    @pl.when(block == 0)
    def _():
        state[...] = jnp.zeros_like(state)
        padded[pl.ds(0, 8), :] = jnp.zeros((8, mixed), F32)

    row_col, row_row, seg_col, seg_row = block_frame(block, first, second)
    seg_start = jnp.where(seg_col == 0, 0, jnp.where(seg_col == 1, first, second))
    within = row_col - seg_start
    product = dot_nn(rows_ref[...], w_ref[:, inner:])
    gate = product[:, :inner]
    mixed_in = product[:, inner : inner + mixed]
    dt_raw = product[:, inner + mixed :]
    z_ref[...] = gate
    in_ref[...] = mixed_in
    dt_ref[...] = dt_raw
    padded[pl.ds(8, BLK), :] = mixed_in
    taps = taps_ref[...]
    conv = taps[CONV : CONV + 1] + taps[CONV - 1 : CONV] * mixed_in
    for delay in range(1, CONV):
        shifted_in = padded[pl.ds(8 - delay, BLK), :]
        conv = conv + taps[CONV - 1 - delay : CONV - delay] * jnp.where(within >= delay, shifted_in, 0.0)
    padded[pl.ds(0, 8), :] = padded[pl.ds(BLK, 8), :]
    pre_ref[...] = conv
    mixed_low = (conv * sigmoid(conv)).astype(BF16)
    x_low = mixed_low[:, :inner]
    b_low = mixed_low[:, inner : inner + STATE]
    c_low = mixed_low[:, inner + STATE :]
    head = head_ref[...]
    spread = spread_ref[...]
    shifted, steps, cum2, entering, tail, retained = decay_parts(block, dt_raw, head, seg_col, first, second)
    cum_row = jnp.transpose(cum2)
    x_in = x_low.astype(F32)
    x_steps = spread_heads(steps, spread) * x_in
    x_steps_low = x_steps.astype(BF16)
    allowed = (seg_col == seg_row) & (row_col >= row_row)
    scores = jnp.where(allowed, dot_nt(c_low, b_low), 0.0)
    old_state = state[...]
    st_ref[0] = old_state
    carried = spread_heads(entering, spread) * dot_nn(c_low, old_state.astype(BF16))
    wide = wide_ref[...]
    pieces = []
    for pair in range(inner // LANES):
        columns = slice(pair * LANES, (pair + 1) * LANES)
        total = None
        for head_index in (2 * pair, 2 * pair + 1):
            gaps = cum2[:, head_index : head_index + 1] - cum_row[head_index : head_index + 1, :]
            coupling = (jnp.exp2(jnp.minimum(gaps, 0.0)) * scores).astype(BF16)
            term = dot_nn(coupling, head_half(x_steps_low[:, columns], head_index))
            total = term if total is None else total + term
        pieces.append(total)
    mixed_out = jnp.concatenate(pieces, axis=1) + carried + wide[0:1] * x_in
    tailed = (spread_heads(tail, spread) * x_steps).astype(BF16)
    keep = spread_heads(jnp.broadcast_to(retained, (8, LANES)), spread)[0:1]
    state[...] = old_state * keep + dot_tn(b_low, tailed)
    y_ref[...] = mixed_out
    gated = mixed_out * (gate * sigmoid(gate))
    sq_ref[...] = jnp.sum(gated * gated, axis=1, keepdims=True)
    gained = (gated * wide[1:2]).astype(BF16)
    gg_ref[...] = gained
    part_ref[...] = dot_nt(gained, w_ref[:, :inner]).astype(BF16)


def backward_kernel(
    off_ref, sg_ref, g2_ref, w_ref, taps_ref, head_ref, wide_ref, spread_ref,
    z_ref, in_ref, pre_ref, dt_ref, y_ref, st_ref,
    part_ref, gproj_ref, gtaps_ref, ghead_ref, gwide_ref,
    dstate, padded,
):
    step = pl.program_id(0)
    block = pl.num_programs(0) - 1 - step
    inner = y_ref.shape[1]
    mixed = in_ref.shape[1]
    first, second = off_ref[0], off_ref[1]

    @pl.when(step == 0)
    def _():
        dstate[...] = jnp.zeros_like(dstate)
        padded[pl.ds(BLK, 8), :] = jnp.zeros((8, mixed), F32)
        gtaps_ref[...] = jnp.zeros_like(gtaps_ref)
        ghead_ref[...] = jnp.zeros_like(ghead_ref)
        gwide_ref[...] = jnp.zeros_like(gwide_ref)

    row_col, row_row, seg_col, seg_row = block_frame(block, first, second)
    seg_end = jnp.where(seg_col == 0, first, jnp.where(seg_col == 1, second, pl.num_programs(0) * BLK))
    remaining = seg_end - row_col
    head = head_ref[...]
    wide = wide_ref[...]
    spread = spread_ref[...]
    skip, gain = wide[0:1], wide[1:2]
    gate = z_ref[...]
    mixed_out = y_ref[...]
    conv = pre_ref[...]
    gate_sig = sigmoid(gate)
    gate_silu = gate * gate_sig
    gated = mixed_out * gate_silu
    grad_scaled = dot_nn(sg_ref[...], w_ref[:, :inner])
    grad_gated = grad_scaled * gain + g2_ref[...] * gated
    grad_out = grad_gated * gate_silu
    grad_gate = grad_gated * mixed_out * (gate_sig * (1.0 + gate * (1.0 - gate_sig)))
    grad_out_low = grad_out.astype(BF16)

    conv_sig = sigmoid(conv)
    mixed_low = (conv * conv_sig).astype(BF16)
    x_low = mixed_low[:, :inner]
    b_low = mixed_low[:, inner : inner + STATE]
    c_low = mixed_low[:, inner + STATE :]
    x_in = x_low.astype(F32)
    shifted, steps, cum2, entering, tail, retained = decay_parts(block, dt_ref[...], head, seg_col, first, second)
    cum_row = jnp.transpose(cum2)
    steps_wide = spread_heads(steps, spread)
    x_steps_low = (steps_wide * x_in).astype(BF16)
    x_steps = x_steps_low.astype(F32)

    allowed = (seg_col == seg_row) & (row_col <= row_row)
    scores = jnp.where(allowed, dot_nt(b_low, c_low), 0.0)
    grad_scores = jnp.zeros((BLK, BLK), F32)
    pieces = []
    for pair in range(inner // LANES):
        columns = slice(pair * LANES, (pair + 1) * LANES)
        total = None
        for head_index in (2 * pair, 2 * pair + 1):
            gaps = cum_row[head_index : head_index + 1, :] - cum2[:, head_index : head_index + 1]
            decays = jnp.exp2(jnp.minimum(gaps, 0.0))
            coupling = (decays * scores).astype(BF16)
            term = dot_nn(coupling, head_half(grad_out_low[:, columns], head_index))
            total = term if total is None else total + term
            grad_scores = grad_scores + decays * dot_nt(
                head_half(x_steps_low[:, columns], head_index), grad_out_low[:, columns]
            )
        pieces.append(total)
    grad_scores_low = jnp.where(allowed, grad_scores, 0.0).astype(BF16)
    old_dstate = dstate[...]
    old_dstate_low = old_dstate.astype(BF16)
    old_state = st_ref[0]
    tail_wide = spread_heads(tail, spread)
    from_state = tail_wide * dot_nn(b_low, old_dstate_low)
    grad_unit = jnp.concatenate(pieces, axis=1) + from_state
    entered = (spread_heads(entering, spread) * grad_out).astype(BF16)
    tailed = (tail_wide * x_steps).astype(BF16)
    grad_c = dot_tn(grad_scores_low, b_low) + dot_nt(entered, old_state.astype(BF16))
    grad_b = dot_nn(grad_scores_low, c_low) + dot_nt(tailed, old_dstate_low)
    keep = spread_heads(jnp.broadcast_to(retained, (8, LANES)), spread)[0:1]
    dstate[...] = old_dstate * keep + dot_tn(c_low, entered)

    balance = gather_heads(grad_out_low.astype(F32) * (mixed_out - skip * x_in) - x_steps * grad_unit, spread)
    direct = gather_heads(x_in * grad_unit, spread)
    final_wide = jnp.sum(x_steps * from_state, axis=0, keepdims=True) + keep * jnp.sum(
        old_dstate * old_state, axis=0, keepdims=True
    )
    final = gather_heads(jnp.broadcast_to(final_wide, (8, inner)), spread)[0:1]
    above = lax.broadcasted_iota(jnp.int32, (BLK, BLK), 0)
    below = lax.broadcasted_iota(jnp.int32, (BLK, BLK), 1)
    upper = jnp.where(above <= below, 1.0, 0.0).astype(BF16)
    parts = dot_nn(upper, jnp.concatenate(split_three(balance), axis=1))
    grad_log = parts[:, :LANES] + parts[:, LANES : 2 * LANES] + parts[:, 2 * LANES :] + final
    grad_steps = direct + grad_log * head[1:2]
    grad_dt = grad_steps * sigmoid(shifted)
    ghead_ref[0:1, :] += jnp.sum(grad_dt, axis=0, keepdims=True)
    ghead_ref[1:2, :] += jnp.sum(grad_log * steps, axis=0, keepdims=True) * head[1:2]
    gwide_ref[0:1, :] += jnp.sum(grad_out * x_in, axis=0, keepdims=True)
    gwide_ref[1:2, :] += jnp.sum(grad_scaled * gated, axis=0, keepdims=True)

    grad_x = steps_wide * grad_unit + skip * grad_out
    grad_conv = jnp.concatenate([grad_x, grad_b, grad_c], axis=1) * (
        conv_sig * (1.0 + conv * (1.0 - conv_sig))
    )
    padded[pl.ds(0, BLK), :] = grad_conv
    mixed_in = in_ref[...]
    taps = taps_ref[...]
    grad_in = taps[CONV - 1 : CONV] * grad_conv
    gtaps_ref[CONV : CONV + 1, :] += jnp.sum(grad_conv, axis=0, keepdims=True)
    gtaps_ref[CONV - 1 : CONV, :] += jnp.sum(mixed_in * grad_conv, axis=0, keepdims=True)
    for delay in range(1, CONV):
        later = jnp.where(remaining > delay, padded[pl.ds(delay, BLK), :], 0.0)
        grad_in = grad_in + taps[CONV - 1 - delay : CONV - delay] * later
        gtaps_ref[CONV - 1 - delay : CONV - delay, :] += jnp.sum(mixed_in * later, axis=0, keepdims=True)
    padded[pl.ds(BLK, 8), :] = padded[pl.ds(0, 8), :]
    gproj = jnp.concatenate([grad_gate.astype(BF16), grad_in.astype(BF16), grad_dt.astype(BF16)], axis=1)
    gproj_ref[...] = gproj
    part_ref[...] = dot_nt(gproj, w_ref[:, inner:]).astype(BF16)


def whole(shape):
    return pl.BlockSpec(shape, lambda b: (0,) * len(shape))


def layer_forward(offsets, rows, weights, taps, head, wide, spread):
    count, width = rows.shape
    inner, mixed = wide.shape[1], taps.shape[1]
    blocks = count // BLK
    total = weights.shape[1]

    def by_block(columns):
        return pl.BlockSpec((BLK, columns), lambda b: (b, 0))

    return pl.pallas_call(
        forward_kernel,
        grid=(blocks,),
        in_specs=[
            pl.BlockSpec(memory_space=pltpu.SMEM),
            by_block(width), whole((width, total)), whole((8, mixed)), whole((8, LANES)), whole((8, inner)),
            whole((2 * LANES, inner)),
        ],
        out_specs=[
            by_block(width), by_block(1), by_block(inner), by_block(mixed), by_block(mixed),
            by_block(LANES), by_block(inner), by_block(inner),
            pl.BlockSpec((1, STATE, inner), lambda b: (b, 0, 0)),
        ],
        out_shape=[
            jax.ShapeDtypeStruct((count, width), BF16),
            jax.ShapeDtypeStruct((count, 1), F32),
            jax.ShapeDtypeStruct((count, inner), F32),
            jax.ShapeDtypeStruct((count, mixed), F32),
            jax.ShapeDtypeStruct((count, mixed), F32),
            jax.ShapeDtypeStruct((count, LANES), F32),
            jax.ShapeDtypeStruct((count, inner), F32),
            jax.ShapeDtypeStruct((count, inner), BF16),
            jax.ShapeDtypeStruct((blocks, STATE, inner), F32),
        ],
        scratch_shapes=[pltpu.VMEM((STATE, inner), F32), pltpu.VMEM((BLK + 8, mixed), F32)],
        compiler_params=pltpu.CompilerParams(vmem_limit_bytes=48 * 1024 * 1024),
        name="layer_forward",
    )(offsets, rows, weights, taps, head, wide, spread)


def layer_backward(offsets, spread_grad, twice, weights, taps, head, wide, spread, saved):
    gate, mixed_in, conv, dt_raw, mixed_out, states = saved
    count, width = spread_grad.shape
    inner, mixed = wide.shape[1], taps.shape[1]
    blocks = count // BLK
    total = weights.shape[1]

    def by_block(columns):
        return pl.BlockSpec((BLK, columns), lambda b: (blocks - 1 - b, 0))

    return pl.pallas_call(
        backward_kernel,
        grid=(blocks,),
        in_specs=[
            pl.BlockSpec(memory_space=pltpu.SMEM),
            by_block(width), by_block(1), whole((width, total)), whole((8, mixed)), whole((8, LANES)),
            whole((8, inner)), whole((2 * LANES, inner)),
            by_block(inner), by_block(mixed), by_block(mixed), by_block(LANES), by_block(inner),
            pl.BlockSpec((1, STATE, inner), lambda b: (blocks - 1 - b, 0, 0)),
        ],
        out_specs=[
            by_block(width), by_block(total - inner),
            whole((8, mixed)), whole((8, LANES)), whole((8, inner)),
        ],
        out_shape=[
            jax.ShapeDtypeStruct((count, width), BF16),
            jax.ShapeDtypeStruct((count, total - inner), BF16),
            jax.ShapeDtypeStruct((8, mixed), F32),
            jax.ShapeDtypeStruct((8, LANES), F32),
            jax.ShapeDtypeStruct((8, inner), F32),
        ],
        scratch_shapes=[pltpu.VMEM((STATE, inner), F32), pltpu.VMEM((BLK + 8, mixed), F32)],
        compiler_params=pltpu.CompilerParams(vmem_limit_bytes=48 * 1024 * 1024),
        name="layer_backward",
    )(offsets, spread_grad, twice, weights, taps, head, wide, spread, gate, mixed_in, conv, dt_raw, mixed_out, states)


def spread_matrix(inner, heads):
    lane_head = lax.broadcasted_iota(jnp.int32, (2 * LANES, inner), 1) // (inner // heads)
    row_head = lax.broadcasted_iota(jnp.int32, (2 * LANES, inner), 0) % LANES
    return jnp.where(lane_head == row_head, 1.0, 0.0).astype(BF16)


def pre_norm(hidden, gain_full):
    return hidden * lax.rsqrt(jnp.mean(hidden * hidden, axis=-1, keepdims=True) + eps) * gain_full


def pad_to(values, rows, columns):
    return jnp.pad(values, ((0, rows - values.shape[0]), (0, columns - values.shape[1])))


def on_device(
    tokens, cotangent, lengths, packing, pre_gain, w_z, w_x, w_bc, w_dt, conv_x, conv_bc, head_params, norm_gain, w_out,
):
    dp_count = lax.axis_size("dp")
    bin_index = lax.axis_index("dp")
    seq_total, pos_here, cols_here = tokens.shape
    inner_part = conv_x.shape[2]
    heads_here = head_params.shape[2]
    dp_rows = w_z.shape[1]
    mixed = inner_part + 2 * STATE
    triples = lengths[packing].reshape(dp_count, 3)
    offsets = jnp.cumsum(triples, axis=1) - triples
    my_offsets = offsets[bin_index]
    my_lengths = triples[bin_index]
    bounds = my_offsets[1:3]
    bin_rows = jnp.arange(BIN, dtype=jnp.int32)
    segment = segment_of(bin_rows, my_offsets[1], my_offsets[2])
    seg_start = jnp.where(segment == 0, my_offsets[0], jnp.where(segment == 1, my_offsets[1], my_offsets[2]))
    within = bin_rows - seg_start
    pick_rows = (within // pos_here * 3 + segment) * pos_here + within % pos_here
    groups = packing.reshape(dp_count, 3)

    def to_bins(given):
        arrived = lax.all_to_all(given[groups], "dp", split_axis=0, concat_axis=0, tiled=True)
        flat = arrived.reshape(-1, cols_here)[pick_rows]
        return lax.all_to_all(flat, "tensor", split_axis=0, concat_axis=1, tiled=True)

    spread = spread_matrix(inner_part, heads_here)
    gains = lax.all_gather(pre_gain, "dp", axis=1, tiled=True).astype(F32)
    packs = []
    for layer in range(LAYERS):
        own = jnp.concatenate(
            [w_out[layer].T, w_z[layer], w_x[layer], w_bc[layer], pad_to(w_dt[layer], dp_rows, LANES)], axis=1
        )
        taps = jnp.concatenate([conv_x[layer], conv_bc[layer]], axis=1).astype(F32)
        head = jnp.stack([head_params[layer, 0], -jnp.exp(head_params[layer, 1])])
        wide = jnp.stack(
            [jnp.repeat(head_params[layer, 2], inner_part // heads_here), norm_gain[layer].astype(F32)]
        )
        packs.append((own, pad_to(taps, 8, mixed), pad_to(head, 8, LANES), pad_to(wide, 8, inner_part)))

    row_tokens = to_bins(tokens)
    hidden = row_tokens.astype(F32)
    records = []
    for layer in range(LAYERS):
        own, taps, head, wide = packs[layer]
        weights = lax.all_gather(own, "dp", axis=0, tiled=True)
        normed, norm_back = jax.vjp(pre_norm, hidden, gains[layer])
        rows = lax.all_gather(normed.astype(BF16), "tensor", axis=0, tiled=True)
        part, squares, gate, mixed_in, conv, dt_raw, mixed_out, gained, states = layer_forward(
            bounds, rows, weights, taps, head, wide, spread
        )
        total = lax.psum_scatter(part, "tensor", scatter_dimension=0, tiled=True).astype(F32)
        own_squares = lax.psum_scatter(squares[:, 0], "tensor", scatter_dimension=0, tiled=True)
        scale = lax.rsqrt(own_squares / INNER + eps)[:, None]
        hidden = hidden + total * scale
        records.append((norm_back, rows, weights, gained, total, scale, (gate, mixed_in, conv, dt_raw, mixed_out, states)))
    final_rows = hidden.astype(BF16)

    grad_hidden = to_bins(cotangent).astype(F32)
    collected = [None] * LAYERS
    for layer in reversed(range(LAYERS)):
        own, taps, head, wide = packs[layer]
        norm_back, rows, weights, gained, total, scale, saved = records[layer]
        grad_branch = grad_hidden.astype(BF16).astype(F32)
        twice = 2.0 * (-(scale**3) / (2 * INNER)) * jnp.sum(grad_branch * total, axis=1, keepdims=True)
        spread_grad = lax.all_gather((grad_branch * scale).astype(BF16), "tensor", axis=0, tiled=True)
        spread_twice = lax.all_gather(twice, "tensor", axis=0, tiled=True)
        part, gproj, gtaps, ghead, gwide = layer_backward(
            bounds, spread_grad, spread_twice, weights, taps, head, wide, spread, saved
        )
        grad_normed = lax.psum_scatter(part, "tensor", scatter_dimension=0, tiled=True).astype(F32)
        grad_weights = jnp.concatenate(
            [dot_tn(spread_grad, gained).astype(BF16), dot_tn(rows, gproj).astype(BF16)], axis=1
        )
        own_weights = lax.psum_scatter(grad_weights, "dp", scatter_dimension=0, tiled=True)
        grad_before, grad_gain = norm_back(grad_normed)
        grad_hidden = grad_hidden + grad_before
        collected[layer] = (own_weights, grad_gain, gtaps, ghead, gwide)

    heads_first = (
        jnp.stack([item[2][: CONV + 1, :inner_part] for item in collected]),
        jnp.stack(
            [
                jnp.concatenate(
                    [item[3][:2, :heads_here], jnp.sum(item[4][0:1].reshape(1, heads_here, -1), axis=2)], axis=0
                )
                for item in collected
            ]
        ),
        jnp.stack([item[4][1] for item in collected]),
    )
    shared = (
        jnp.stack([item[2][: CONV + 1, inner_part:] for item in collected]),
        jnp.stack([item[1] for item in collected]),
    )
    grad_convx, grad_head, grad_norm, shared_convbc, shared_pre = lax.psum(heads_first + shared, "dp")
    own_weights = jnp.stack([item[0] for item in collected])
    shared_bc = own_weights[:, :, 3 * inner_part : 3 * inner_part + 2 * STATE].astype(F32)
    grad_convbc, grad_pre, grad_bc = lax.psum((shared_convbc, shared_pre, shared_bc), "tensor")
    shard_pre = lax.dynamic_slice_in_dim(grad_pre, bin_index * dp_rows, dp_rows, 1)
    own_weights = own_weights.astype(F32)
    grad_out = jnp.swapaxes(own_weights[:, :, :inner_part], 1, 2)
    grad_z = own_weights[:, :, inner_part : 2 * inner_part]
    grad_x = own_weights[:, :, 2 * inner_part : 3 * inner_part]
    grad_dt = own_weights[:, :, 3 * inner_part + 2 * STATE : 3 * inner_part + 2 * STATE + heads_here]

    dev_grid = jnp.arange(dp_count, dtype=jnp.int32)[:, None, None]
    pos_grid = jnp.arange(pos_here, dtype=jnp.int32)[None, None, :]
    seq_pos = dev_grid * pos_here + pos_grid
    live_slot = (seq_pos < my_lengths[None, :, None]).reshape(-1, 1)
    source = jnp.minimum(my_offsets[None, :, None] + seq_pos, BIN - 1).reshape(-1)
    rank_of = jnp.zeros_like(packing).at[packing].set(jnp.arange(seq_total, dtype=jnp.int32))

    def from_bins(rows):
        columns = lax.all_to_all(rows, "tensor", split_axis=1, concat_axis=0, tiled=True)
        slots = jnp.where(live_slot, columns[source], 0).reshape(dp_count, 3, pos_here, cols_here)
        returned = lax.all_to_all(slots, "dp", split_axis=0, concat_axis=0, tiled=True)
        return returned.reshape(seq_total, pos_here, cols_here)[rank_of]

    activations = from_bins(final_rows)
    input_grad = from_bins(grad_hidden.astype(BF16))
    return (
        activations, input_grad, shard_pre, grad_z, grad_x, grad_bc, grad_dt,
        grad_convx, grad_convbc, grad_head, grad_norm, grad_out,
    )


def solution(mesh):
    placed = (
        P(None, "dp", "tensor"), P(None, "dp", "tensor"), P(), P(), P(None, "dp"),
        P(None, "dp", "tensor"), P(None, "dp", "tensor"), P(None, "dp", None), P(None, "dp", "tensor"),
        P(None, None, "tensor"), P(), P(None, None, "tensor"), P(None, "tensor"), P(None, "tensor", "dp"),
    )
    results = (
        P(None, "dp", "tensor"), P(None, "dp", "tensor"), P(None, "dp"),
        P(None, "dp", "tensor"), P(None, "dp", "tensor"), P(None, "dp", None), P(None, "dp", "tensor"),
        P(None, None, "tensor"), P(), P(None, None, "tensor"), P(None, "tensor"), P(None, "tensor", "dp"),
    )
    return jax.shard_map(on_device, mesh=mesh, in_specs=placed, out_specs=results, check_vma=False)
```

time: 2320 us -> 991 us (0.43)
  local copies, waits for them, and re-layouts: 729 us -> 91.4 us
  matrix products: 343 us -> 28.9 us
  other arithmetic: 288 us -> 38.6 us
  Pallas kernels: 0 us -> 139 us
  waiting for transfers between devices: 592 us -> 486 us
  blocking collectives: 244 us -> 144 us
  loops' own time: 45.4 us -> 0 us
    dynamic_update_slice x66 -> x0, local copies, waits for them, and re-layouts: 424 us -> none  [the longest x64 424 us: state_space(): lax.scan(jax.checkpoint(one_block), start_state, blocked)]
    dot_general x236 -> x4, matrix products: 343 us -> 28.9 us  [dot_tn(): lax.dot_general(left, right, (((0,), (0,)), ((), ())), preferred_element_...]
    reduce_scatter x8 -> x6, waiting for transfers between devices: 385 us -> 191 us  [the longest x2 111 us: on_device(): lax.psum_scatter(grad_weights, 'dp', scatter_dimension=0, tiled=True)]
    all_gather x10 -> x6, waiting for transfers between devices: 49.5 us -> 195 us  [the longest x2 71.7 us: on_device(): rows = lax.all_gather(normed.astype(BF16), 'tensor', axis=0, tiled=True)]
    pallas_call x0 -> x4, Pallas kernels: none -> 139 us  [the longest x2 82.3 us: layer_backward(): pl.pallas_call(backward_kernel, grid=(blocks,), in_specs=[pl.BlockSpec(me...]
    another operation x144 -> x11, other arithmetic: 102 us -> 0.1 us  [the longest x3 0.03 us: on_device(): jnp.stack([jnp.concatenate([item[3][:2, :heads_here], jnp.sum(item[4][0:1...]
    all_gather x6 -> x3, blocking collectives: 122 us -> 25.5 us  [the longest x1 13.9 us: on_device(): gains = lax.all_gather(pre_gain, 'dp', axis=1, tiled=True).astype(F32)]
    reduce_sum x41 -> x4, other arithmetic: 75.6 us -> 5.41 us  [the longest x2 5.17 us: on_device(): jnp.sum(grad_branch * total, axis=1, keepdims=True)]
  transfers between devices with their start and end apart: 26 -> 19, of which waited for: 14 -> 14; matrix products, arithmetic and copies ran while one was open for 27% -> 13% of each run, Pallas kernels for 0% -> 0%
where the time goes in v1:
time: 991 us; the launch traced here: 981 us
  waiting for transfers between devices  486 us (49%)
  blocking collectives  144 us (15%)
  Pallas kernels  139 us (14%)
  local copies, waits for them, and re-layouts  91.4 us (9%)
  other arithmetic  38.6 us (4%)
  starting transfers between devices  37.2 us (4%)
  matrix products  28.9 us (3%)
  between operations  15.8 us (2%)
    reduce_scatter x2, waiting for transfers between devices, on_device(): lax.psum_scatter(grad_weights, 'dp', scatter_dimension=0, tiled=True)  111 us
    pallas_call x2, Pallas kernels, layer_backward(): pl.pallas_call(backward_kernel, grid=(blocks,), in_specs=[pl.BlockSpec(me...  82.3 us
    reduce_scatter x4, waiting for transfers between devices, on_device(): lax.psum_scatter(part, 'tensor', scatter_dimension=0, tiled=True)  79.6 us
    all_gather x2, waiting for transfers between devices, on_device(): rows = lax.all_gather(normed.astype(BF16), 'tensor', axis=0, tiled=True)  71.7 us
    all_gather x2, waiting for transfers between devices, on_device(): weights = lax.all_gather(own, 'dp', axis=0, tiled=True)  67.7 us
    pallas_call x2, Pallas kernels, layer_forward(): pl.pallas_call(forward_kernel, grid=(blocks,), in_specs=[pl.BlockSpec(mem...  56.8 us
    all_gather x2, waiting for transfers between devices, on_device(): lax.all_gather((grad_branch * scale).astype(BF16), 'tensor', axis=0, tile...  55.6 us
    all_to_all x1, waiting for transfers between devices, to_bins(): lax.all_to_all(given[groups], 'dp', split_axis=0, concat_axis=0, tiled=True)  48.3 us
  transfers between devices with their start and end apart: 19, of which 14 were waited for; matrix products, arithmetic and copies ran while one was open for 13% of the time, Pallas kernels for 0%

profile of v1, /device:TPU:1, one launch (start us, length us, event | category | flops | bytes accessed | tf_op | source)
XLA Modules:
  0.0 981.0 jit_solution(4903692225930946548)
XLA Ops:
  16.0 6.5 all-to-all-start
  26.1 48.3 %all-to-all-done = bf16[8,3,128,256]{3,2,1,0:T(8,128)(2,1)S(1)} async-done(((bf16[8,3,128,256]{3,2,1,0:T(8,128)(2,1)}), bf16[8,3,128,256]{3,2,1,0:T(8,128)(2,1)S(1)}, u32[]{:S(2)}, u32[]{:S(2)}) %all-to-all-start) | async-done | bytes 1572896 | tf_op jit(solution)/shard_map/all_to_all | solution.py:409
  74.4 9.0 gather_fusion.2
  83.5 9.7 all-to-all-start.1
  93.2 13.9 %all_gather.27 = bf16[2,1024]{1,0:T(2,128)(2,1)S(1)} all-gather(bf16[2,128]{1,0:T(2,128)(2,1)S(1)} %copy-done.49), channel_id=1, replica_groups=mesh['dp'=8,'tensor'=4] {'dp'}, dimensions={1}, use_global_device_ids=true | all-gather | bytes 4608 | tf_op jit(solution)/shard_map/all_gather | solution.py:414
  113.3 35.3 %all-gather.11.cloned.1.call-done.rows_ref = bf16[2048,1024]{1,0:T(8,128)(2,1)} async-done(((bf16[512,1024]{1,0:T(8,128)(2,1)}), bf16[2048,1024]{1,0:T(8,128)(2,1)}) %all-gather.11.cloned.1.call-update) | async-done | bytes 4194320 | tf_op jit(solution)/shard_map/all_gather | solution.py:434
  148.6 28.4 %layer_forward.2 = (bf16[2048,1024]{1,0:T(8,128)(2,1)}, f32[2048,1]{1,0:T(8,128)S(1)}, f32[2048,512]{1,0:T(8,128)}, f32[2048,768]{1,0:T(8,128)}, f32[2048,768]{1...) custom-call(s32[2]{0:T(128)S(1)} %slice_bitcast_fusion.9.off_ref, ...), custom_call_target="tpu_custom_call" | custom-call | tf_op jit(solution)/shard_map/layer_forward/pallas_call | solution.py:305
  187.2 35.0 %reduce-scatter.7.cloned.1.call-done = bf16[512,1024]{1,0:T(8,128)(2,1)} async-done(((bf16[2048,1024]{1,0:T(8,128)(2,1)}), bf16[512,1024]{1,0:T(8,128)(2,1)}) %reduce-scatter.7.cloned.1.call-update) | async-done | bytes 1048592 | tf_op jit(solution)/shard_map/reduce_scatter | solution.py:438
  226.5 67.6 %all-gather.17.cloned.1.call-done.w_ref = bf16[1024,1920]{1,0:T(8,128)(2,1)} async-done(((bf16[128,1920]{1,0:T(8,128)(2,1)}), bf16[1024,1920]{1,0:T(8,128)(2,1)}) %all-gather.17.cloned.1.call-update) | async-done | bytes 3932176 | tf_op jit(solution)/shard_map/all_gather | solution.py:432
  294.1 36.4 %all-gather.15.cloned.1.call-done.rows_ref = bf16[2048,1024]{1,0:T(8,128)(2,1)} async-done(((bf16[512,1024]{1,0:T(8,128)(2,1)}), bf16[2048,1024]{1,0:T(8,128)(2,1)}) %all-gather.15.cloned.1.call-update) | async-done | bytes 4194320 | tf_op jit(solution)/shard_map/all_gather | solution.py:434
  330.6 28.5 %layer_forward.3 = (bf16[2048,1024]{1,0:T(8,128)(2,1)}, f32[2048,1]{1,0:T(8,128)S(1)}, f32[2048,512]{1,0:T(8,128)}, f32[2048,768]{1,0:T(8,128)}, f32[2048,768]{1...) custom-call(s32[2]{0:T(128)S(1)} %slice_bitcast_fusion.9.off_ref, ...), custom_call_target="tpu_custom_call" | custom-call | tf_op jit(solution)/shard_map/layer_forward/pallas_call | solution.py:305
  364.7 41.5 %all_to_all.84 = bf16[8,3,128,256]{3,2,1,0:T(8,128)(2,1)S(1)} all-to-all(bf16[8,3,128,256]{3,2,1,0:T(8,128)(2,1)} %bitcast.135), channel_id=1, replica_groups=mesh['dp'=8,'tensor'=4] {'dp'}, dimensions={0} | all-to-all | bytes 3145728 | tf_op jit(solution)/shard_map/all_to_all | solution.py:409
  406.1 9.0 gather_fusion.6
  415.2 18.6 %all_to_all.85 = bf16[4,512,256]{2,1,0:T(8,128)(2,1)S(1)} all-to-all(bf16[4,512,256]{2,1,0:T(8,128)(2,1)} %bitcast.139), channel_id=1, replica_groups=mesh['dp'=8,'tensor'=4] {'tensor'}, dimensions={0} | all-to-all | bytes 2097152 | tf_op jit(solution)/shard_map/all_to_all | solution.py:411
  434.6 6.3 all-reduce.9
  445.5 5.7 all-gather.2
  451.6 27.5 %all-gather.19.cloned.1.call-done.sg_ref = bf16[2048,1024]{1,0:T(8,128)(2,1)} async-done(((bf16[512,1024]{1,0:T(8,128)(2,1)}), bf16[2048,1024]{1,0:T(8,128)(2,1)}) %all-gather.19.cloned.1.call-update) | async-done | bytes 4194320 | tf_op jit(solution)/shard_map/all_gather | solution.py:452
  480.3 41.2 %layer_backward.2 = (bf16[2048,1024]{1,0:T(8,128)(2,1)}, bf16[2048,1408]{1,0:T(8,128)(2,1)}, f32[8,768]{1,0:T(8,128)S(1)}, f32[8,128]{1,0:T(8,128)S(1)}, f32[8,512]{1,0:T(8,128)S(1)}) custom-call(s32[2]{0:T(128)S(1)} %slice_bitcast_fusion.9.off_ref, bf16[2048,1024]{1,0:T(8,128)(2,1)} %all-gather.19.cloned.1.call-done.sg_ref, f32[2048,1]{1,0:T(8,128)S(1)} %copy.77.g2_ref, ...), custom_call_target="tpu_custom_call" | custom-call | tf_op jit(solution)/shard_map/layer_backward/pallas_call | solution.py:345
  521.7 44.1 %reduce-scatter.11.cloned.1.call-done = bf16[512,1024]{1,0:T(8,128)(2,1)} async-done(((bf16[2048,1024]{1,0:T(8,128)(2,1)}), bf16[512,1024]{1,0:T(8,128)(2,1)}) %reduce-scatter.11.cloned.1.call-update) | async-done | bytes 1048592 | tf_op jit(solution)/shard_map/reduce_scatter | solution.py:457
  575.5 5.8 all-gather.3
  581.7 28.0 %all-gather.21.cloned.1.call-done.sg_ref = bf16[2048,1024]{1,0:T(8,128)(2,1)} async-done(((bf16[512,1024]{1,0:T(8,128)(2,1)}), bf16[2048,1024]{1,0:T(8,128)(2,1)}) %all-gather.21.cloned.1.call-update) | async-done | bytes 4194320 | tf_op jit(solution)/shard_map/all_gather | solution.py:452
  611.0 41.1 %layer_backward.3 = (bf16[2048,1024]{1,0:T(8,128)(2,1)}, bf16[2048,1408]{1,0:T(8,128)(2,1)}, f32[8,768]{1,0:T(8,128)S(1)}, f32[8,128]{1,0:T(8,128)S(1)}, f32[8,512]{1,0:T(8,128)S(1)}) custom-call(s32[2]{0:T(128)S(1)} %slice_bitcast_fusion.9.off_ref, bf16[2048,1024]{1,0:T(8,128)(2,1)} %all-gather.21.cloned.1.call-done.sg_ref, f32[2048,1]{1,0:T(8,128)S(1)} %copy.78.g2_ref, ...), custom_call_target="tpu_custom_call" | custom-call | tf_op jit(solution)/shard_map/layer_backward/pallas_call | solution.py:345
  658.4 9.3 convolution_convert_fusion
  677.1 10.3 %convolution_convert_fusion.1 = bf16[1024,1408]{1,0:T(8,128)(2,1)S(1)} fusion(bf16[2048,1024]{1,0:T(8,128)(2,1)} %all-gather.11.cloned.1.call-done.rows_ref, bf16[2048,1408]{1,0:T(8,128)(2,1)} %get-tuple-element.59), kind=kOutput, calls=%fused_computation.13 | convolution fusion | flops 5907021824 | bytes 12845056 | tf_op jit(solution)/shard_map/dot_general | solution.py:31
  702.5 7.1 all-to-all-done.2
  714.0 13.0 %gather_fusion.3 = bf16[3072,256]{1,0:T(8,128)(2,1)} fusion(bf16[2048,256]{1,0:T(8,128)(2,1)S(1)} %bitcast.126, s32[3072]{0:T(1024)S(1)} %broadcast_clamp_fusion), kind=kCustom, calls=%fused_computation.3 | custom fusion | bytes 3158016 | tf_op jit(solution)/shard_map/gather | solution.py:502
  727.7 13.0 %gather_fusion.7 = bf16[3072,256]{1,0:T(8,128)(2,1)} fusion(bf16[2048,256]{1,0:T(8,128)(2,1)S(1)} %bitcast.127, s32[3072]{0:T(1024)S(1)} %broadcast_clamp_fusion), kind=kCustom, calls=%fused_computation.7 | custom fusion | bytes 3158016 | tf_op jit(solution)/shard_map/gather | solution.py:502
  749.7 43.7 %all-to-all-done.7 = bf16[8,3,128,256]{3,2,1,0:T(8,128)(2,1)S(1)} async-done(((bf16[8,3,128,256]{3,2,1,0:T(8,128)(2,1)}), bf16[8,3,128,256]{3,2,1,0:T(8,128)(2,1)S(1)}, u32[]{:S(2)}, u32[]{:S(2)}) %all-to-all-start.7) | async-done | bytes 1572896 | tf_op jit(solution)/shard_map/all_to_all | solution.py:503
  793.4 7.6 all-to-all-start.3
  803.3 109.5 %reduce-scatter.15.cloned.1.call-done = bf16[128,1920]{1,0:T(8,128)(2,1)} async-done(((bf16[1024,1920]{1,0:T(8,128)(2,1)}), bf16[128,1920]{1,0:T(8,128)(2,1)}) %reduce-scatter.15.cloned.1.call-update) | async-done | bytes 491536 | tf_op jit(solution)/shard_map/reduce_scatter | solution.py:461
  917.7 29.6 %all-reduce.10 = (f32[2,1024]{1,0:T(2,128)S(1)}, f32[2,5,512]{2,1,0:T(8,128)S(1)}, f32[2,5,256]{2,1,0:T(8,128)S(1)}, f32[2,3,8]{2,1,0:T(4,128)S(1)}, f32[2,512]{1,0:T(2,128)}) all-reduce(f32[2,1024]{1,0:T(2,128)S(1)} %pad_maximum_fusion.5, f32[2,5,512]{2,1,0:T(8,128)S(1)} %pad_maximum_fusion.3, ...), channel_id=1, replica_groups=mesh['dp'=8,'tensor'=4] {'dp'}, use_global_device_ids=true, to_apply=%region_16.17 | all-reduce | flops 10800 | bytes 86400 | tf_op jit(solution)/shard_map/psum | solution.py:482
  947.4 17.5 %all-reduce.11 = (f32[2,1024]{1,0:T(2,128)S(1)}, f32[2,5,256]{2,1,0:T(8,128)S(1)}) all-reduce(f32[2,1024]{1,0:T(2,128)S(1)} %get-tuple-element.108, f32[2,5,256]{2,1,0:T(8,128)S(1)} %get-tuple-element.110), channel_id=1, replica_groups=mesh['dp'=8,'tensor'=4] {'tensor'}, use_global_device_ids=true, to_apply=%region_17.18 | all-reduce | flops 4608 | bytes 36864 | tf_op jit(solution)/shard_map/psum | solution.py:485
  (274 shorter events, 116.8 us)
Async XLA Ops:
  7.2 7.0 copy-start
  7.2 106.1 %all-gather.13.cloned.1.call-start = ((), (), s32[]{:S(2)}) async-start(), calls=%async_computation.15 | async-start | bytes 4423680 | tf_op jit(solution)/shard_map/all_gather | solution.py:432
  16.0 58.5 %all-to-all-start = ((bf16[8,3,128,256]{3,2,1,0:T(8,128)(2,1)}), bf16[8,3,128,256]{3,2,1,0:T(8,128)(2,1)S(1)}, u32[]{:S(2)}, u32[]{:S(2)}) async-start(bf16[8,3,128,256]{3,2,1,0:T(8,128)(2,1)} %bitcast.1), calls=%async_computation | async-start | bytes 3145728 | tf_op jit(solution)/shard_map/all_to_all | solution.py:409
  23.3 60.2 %copy-start.29 = (s32[8,3]{1,0:T(8,128)}, s32[8,3]{1,0:T(8,128)S(1)}, u32[]{:S(2)}) copy-start(s32[8,3]{1,0:T(8,128)S(1)} %reshape.400) | copy-start | bytes 292
  23.4 60.0 %copy-start.46 = (s32[8,3]{1,0:T(8,128)}, s32[8,3]{1,0:T(8,128)S(1)}, u32[]{:S(2)}) copy-start(s32[8,3]{1,0:T(8,128)S(1)} %sub.32) | copy-start | bytes 292
  83.5 9.7 copy-start.49
  83.5 23.6 %all-to-all-start.1 = ((bf16[4,512,256]{2,1,0:T(8,128)(2,1)}), bf16[4,512,256]{2,1,0:T(8,128)(2,1)S(1)}, u32[]{:S(2)}, u32[]{:S(2)}) async-start(bf16[4,512,256]{2,1,0:T(8,128)(2,1)} %bitcast.7), calls=%async_computation.1 | async-start | bytes 2097152 | tf_op jit(solution)/shard_map/all_to_all | solution.py:411
  93.2 55.4 %all-gather.11.cloned.1.call-start = ((), (), s32[]{:S(2)}) async-start(), calls=%async_computation.14 | async-start | bytes 5242880 | tf_op jit(solution)/shard_map/all_gather | solution.py:434
  112.6 109.6 %reduce-scatter.7.cloned.1.call-start = ((), (), s32[]{:S(2)}) async-start(), calls=%async_computation.16 | async-start | bytes 5242880 | tf_op jit(solution)/shard_map/reduce_scatter | solution.py:438
  179.3 114.8 %all-gather.17.cloned.1.call-start = ((), (), s32[]{:S(2)}) async-start(), calls=%async_computation.18 | async-start | bytes 4423680 | tf_op jit(solution)/shard_map/all_gather | solution.py:432
  180.1 150.5 %all-gather.15.cloned.1.call-start = ((), (), s32[]{:S(2)}) async-start(), calls=%async_computation.17 | async-start | bytes 5242880 | tf_op jit(solution)/shard_map/all_gather | solution.py:434
  187.1 37.5 %copy-start.39 = (f32[2048]{0:T(1024)}, f32[2048]{0:T(1024)S(1)}, u32[]{:S(2)}) copy-start(f32[2048]{0:T(1024)S(1)} %all-reduce.8) | copy-start | bytes 24580
  187.2 37.4 %copy-start.40 = (f32[512]{0:T(512)}, f32[512]{0:T(512)S(1)}, u32[]{:S(2)}) copy-start(f32[512]{0:T(512)S(1)} %fusion.43) | copy-start | bytes 6148
  226.3 214.6 %reduce-scatter.9.cloned.1.call-start = ((), (), s32[]{:S(2)}) async-start(), calls=%async_computation.19 | async-start | bytes 5242880 | tf_op jit(solution)/shard_map/reduce_scatter | solution.py:438
  361.4 117.7 %all-gather.19.cloned.1.call-start = ((), (), s32[]{:S(2)}) async-start(), calls=%async_computation.20 | async-start | bytes 5242880 | tf_op jit(solution)/shard_map/all_gather | solution.py:452
  434.2 8.3 copy-start.15
  442.5 36.6 %copy-start.3 = (f32[8,128,512]{2,1,0:T(8,128)S(1)}, f32[8,128,512]{2,1,0:T(8,128)}, u32[]{:S(2)}) copy-start(f32[8,128,512]{2,1,0:T(8,128)} %get-tuple-element.49.st_ref) | copy-start | bytes 6291460
  445.4 120.4 %reduce-scatter.11.cloned.1.call-start = ((), (), s32[]{:S(2)}) async-start(), calls=%async_computation.21 | async-start | bytes 5242880 | tf_op jit(solution)/shard_map/reduce_scatter | solution.py:457
  521.5 44.3 %copy-start.14 = (f32[512,1024]{1,0:T(8,128)S(1)}, f32[512,1024]{1,0:T(8,128)}, u32[]{:S(2)}) copy-start(f32[512,1024]{1,0:T(8,128)} %copy-done.13) | copy-start | bytes 6291460
  521.5 44.3 %copy-start.33 = (f32[512]{0:T(512)S(1)}, f32[512]{0:T(512)}, u32[]{:S(2)}) copy-start(f32[512]{0:T(512)} %copy-done.32) | copy-start | bytes 6148
  521.6 46.9 %copy-start.38 = (f32[512]{0:T(512)S(1)}, f32[512]{0:T(512)}, u32[]{:S(2)}) copy-start(f32[512]{0:T(512)} %copy-done.37) | copy-start | bytes 6148
  521.6 46.9 %copy-start.43 = (f32[512]{0:T(512)S(1)}, f32[512]{0:T(512)}, u32[]{:S(2)}) copy-start(f32[512]{0:T(512)} %copy-done.42) | copy-start | bytes 6148
  521.6 88.2 %all-gather.21.cloned.1.call-start = ((), (), s32[]{:S(2)}) async-start(), calls=%async_computation.22 | async-start | bytes 5242880 | tf_op jit(solution)/shard_map/all_gather | solution.py:452
  573.5 36.2 %copy-start.2 = (f32[8,128,512]{2,1,0:T(8,128)S(1)}, f32[8,128,512]{2,1,0:T(8,128)}, u32[]{:S(2)}) copy-start(f32[8,128,512]{2,1,0:T(8,128)} %get-tuple-element.56.st_ref) | copy-start | bytes 6291460
  574.7 121.7 %reduce-scatter.13.cloned.1.call-start = ((), (), s32[]{:S(2)}) async-start(), calls=%async_computation.23 | async-start | bytes 5242880 | tf_op jit(solution)/shard_map/reduce_scatter | solution.py:457
  652.1 151.2 %reduce-scatter.17.cloned.1.call-start = ((), (), s32[]{:S(2)}) async-start(), calls=%async_computation.25 | async-start | bytes 4423680 | tf_op jit(solution)/shard_map/reduce_scatter | solution.py:461
  669.9 242.8 %reduce-scatter.15.cloned.1.call-start = ((), (), s32[]{:S(2)}) async-start(), calls=%async_computation.24 | async-start | bytes 4423680 | tf_op jit(solution)/shard_map/reduce_scatter | solution.py:461
  692.4 17.2 %all-to-all-start.2 = ((bf16[512,4,256]{2,0,1:T(8,128)(2,1)}), bf16[512,4,256]{2,0,1:T(8,128)(2,1)S(1)}, u32[]{:S(2)}, u32[]{:S(2)}) async-start(bf16[512,4,256]{2,0,1:T(8,128)(2,1)} %bitcast.121), calls=%async_computation.4 | async-start | bytes 2097152 | tf_op jit(solution)/shard_map/all_to_all | solution.py:501
  709.6 18.1 %all-to-all-start.6 = ((bf16[512,4,256]{2,0,1:T(8,128)(2,1)}), bf16[512,4,256]{2,0,1:T(8,128)(2,1)S(1)}, u32[]{:S(2)}, u32[]{:S(2)}) async-start(bf16[512,4,256]{2,0,1:T(8,128)(2,1)} %bitcast.120), calls=%async_computation.10 | async-start | bytes 2097152 | tf_op jit(solution)/shard_map/all_to_all | solution.py:501
  744.0 49.4 %all-to-all-start.7 = ((bf16[8,3,128,256]{3,2,1,0:T(8,128)(2,1)}), bf16[8,3,128,256]{3,2,1,0:T(8,128)(2,1)S(1)}, u32[]{:S(2)}, u32[]{:S(2)}) async-start(bf16[8,3,128,256]{3,2,1,0:T(8,128)(2,1)} %get-tuple-element.141), calls=%async_computation.11 | async-start | bytes 3145728 | tf_op jit(solution)/shard_map/all_to_all | solution.py:503
  793.4 175.7 %all-to-all-start.3 = ((bf16[8,3,128,256]{3,2,1,0:T(8,128)(2,1)}), bf16[8,3,128,256]{3,2,1,0:T(8,128)(2,1)}, u32[]{:S(2)}, u32[]{:S(2)}) async-start(bf16[8,3,128,256]{3,2,1,0:T(8,128)(2,1)} %get-tuple-element.142), calls=%async_computation.5 | async-start | bytes 3145728 | tf_op jit(solution)/shard_map/all_to_all | solution.py:503
  801.0 171.4 %all-reduce.14.cloned.1.call-start = ((), (), s32[]{:S(2)}) async-start(), calls=%async_computation.26 | async-start | bytes 524288 | tf_op jit(solution)/shard_map/psum | solution.py:485
  (39 other events, 109.4 us)
Sparse Core Ops, SparseCore 0:
  14.0 94.0 all-gather.12
  112.7 35.8 all-gather.10
  178.1 44.0 reduce-scatter.6
  225.1 68.9 all-gather.16
  296.2 34.3 all-gather.14
  360.1 44.1 reduce-scatter.8
  445.5 33.5 all-gather.18
  521.7 44.0 reduce-scatter.10
  574.8 34.8 all-gather.20
  652.2 44.1 reduce-scatter.12
  700.1 103.1 reduce-scatter.16
  807.3 105.4 reduce-scatter.14
  917.2 30.3 all-reduce.13

commit v2 on v1

--- a/solution.py
+++ b/solution.py
@@ -97,25 +97,125 @@
     return jnp.where(keep, pair, jnp.zeros_like(pair))
 
 
+SHARE = BLK // 4
+AG_OWN, AG_ACROSS, AG_PASS, RS_PAIR, RS_ACROSS, SM_PAIR, SM_ACROSS = range(7)
+
+
+class Ring:
+    def __init__(self, sems):
+        me = lax.axis_index("tensor")
+        self.low, self.high = me % 2, me // 2
+        self.me = me
+        self.sibling = self.high * 2 + (1 - self.low)
+        self.across = (1 - self.high) * 2 + self.low
+        self.beyond = (1 - self.high) * 2 + (1 - self.low)
+        self.sems = sems
+
+    def greet(self):
+        barrier = pltpu.get_barrier_semaphore()
+        for other in (self.sibling, self.across):
+            pl.semaphore_signal(barrier, inc=1, device_id={"tensor": other}, device_id_type=pl.DeviceIdType.MESH)
+        pl.semaphore_wait(barrier, 2)
+
+    def slot(self, owner):
+        return ((self.low + owner % 2) % 2) * 2 + (self.high + owner // 2) % 2
+
+    def copy(self, kind, block, source, target, other):
+        return pltpu.make_async_remote_copy(
+            src_ref=source, dst_ref=target,
+            send_sem=self.sems.at[kind, block, 0], recv_sem=self.sems.at[kind, block, 1],
+            device_id={"tensor": other}, device_id_type=pl.DeviceIdType.MESH,
+        )
+
+
+def gather_copy(ring, kind, block, own, rows):
+    if kind == AG_PASS:
+        passed = rows.at[block, pl.ds(ring.across * SHARE, SHARE), :]
+        return ring.copy(kind, block, passed, passed, ring.sibling)
+    mine = own.at[pl.ds(block * SHARE, SHARE), :]
+    place = rows.at[block, pl.ds(ring.me * SHARE, SHARE), :]
+    return ring.copy(kind, block, mine, place, ring.sibling if kind == AG_OWN else ring.across)
+
+
+def pair_copy(ring, block, parts, from_pair):
+    return ring.copy(RS_PAIR, block, parts.at[block, pl.ds(2 * SHARE, 2 * SHARE), :], from_pair.at[block], ring.sibling)
+
+
+def across_copy(ring, block, sums, from_across):
+    return ring.copy(RS_ACROSS, block, sums.at[block], from_across.at[block], ring.across)
+
+
+def store_parts(ring, block, part, parts):
+    for owner in range(4):
+        parts[block, pl.ds(ring.slot(owner) * SHARE, SHARE), :] = part[owner * SHARE : (owner + 1) * SHARE].astype(BF16)
+
+
+def add_pair(block, parts, from_pair, sums):
+    sums[block] = (
+        parts[block, pl.ds(SHARE, SHARE), :].astype(F32) + from_pair[block, pl.ds(SHARE, SHARE), :].astype(F32)
+    ).astype(BF16)
+
+
+def add_all(block, parts, from_pair, from_across):
+    return (
+        parts[block, pl.ds(0, SHARE), :].astype(F32)
+        + from_pair[block, pl.ds(0, SHARE), :].astype(F32)
+        + from_across[block].astype(F32)
+    )
+
+
+def own_column(line, first_lane):
+    lanes = lax.broadcasted_iota(jnp.int32, (SHARE, line.shape[1]), 1)
+    rows = lax.broadcasted_iota(jnp.int32, (SHARE, line.shape[1]), 0)
+    return jnp.sum(jnp.where(lanes == rows + first_lane, line, 0.0), axis=1, keepdims=True)
+
+
 def forward_kernel(
-    off_ref, rows_ref, w_ref, taps_ref, head_ref, wide_ref, spread_ref,
-    part_ref, sq_ref, z_ref, in_ref, pre_ref, dt_ref, y_ref, gg_ref, st_ref,
-    state, padded,
+    off_ref, own_ref, hid_ref, w_ref, taps_ref, head_ref, wide_ref, spread_ref, next_ref,
+    rows_ref, z_ref, in_ref, pre_ref, dt_ref, y_ref, gg_ref, st_ref, hnext_ref, tot_ref, scale_ref, normed_ref,
+    state, padded, rows, parts, from_pair, sums, from_across, sq_own, sq_pair, sq_sums, sq_across, sems,
 ):
     block = pl.program_id(0)
     inner = y_ref.shape[1]
     mixed = in_ref.shape[1]
     first, second = off_ref[0], off_ref[1]
+    blocks = rows.shape[0]
+    ring = Ring(sems)
+
+    def sq_pair_copy(at):
+        return ring.copy(SM_PAIR, at, sq_own.at[at], sq_pair.at[at], ring.sibling)
+
+    def sq_across_copy(at):
+        return ring.copy(SM_ACROSS, at, sq_sums.at[at], sq_across.at[at], ring.across)
 
     @pl.when(block == 0)
     def _():
+        ring.greet()
+
+        @pl.loop(0, blocks)
+        def _(at):
+            gather_copy(ring, AG_ACROSS, at, own_ref, rows).start()
+            gather_copy(ring, AG_OWN, at, own_ref, rows).start()
+
         state[...] = jnp.zeros_like(state)
         padded[pl.ds(0, 8), :] = jnp.zeros((8, mixed), F32)
+
+        @pl.loop(0, blocks)
+        def _(at):
+            rows[at, pl.ds(ring.me * SHARE, SHARE), :] = own_ref[pl.ds(at * SHARE, SHARE), :]
+
+        gather_copy(ring, AG_ACROSS, 0, own_ref, rows).wait_recv()
+        gather_copy(ring, AG_PASS, 0, own_ref, rows).start()
+
+    gather_copy(ring, AG_OWN, block, own_ref, rows).wait_recv()
+    gather_copy(ring, AG_PASS, block, own_ref, rows).wait_recv()
+    here = rows[block]
+    rows_ref[...] = here
 
     row_col, row_row, seg_col, seg_row = block_frame(block, first, second)
     seg_start = jnp.where(seg_col == 0, 0, jnp.where(seg_col == 1, first, second))
     within = row_col - seg_start
-    product = dot_nn(rows_ref[...], w_ref[:, inner:])
+    product = dot_nn(here, w_ref[:, inner:])
     gate = product[:, :inner]
     mixed_in = product[:, inner : inner + mixed]
     dt_raw = product[:, inner + mixed :]
@@ -163,32 +263,121 @@
     state[...] = old_state * keep + dot_tn(b_low, tailed)
     y_ref[...] = mixed_out
     gated = mixed_out * (gate * sigmoid(gate))
-    sq_ref[...] = jnp.sum(gated * gated, axis=1, keepdims=True)
     gained = (gated * wide[1:2]).astype(BF16)
     gg_ref[...] = gained
-    part_ref[...] = dot_nt(gained, w_ref[:, :inner]).astype(BF16)
+    store_parts(ring, block, dot_nt(gained, w_ref[:, :inner]), parts)
+    high, low = split_two(gated * gated)
+    ones = jnp.ones((8, inner), BF16)
+    sq_own[block] = dot_nt(ones, high) + dot_nt(ones, low)
+    pair_copy(ring, block, parts, from_pair).start()
+    sq_pair_copy(block).start()
+
+    def second_stage(at):
+        pair_copy(ring, at, parts, from_pair).wait_recv()
+        sq_pair_copy(at).wait_recv()
+        add_pair(at, parts, from_pair, sums)
+        sq_sums[at] = sq_own[at] + sq_pair[at]
+        across_copy(ring, at, sums, from_across).start()
+        sq_across_copy(at).start()
+
+    def last_stage(at):
+        across_copy(ring, at, sums, from_across).wait_recv()
+        sq_across_copy(at).wait_recv()
+        total = add_all(at, parts, from_pair, from_across)
+        squares = own_column((sq_sums[at] + sq_across[at])[0:1], ring.me * SHARE)
+        scale = lax.rsqrt(squares / INNER + eps)
+        here = pl.ds(at * SHARE, SHARE)
+        hidden = hid_ref[here, :] + total * scale
+        hnext_ref[here, :] = hidden
+        tot_ref[here, :] = total
+        scale_ref[here, :] = scale
+        mean = jnp.sum(hidden * hidden, axis=1, keepdims=True) / hidden.shape[1]
+        normed_ref[here, :] = (hidden * lax.rsqrt(mean + eps) * next_ref[0:1]).astype(BF16)
+
+    @pl.when(block < blocks - 1)
+    def _():
+        gather_copy(ring, AG_ACROSS, block + 1, own_ref, rows).wait_recv()
+        gather_copy(ring, AG_PASS, block + 1, own_ref, rows).start()
+
+    @pl.when(block >= 1)
+    def _():
+        second_stage(block - 1)
+
+    @pl.when(block >= 2)
+    def _():
+        last_stage(block - 2)
+
+    @pl.when(block == blocks - 1)
+    def _():
+        second_stage(block)
+        last_stage(block - 1)
+        last_stage(block)
+
+        @pl.loop(0, blocks)
+        def _(at):
+            for kind in (AG_OWN, AG_ACROSS, AG_PASS):
+                gather_copy(ring, kind, at, own_ref, rows).wait_send()
+            pair_copy(ring, at, parts, from_pair).wait_send()
+            across_copy(ring, at, sums, from_across).wait_send()
+            sq_pair_copy(at).wait_send()
+            sq_across_copy(at).wait_send()
 
 
 def backward_kernel(
-    off_ref, sg_ref, g2_ref, w_ref, taps_ref, head_ref, wide_ref, spread_ref,
+    off_ref, own_ref, tw_ref, w_ref, taps_ref, head_ref, wide_ref, spread_ref,
     z_ref, in_ref, pre_ref, dt_ref, y_ref, st_ref,
-    part_ref, gproj_ref, gtaps_ref, ghead_ref, gwide_ref,
-    dstate, padded,
+    rows_ref, gnormed_ref, gproj_ref, gtaps_ref, ghead_ref, gwide_ref,
+    dstate, padded, rows, parts, from_pair, sums, from_across, twice, sems,
 ):
     step = pl.program_id(0)
     block = pl.num_programs(0) - 1 - step
     inner = y_ref.shape[1]
     mixed = in_ref.shape[1]
     first, second = off_ref[0], off_ref[1]
+    blocks = rows.shape[0]
+    ring = Ring(sems)
+
+    def twice_copies():
+        return (
+            ring.copy(SM_PAIR, 0, tw_ref, twice.at[ring.me], ring.sibling),
+            ring.copy(SM_ACROSS, 0, tw_ref, twice.at[ring.me], ring.across),
+            ring.copy(SM_PAIR, 1, twice.at[ring.across], twice.at[ring.across], ring.sibling),
+        )
 
     @pl.when(step == 0)
     def _():
+        ring.greet()
+        to_sibling, to_across, onward = twice_copies()
+        to_across.start()
+        to_sibling.start()
+
+        @pl.loop(0, blocks)
+        def _(at):
+            gather_copy(ring, AG_ACROSS, blocks - 1 - at, own_ref, rows).start()
+            gather_copy(ring, AG_OWN, blocks - 1 - at, own_ref, rows).start()
+
+        @pl.loop(0, blocks)
+        def _(at):
+            rows[at, pl.ds(ring.me * SHARE, SHARE), :] = own_ref[pl.ds(at * SHARE, SHARE), :]
+
+        twice[ring.me] = tw_ref[...]
+        to_across.wait_recv()
+        onward.start()
+        gather_copy(ring, AG_ACROSS, blocks - 1, own_ref, rows).wait_recv()
+        gather_copy(ring, AG_PASS, blocks - 1, own_ref, rows).start()
+        to_sibling.wait_recv()
+        onward.wait_recv()
         dstate[...] = jnp.zeros_like(dstate)
         padded[pl.ds(BLK, 8), :] = jnp.zeros((8, mixed), F32)
         gtaps_ref[...] = jnp.zeros_like(gtaps_ref)
         ghead_ref[...] = jnp.zeros_like(ghead_ref)
         gwide_ref[...] = jnp.zeros_like(gwide_ref)
 
+    gather_copy(ring, AG_OWN, block, own_ref, rows).wait_recv()
+    gather_copy(ring, AG_PASS, block, own_ref, rows).wait_recv()
+    here = rows[block]
+    rows_ref[...] = here
+    twice_here = jnp.concatenate([own_column(twice[owner, block][0:1], 0) for owner in range(4)], axis=0)
     row_col, row_row, seg_col, seg_row = block_frame(block, first, second)
     seg_end = jnp.where(seg_col == 0, first, jnp.where(seg_col == 1, second, pl.num_programs(0) * BLK))
     remaining = seg_end - row_col
@@ -202,8 +391,8 @@
     gate_sig = sigmoid(gate)
     gate_silu = gate * gate_sig
     gated = mixed_out * gate_silu
-    grad_scaled = dot_nn(sg_ref[...], w_ref[:, :inner])
-    grad_gated = grad_scaled * gain + g2_ref[...] * gated
+    grad_scaled = dot_nn(here, w_ref[:, :inner])
+    grad_gated = grad_scaled * gain + twice_here * gated
     grad_out = grad_gated * gate_silu
     grad_gate = grad_gated * mixed_out * (gate_sig * (1.0 + gate * (1.0 - gate_sig)))
     grad_out_low = grad_out.astype(BF16)
@@ -260,8 +449,8 @@
     above = lax.broadcasted_iota(jnp.int32, (BLK, BLK), 0)
     below = lax.broadcasted_iota(jnp.int32, (BLK, BLK), 1)
     upper = jnp.where(above <= below, 1.0, 0.0).astype(BF16)
-    parts = dot_nn(upper, jnp.concatenate(split_three(balance), axis=1))
-    grad_log = parts[:, :LANES] + parts[:, LANES : 2 * LANES] + parts[:, 2 * LANES :] + final
+    thirds = dot_nn(upper, jnp.concatenate(split_three(balance), axis=1))
+    grad_log = thirds[:, :LANES] + thirds[:, LANES : 2 * LANES] + thirds[:, 2 * LANES :] + final
     grad_steps = direct + grad_log * head[1:2]
     grad_dt = grad_steps * sigmoid(shifted)
     ghead_ref[0:1, :] += jnp.sum(grad_dt, axis=0, keepdims=True)
@@ -286,15 +475,64 @@
     padded[pl.ds(BLK, 8), :] = padded[pl.ds(0, 8), :]
     gproj = jnp.concatenate([grad_gate.astype(BF16), grad_in.astype(BF16), grad_dt.astype(BF16)], axis=1)
     gproj_ref[...] = gproj
-    part_ref[...] = dot_nt(gproj, w_ref[:, inner:]).astype(BF16)
+    store_parts(ring, block, dot_nt(gproj, w_ref[:, inner:]), parts)
+    pair_copy(ring, block, parts, from_pair).start()
+
+    def second_stage(at):
+        pair_copy(ring, at, parts, from_pair).wait_recv()
+        add_pair(at, parts, from_pair, sums)
+        across_copy(ring, at, sums, from_across).start()
+
+    def last_stage(at):
+        across_copy(ring, at, sums, from_across).wait_recv()
+        gnormed_ref[pl.ds(at * SHARE, SHARE), :] = add_all(at, parts, from_pair, from_across)
+
+    @pl.when(step < blocks - 1)
+    def _():
+        gather_copy(ring, AG_ACROSS, block - 1, own_ref, rows).wait_recv()
+        gather_copy(ring, AG_PASS, block - 1, own_ref, rows).start()
+
+    @pl.when(step >= 1)
+    def _():
+        second_stage(block + 1)
+
+    @pl.when(step >= 2)
+    def _():
+        last_stage(block + 2)
+
+    @pl.when(step == blocks - 1)
+    def _():
+        second_stage(block)
+        last_stage(block + 1)
+        last_stage(block)
+        for copy in twice_copies():
+            copy.wait_send()
+
+        @pl.loop(0, blocks)
+        def _(at):
+            for kind in (AG_OWN, AG_ACROSS, AG_PASS):
+                gather_copy(ring, kind, at, own_ref, rows).wait_send()
+            pair_copy(ring, at, parts, from_pair).wait_send()
+            across_copy(ring, at, sums, from_across).wait_send()
 
 
 def whole(shape):
     return pl.BlockSpec(shape, lambda b: (0,) * len(shape))
 
 
-def layer_forward(offsets, rows, weights, taps, head, wide, spread):
-    count, width = rows.shape
+def exchange_scratch(blocks, width):
+    return [
+        pltpu.VMEM((blocks, BLK, width), BF16),
+        pltpu.VMEM((blocks, BLK, width), BF16),
+        pltpu.VMEM((blocks, 2 * SHARE, width), BF16),
+        pltpu.VMEM((blocks, SHARE, width), BF16),
+        pltpu.VMEM((blocks, SHARE, width), BF16),
+    ]
+
+
+def layer_forward(offsets, own, hidden, weights, taps, head, wide, spread, next_gain):
+    own_rows, width = own.shape
+    count = 4 * own_rows
     inner, mixed = wide.shape[1], taps.shape[1]
     blocks = count // BLK
     total = weights.shape[1]
@@ -307,17 +545,17 @@
         grid=(blocks,),
         in_specs=[
             pl.BlockSpec(memory_space=pltpu.SMEM),
-            by_block(width), whole((width, total)), whole((8, mixed)), whole((8, LANES)), whole((8, inner)),
-            whole((2 * LANES, inner)),
+            whole((own_rows, width)), whole((own_rows, width)), whole((width, total)), whole((8, mixed)),
+            whole((8, LANES)), whole((8, inner)), whole((2 * LANES, inner)), whole((8, width)),
         ],
         out_specs=[
-            by_block(width), by_block(1), by_block(inner), by_block(mixed), by_block(mixed),
+            by_block(width), by_block(inner), by_block(mixed), by_block(mixed),
             by_block(LANES), by_block(inner), by_block(inner),
             pl.BlockSpec((1, STATE, inner), lambda b: (b, 0, 0)),
+            whole((own_rows, width)), whole((own_rows, width)), whole((own_rows, 1)), whole((own_rows, width)),
         ],
         out_shape=[
             jax.ShapeDtypeStruct((count, width), BF16),
-            jax.ShapeDtypeStruct((count, 1), F32),
             jax.ShapeDtypeStruct((count, inner), F32),
             jax.ShapeDtypeStruct((count, mixed), F32),
             jax.ShapeDtypeStruct((count, mixed), F32),
@@ -325,16 +563,26 @@
             jax.ShapeDtypeStruct((count, inner), F32),
             jax.ShapeDtypeStruct((count, inner), BF16),
             jax.ShapeDtypeStruct((blocks, STATE, inner), F32),
+            jax.ShapeDtypeStruct((own_rows, width), F32),
+            jax.ShapeDtypeStruct((own_rows, width), F32),
+            jax.ShapeDtypeStruct((own_rows, 1), F32),
+            jax.ShapeDtypeStruct((own_rows, width), BF16),
         ],
-        scratch_shapes=[pltpu.VMEM((STATE, inner), F32), pltpu.VMEM((BLK + 8, mixed), F32)],
-        compiler_params=pltpu.CompilerParams(vmem_limit_bytes=48 * 1024 * 1024),
+        scratch_shapes=[pltpu.VMEM((STATE, inner), F32), pltpu.VMEM((BLK + 8, mixed), F32)]
+        + exchange_scratch(blocks, width)
+        + [pltpu.VMEM((blocks, 8, BLK), F32)] * 4
+        + [pltpu.SemaphoreType.DMA((7, blocks, 2))],
+        compiler_params=pltpu.CompilerParams(
+            vmem_limit_bytes=56 * 1024 * 1024, collective_id=1, has_side_effects=True
+        ),
         name="layer_forward",
-    )(offsets, rows, weights, taps, head, wide, spread)
-
-
-def layer_backward(offsets, spread_grad, twice, weights, taps, head, wide, spread, saved):
+    )(offsets, own, hidden, weights, taps, head, wide, spread, next_gain)
+
+
+def layer_backward(offsets, own, twice, weights, taps, head, wide, spread, saved):
     gate, mixed_in, conv, dt_raw, mixed_out, states = saved
-    count, width = spread_grad.shape
+    own_rows, width = own.shape
+    count = 4 * own_rows
     inner, mixed = wide.shape[1], taps.shape[1]
     blocks = count // BLK
     total = weights.shape[1]
@@ -347,26 +595,32 @@
         grid=(blocks,),
         in_specs=[
             pl.BlockSpec(memory_space=pltpu.SMEM),
-            by_block(width), by_block(1), whole((width, total)), whole((8, mixed)), whole((8, LANES)),
-            whole((8, inner)), whole((2 * LANES, inner)),
+            whole((own_rows, width)), whole((blocks, 8, LANES)), whole((width, total)), whole((8, mixed)),
+            whole((8, LANES)), whole((8, inner)), whole((2 * LANES, inner)),
             by_block(inner), by_block(mixed), by_block(mixed), by_block(LANES), by_block(inner),
             pl.BlockSpec((1, STATE, inner), lambda b: (blocks - 1 - b, 0, 0)),
         ],
         out_specs=[
-            by_block(width), by_block(total - inner),
+            by_block(width), whole((own_rows, width)), by_block(total - inner),
             whole((8, mixed)), whole((8, LANES)), whole((8, inner)),
         ],
         out_shape=[
             jax.ShapeDtypeStruct((count, width), BF16),
+            jax.ShapeDtypeStruct((own_rows, width), F32),
             jax.ShapeDtypeStruct((count, total - inner), BF16),
             jax.ShapeDtypeStruct((8, mixed), F32),
             jax.ShapeDtypeStruct((8, LANES), F32),
             jax.ShapeDtypeStruct((8, inner), F32),
         ],
-        scratch_shapes=[pltpu.VMEM((STATE, inner), F32), pltpu.VMEM((BLK + 8, mixed), F32)],
-        compiler_params=pltpu.CompilerParams(vmem_limit_bytes=48 * 1024 * 1024),
+        scratch_shapes=[pltpu.VMEM((STATE, inner), F32), pltpu.VMEM((BLK + 8, mixed), F32)]
+        + exchange_scratch(blocks, width)
+        + [pltpu.VMEM((4, blocks, 8, LANES), F32)]
+        + [pltpu.SemaphoreType.DMA((7, blocks, 2))],
+        compiler_params=pltpu.CompilerParams(
+            vmem_limit_bytes=56 * 1024 * 1024, collective_id=2, has_side_effects=True
+        ),
         name="layer_backward",
-    )(offsets, spread_grad, twice, weights, taps, head, wide, spread, gate, mixed_in, conv, dt_raw, mixed_out, states)
+    )(offsets, own, twice, weights, taps, head, wide, spread, gate, mixed_in, conv, dt_raw, mixed_out, states)
 
 
 def spread_matrix(inner, heads):
@@ -403,6 +657,8 @@
     seg_start = jnp.where(segment == 0, my_offsets[0], jnp.where(segment == 1, my_offsets[1], my_offsets[2]))
     within = bin_rows - seg_start
     pick_rows = (within // pos_here * 3 + segment) * pos_here + within % pos_here
+    blocks = BIN // BLK
+    pick_rows = jnp.swapaxes(pick_rows.reshape(blocks, 4, SHARE), 0, 1).reshape(-1)
     groups = packing.reshape(dp_count, 3)
 
     def to_bins(given):
@@ -430,31 +686,29 @@
     for layer in range(LAYERS):
         own, taps, head, wide = packs[layer]
         weights = lax.all_gather(own, "dp", axis=0, tiled=True)
-        normed, norm_back = jax.vjp(pre_norm, hidden, gains[layer])
-        rows = lax.all_gather(normed.astype(BF16), "tensor", axis=0, tiled=True)
-        part, squares, gate, mixed_in, conv, dt_raw, mixed_out, gained, states = layer_forward(
-            bounds, rows, weights, taps, head, wide, spread
+        before = hidden
+        if layer == 0:
+            normed = pre_norm(hidden, gains[layer]).astype(BF16)
+        rows, gate, mixed_in, conv, dt_raw, mixed_out, gained, states, hidden, total, scale, normed = layer_forward(
+            bounds, normed, hidden, weights, taps, head, wide, spread,
+            jnp.broadcast_to(gains[min(layer + 1, LAYERS - 1)], (8, gains.shape[1])),
         )
-        total = lax.psum_scatter(part, "tensor", scatter_dimension=0, tiled=True).astype(F32)
-        own_squares = lax.psum_scatter(squares[:, 0], "tensor", scatter_dimension=0, tiled=True)
-        scale = lax.rsqrt(own_squares / INNER + eps)[:, None]
-        hidden = hidden + total * scale
-        records.append((norm_back, rows, weights, gained, total, scale, (gate, mixed_in, conv, dt_raw, mixed_out, states)))
+        saved = (gate, mixed_in, conv, dt_raw, mixed_out, states)
+        records.append((before, rows, weights, gained, total, scale, saved))
     final_rows = hidden.astype(BF16)
 
     grad_hidden = to_bins(cotangent).astype(F32)
     collected = [None] * LAYERS
     for layer in reversed(range(LAYERS)):
         own, taps, head, wide = packs[layer]
-        norm_back, rows, weights, gained, total, scale, saved = records[layer]
+        before, rows, weights, gained, total, scale, saved = records[layer]
+        normed, norm_back = jax.vjp(pre_norm, before, gains[layer])
         grad_branch = grad_hidden.astype(BF16).astype(F32)
         twice = 2.0 * (-(scale**3) / (2 * INNER)) * jnp.sum(grad_branch * total, axis=1, keepdims=True)
-        spread_grad = lax.all_gather((grad_branch * scale).astype(BF16), "tensor", axis=0, tiled=True)
-        spread_twice = lax.all_gather(twice, "tensor", axis=0, tiled=True)
-        part, gproj, gtaps, ghead, gwide = layer_backward(
-            bounds, spread_grad, spread_twice, weights, taps, head, wide, spread, saved
+        twice_rows = jnp.broadcast_to(pad_to(twice.reshape(blocks, SHARE), blocks, LANES)[:, None], (blocks, 8, LANES))
+        spread_grad, grad_normed, gproj, gtaps, ghead, gwide = layer_backward(
+            bounds, (grad_branch * scale).astype(BF16), twice_rows, weights, taps, head, wide, spread, saved
         )
-        grad_normed = lax.psum_scatter(part, "tensor", scatter_dimension=0, tiled=True).astype(F32)
         grad_weights = jnp.concatenate(
             [dot_tn(spread_grad, gained).astype(BF16), dot_tn(rows, gproj).astype(BF16)], axis=1
         )
@@ -495,6 +749,7 @@
     seq_pos = dev_grid * pos_here + pos_grid
     live_slot = (seq_pos < my_lengths[None, :, None]).reshape(-1, 1)
     source = jnp.minimum(my_offsets[None, :, None] + seq_pos, BIN - 1).reshape(-1)
+    source = (source % BLK // SHARE) * (BIN // 4) + source // BLK * SHARE + source % SHARE
     rank_of = jnp.zeros_like(packing).at[packing].set(jnp.arange(seq_total, dtype=jnp.int32))
 
     def from_bins(rows):

time: 991 us -> 754 us (0.76)
  waiting for transfers between devices: 486 us -> 130 us
  Pallas kernels: 139 us -> 281 us
    all_gather x4 -> x0, waiting for transfers between devices: 127 us -> none  [the longest x2 71.7 us: on_device(): rows = lax.all_gather(normed.astype(BF16), 'tensor', axis=0, tiled=True)]
    reduce_scatter x2, waiting for transfers between devices: 111 us -> 0.01 us  [on_device(): lax.psum_scatter(grad_weights, 'dp', scatter_dimension=0, tiled=True)]
    reduce_scatter x4 -> x0, waiting for transfers between devices: 79.6 us -> none  [on_device(): lax.psum_scatter(part, 'tensor', scatter_dimension=0, tiled=True)]
    pallas_call x2, Pallas kernels: 56.8 us -> 136 us  [layer_forward(): pl.pallas_call(forward_kernel, grid=(blocks,), in_specs=[pl.BlockSpec(mem...]
    all_gather x2, waiting for transfers between devices: 67.7 us -> 0.02 us  [on_device(): weights = lax.all_gather(own, 'dp', axis=0, tiled=True)]
    pallas_call x2, Pallas kernels: 82.3 us -> 146 us  [layer_backward(): pl.pallas_call(backward_kernel, grid=(blocks,), in_specs=[pl.BlockSpec(me...]
    all_to_all x1 -> x2, waiting for transfers between devices: 48.3 us -> 94.1 us  [to_bins(): lax.all_to_all(given[groups], 'dp', split_axis=0, concat_axis=0, tiled=True)]
    all_to_all x2 -> x1, waiting for transfers between devices: 43.7 us -> 0.01 us  [from_bins(): lax.all_to_all(slots, 'dp', split_axis=0, concat_axis=0, tiled=True)]
  transfers between devices with their start and end apart: 19 -> 12, of which waited for: 14 -> 6; matrix products, arithmetic and copies ran while one was open for 13% -> 15% of each run, Pallas kernels for 0% -> 19%
where the time goes in v2:
time: 754 us; the launch traced here: 747 us
  Pallas kernels  281 us (37%)
  blocking collectives  137 us (18%)
  waiting for transfers between devices  130 us (17%)
  local copies, waits for them, and re-layouts  85.7 us (11%)
  other arithmetic  36.7 us (5%)
  starting transfers between devices  35.5 us (5%)
  matrix products  26.3 us (3%)
  between operations  14.7 us (2%)
    pallas_call x2, Pallas kernels, layer_backward(): pl.pallas_call(backward_kernel, grid=(blocks,), in_specs=[pl.BlockSpec(me...  146 us
    pallas_call x2, Pallas kernels, layer_forward(): pl.pallas_call(forward_kernel, grid=(blocks,), in_specs=[pl.BlockSpec(mem...  136 us
    all_to_all x2, waiting for transfers between devices, to_bins(): lax.all_to_all(given[groups], 'dp', split_axis=0, concat_axis=0, tiled=True)  94.1 us
    all_to_all x1, blocking collectives, from_bins(): lax.all_to_all(slots, 'dp', split_axis=0, concat_axis=0, tiled=True)  54.3 us
    psum x1, blocking collectives, on_device(): lax.psum(heads_first + shared, 'dp')  49 us
    dot_general x4, matrix products, dot_tn(): lax.dot_general(left, right, (((0,), (0,)), ((), ())), preferred_element_...  26.3 us
    gather x2, local copies, waits for them, and re-layouts, from_bins(): columns[source]  26.1 us
    psum x1, waiting for transfers between devices, on_device(): lax.psum((shared_convbc, shared_pre, shared_bc), 'tensor')  25 us
  transfers between devices with their start and end apart: 12, of which 6 were waited for; matrix products, arithmetic and copies ran while one was open for 15% of the time, Pallas kernels for 19%

profile of v2, /device:TPU:1, one launch (start us, length us, event | category | flops | bytes accessed | tf_op | source)
XLA Modules:
  0.0 747.2 jit_solution(8668352142848930376)
XLA Ops:
  16.0 6.5 all-to-all-start.4
  25.2 49.2 %all-to-all-done.4 = bf16[8,3,128,256]{3,2,1,0:T(8,128)(2,1)S(1)} async-done(((bf16[8,3,128,256]{3,2,1,0:T(8,128)(2,1)}), bf16[8,3,128,256]{3,2,1,0:T(8,128)(2,1)S(1)}, u32[]{:S(2)}, u32[]{:S(2)}) %all-to-all-start.4) | async-done | bytes 1572896 | tf_op jit(solution)/shard_map/all_to_all | solution.py:665
  74.4 6.8 all-to-all-start
  86.6 9.1 %gather_fusion.6 = bf16[2048,256]{1,0:T(8,128)(2,1)} fusion(bf16[3072,256]{1,0:T(8,128)(2,1)S(1)} %bitcast.126, s32[2048]{0:T(1024)S(1)} %broadcast_clamp_fusion.1), kind=kCustom, calls=%fused_computation.6 | custom fusion | bytes 2105344 | tf_op jit(solution)/shard_map/gather | solution.py:666
  95.7 44.9 %all-to-all-done = bf16[8,3,128,256]{3,2,1,0:T(8,128)(2,1)S(1)} async-done(((bf16[8,3,128,256]{3,2,1,0:T(8,128)(2,1)}), bf16[8,3,128,256]{3,2,1,0:T(8,128)(2,1)S(1)}, u32[]{:S(2)}, u32[]{:S(2)}) %all-to-all-start) | async-done | bytes 1572896 | tf_op jit(solution)/shard_map/all_to_all | solution.py:665
  140.5 4.5 all-to-all-start.5
  148.1 9.0 %gather_fusion.2 = bf16[2048,256]{1,0:T(8,128)(2,1)} fusion(bf16[3072,256]{1,0:T(8,128)(2,1)S(1)} %bitcast.127, s32[2048]{0:T(1024)S(1)} %broadcast_clamp_fusion.1), kind=kCustom, calls=%fused_computation.2 | custom fusion | bytes 2105344 | tf_op jit(solution)/shard_map/gather | solution.py:666
  159.7 4.3 all-to-all-start.1
  164.0 15.1 %all_gather.9 = bf16[2,1024]{1,0:T(2,128)(2,1)S(1)} all-gather(bf16[2,128]{1,0:T(2,128)(2,1)S(1)} %copy-done.26), channel_id=1, replica_groups=mesh['dp'=8,'tensor'=4] {'dp'}, dimensions={1}, use_global_device_ids=true | all-gather | bytes 4608 | tf_op jit(solution)/shard_map/all_gather | solution.py:670
  185.7 69.4 %layer_forward.2 = (bf16[2048,1024]{1,0:T(8,128)(2,1)}, f32[2048,512]{1,0:T(8,128)}, f32[2048,768]{1,0:T(8,128)}, f32[2048,768]{1,0:T(8,128)}, f32[2048,128]{1,0...) custom-call(s32[2]{0:T(128)} %slice_bitcast_fusion.9.off_ref, ...), custom_call_target="tpu_custom_call" | custom-call | tf_op jit(solution)/shard_map/layer_forward/pallas_call | solution.py:543
  255.1 66.2 %layer_forward.3 = (bf16[2048,1024]{1,0:T(8,128)(2,1)}, f32[2048,512]{1,0:T(8,128)}, f32[2048,768]{1,0:T(8,128)}, f32[2048,768]{1,0:T(8,128)}, f32[2048,128]{1,0...) custom-call(s32[2]{0:T(128)} %slice_bitcast_fusion.9.off_ref, ...), custom_call_target="tpu_custom_call" | custom-call | tf_op jit(solution)/shard_map/layer_forward/pallas_call | solution.py:543
  325.5 72.7 %layer_backward.2 = (bf16[2048,1024]{1,0:T(8,128)(2,1)}, f32[512,1024]{1,0:T(8,128)}, bf16[2048,1408]{1,0:T(8,128)(2,1)}, f32[8,768]{1,0:T(8,128)}, f32[8,128]{1,0:T(8,128)}, /*index=5*/f32[8,512]{1,0:T(8,128)}) custom-call(s32[2]{0:T(128)} %slice_bitcast_fusion.9.off_ref, bf16[512,1024]{1,0:T(8,128)(2,1)} %multiply_convert_fusion.own_ref, ...), custom_call_target="tpu_custom_call" | custom-call | tf_op jit(solution)/shard_map/layer_backward/pallas_call | solution.py:593
  398.1 9.1 %convolution_convert_fusion = bf16[1024,1408]{1,0:T(8,128)(2,1)S(1)} fusion(bf16[2048,1024]{1,0:T(8,128)(2,1)S(1)} %copy-done.27, bf16[2048,1408]{1,0:T(8,128)(2,1)} %get-tuple-element.75), kind=kOutput, calls=%fused_computation.12 | convolution fusion | flops 5907021824 | bytes 12845056 | tf_op jit(solution)/shard_map/dot_general | solution.py:31
  407.3 2.4 convolution_convert_fusion.2
  409.7 2.2 pad_maximum_fusion.1
  414.4 2.4 multiply_reduce_fusion
  420.2 2.8 fusion.own_ref
  423.5 72.9 %layer_backward.3 = (bf16[2048,1024]{1,0:T(8,128)(2,1)}, f32[512,1024]{1,0:T(8,128)}, bf16[2048,1408]{1,0:T(8,128)(2,1)}, f32[8,768]{1,0:T(8,128)}, f32[8,128]{1,0:T(8,128)}, /*index=5*/f32[8,512]{1,0:T(8,128)}) custom-call(s32[2]{0:T(128)} %slice_bitcast_fusion.9.off_ref, bf16[512,1024]{1,0:T(8,128)(2,1)} %fusion.own_ref, ...), custom_call_target="tpu_custom_call" | custom-call | tf_op jit(solution)/shard_map/layer_backward/pallas_call | solution.py:593
  496.4 4.5 convolution_convert_fusion.3
  501.5 10.2 %convolution_convert_fusion.1 = bf16[1024,1408]{1,0:T(8,128)(2,1)S(1)} fusion(bf16[2048,1024]{1,0:T(8,128)(2,1)} %get-tuple-element.70, bf16[2048,1408]{1,0:T(8,128)(2,1)} %get-tuple-element.71), kind=kOutput, calls=%fused_computation.13 | convolution fusion | flops 5907021824 | bytes 12845056 | tf_op jit(solution)/shard_map/dot_general | solution.py:31
  516.7 4.5 all-to-all-start.2
  521.2 2.3 multiply_reduce_fusion.1
  525.6 9.3 %all-to-all-done.2 = bf16[512,4,256]{2,0,1:T(8,128)(2,1)S(1)} async-done(((bf16[512,4,256]{2,0,1:T(8,128)(2,1)}), bf16[512,4,256]{2,0,1:T(8,128)(2,1)S(1)}, u32[]{:S(2)}, u32[]{:S(2)}) %all-to-all-start.2) | async-done | bytes 1048608 | tf_op jit(solution)/shard_map/all_to_all | solution.py:756
  534.9 4.4 all-to-all-start.6
  539.5 13.0 %gather_fusion.3 = bf16[3072,256]{1,0:T(8,128)(2,1)} fusion(bf16[2048,256]{1,0:T(8,128)(2,1)S(1)} %bitcast.124, s32[3072]{0:T(1024)S(1)} %broadcast_clamp_fusion), kind=kCustom, calls=%fused_computation.3 | custom fusion | bytes 3158016 | tf_op jit(solution)/shard_map/gather | solution.py:757
  552.9 13.0 %gather_fusion.7 = bf16[3072,256]{1,0:T(8,128)(2,1)} fusion(bf16[2048,256]{1,0:T(8,128)(2,1)S(1)} %bitcast.125, s32[3072]{0:T(1024)S(1)} %broadcast_clamp_fusion), kind=kCustom, calls=%fused_computation.7 | custom fusion | bytes 3158016 | tf_op jit(solution)/shard_map/gather | solution.py:757
  565.9 3.0 broadcast_select_fusion
  569.0 54.3 %all_to_all.84 = bf16[8,3,128,256]{3,2,1,0:T(8,128)(2,1)S(1)} all-to-all(bf16[8,3,128,256]{3,2,1,0:T(8,128)(2,1)S(1)} %get-tuple-element.154), channel_id=1, replica_groups=mesh['dp'=8,'tensor'=4] {'dp'}, dimensions={0} | all-to-all | bytes 3145728 | tf_op jit(solution)/shard_map/all_to_all | solution.py:758
  623.3 4.3 all-to-all-start.3
  631.9 49.0 %all-reduce.10 = (f32[2,1024]{1,0:T(2,128)S(1)}, f32[2,5,512]{2,1,0:T(8,128)S(1)}, f32[2,5,256]{2,1,0:T(8,128)S(1)}, f32[2,3,8]{2,1,0:T(4,128)S(1)}, f32[2,512]{1,0:T(2,128)}) all-reduce(f32[2,1024]{1,0:T(2,128)S(1)} %pad_maximum_fusion.5, f32[2,5,512]{2,1,0:T(8,128)S(1)} %pad_maximum_fusion.3, ...), channel_id=1, replica_groups=mesh['dp'=8,'tensor'=4] {'dp'}, use_global_device_ids=true, to_apply=%region_10.11 | all-reduce | flops 10800 | bytes 86400 | tf_op jit(solution)/shard_map/psum | solution.py:736
  681.5 18.4 %all-reduce.11 = (f32[2,1024]{1,0:T(2,128)S(1)}, f32[2,5,256]{2,1,0:T(8,128)S(1)}) all-reduce(f32[2,1024]{1,0:T(2,128)S(1)} %get-tuple-element.126, f32[2,5,256]{2,1,0:T(8,128)S(1)} %get-tuple-element.128), channel_id=1, replica_groups=mesh['dp'=8,'tensor'=4] {'tensor'}, use_global_device_ids=true, to_apply=%region_11.12 | all-reduce | flops 4608 | bytes 36864 | tf_op jit(solution)/shard_map/psum | solution.py:739
  713.8 25.0 %all-reduce.14.cloned.1.call-done = f32[2,128,256]{2,1,0:T(8,128)} async-done(((f32[2,128,256]{2,1,0:T(8,128)}), f32[2,128,256]{2,1,0:T(8,128)}) %all-reduce.14.cloned.1.call-update) | async-done | bytes 262160 | tf_op jit(solution)/shard_map/psum | solution.py:739
  (210 shorter events, 67.7 us)
Async XLA Ops:
  7.2 6.9 copy-start
  7.2 4.6 copy-start.15
  7.2 5.2 copy-start.18
  7.2 6.7 copy-start.25
  7.2 177.8 %all-gather.3.cloned.1.call-start = ((), (), s32[]{:S(2)}) async-start(), calls=%async_computation.10 | async-start | bytes 4423680 | tf_op jit(solution)/shard_map/all_gather | solution.py:688
  16.0 7.3 copy-start.13
  16.0 58.5 %all-to-all-start.4 = ((bf16[8,3,128,256]{3,2,1,0:T(8,128)(2,1)}), bf16[8,3,128,256]{3,2,1,0:T(8,128)(2,1)S(1)}, u32[]{:S(2)}, u32[]{:S(2)}) async-start(bf16[8,3,128,256]{3,2,1,0:T(8,128)(2,1)} %bitcast.40), calls=%async_computation.4 | async-start | bytes 3145728 | tf_op jit(solution)/shard_map/all_to_all | solution.py:665
  22.5 232.6 %all-gather.5.cloned.1.call-start = ((), (), s32[]{:S(2)}) async-start(), calls=%async_computation.11 | async-start | bytes 4423680 | tf_op jit(solution)/shard_map/all_gather | solution.py:688
  25.2 56.1 %copy-start.24 = (f32[2,3,8]{2,0,1:T(2,128)S(1)}, f32[2,3,8]{2,0,1:T(2,128)}, u32[]{:S(2)}) copy-start(f32[2,3,8]{2,0,1:T(2,128)} %param.25) | copy-start | bytes 580
  25.2 56.4 %copy-start.2 = (s32[24]{0:T(128)S(1)}, s32[24]{0:T(128)}, u32[]{:S(2)}) copy-start(s32[24]{0:T(128)} %param.16) | copy-start | bytes 292
  25.2 57.3 %copy-start.22 = (bf16[2,5,256]{2,0,1:T(2,128)(2,1)S(1)}, bf16[2,5,256]{2,0,1:T(2,128)(2,1)}, u32[]{:S(2)}) copy-start(bf16[2,5,256]{2,0,1:T(2,128)(2,1)} %param.24) | copy-start | bytes 15364
  25.2 57.5 %copy-start.19 = (bf16[2,5,512]{2,0,1:T(2,128)(2,1)S(1)}, bf16[2,5,512]{2,0,1:T(2,128)(2,1)}, u32[]{:S(2)}) copy-start(bf16[2,5,512]{2,0,1:T(2,128)(2,1)} %param.23) | copy-start | bytes 30724
  25.2 59.4 %copy-start.23 = (bf16[2,512]{1,0:T(2,128)(2,1)S(1)}, bf16[2,512]{1,0:T(2,128)(2,1)}, u32[]{:S(2)}) copy-start(bf16[2,512]{1,0:T(2,128)(2,1)} %param.26) | copy-start | bytes 6148
  74.4 66.1 %all-to-all-start = ((bf16[8,3,128,256]{3,2,1,0:T(8,128)(2,1)}), bf16[8,3,128,256]{3,2,1,0:T(8,128)(2,1)S(1)}, u32[]{:S(2)}, u32[]{:S(2)}) async-start(bf16[8,3,128,256]{3,2,1,0:T(8,128)(2,1)} %bitcast.135), calls=%async_computation | async-start | bytes 3145728 | tf_op jit(solution)/shard_map/all_to_all | solution.py:665
  140.5 18.2 %all-to-all-start.5 = ((bf16[4,512,256]{2,1,0:T(8,128)(2,1)}), bf16[4,512,256]{2,1,0:T(8,128)(2,1)S(1)}, u32[]{:S(2)}, u32[]{:S(2)}) async-start(bf16[4,512,256]{2,1,0:T(8,128)(2,1)} %bitcast.144), calls=%async_computation.5 | async-start | bytes 2097152 | tf_op jit(solution)/shard_map/all_to_all | solution.py:667
  157.1 6.9 copy-start.26
  159.7 23.2 %all-to-all-start.1 = ((bf16[4,512,256]{2,1,0:T(8,128)(2,1)}), bf16[4,512,256]{2,1,0:T(8,128)(2,1)S(1)}, u32[]{:S(2)}, u32[]{:S(2)}) async-start(bf16[4,512,256]{2,1,0:T(8,128)(2,1)} %bitcast.143), calls=%async_computation.1 | async-start | bytes 2097152 | tf_op jit(solution)/shard_map/all_to_all | solution.py:667
  164.0 541.4 %reduce-scatter.5.cloned.1.call-start = ((), (), s32[]{:S(2)}) async-start(), calls=%async_computation.13 | async-start | bytes 4423680 | tf_op jit(solution)/shard_map/reduce_scatter | solution.py:715
  255.1 66.2 %copy-start.5 = (f32[4,64,8,256]{3,2,0,1:T(8,128)S(1)}, f32[4,64,8,256]{3,2,0,1:T(8,128)}, u32[]{:S(2)}) copy-start(f32[4,64,8,256]{3,2,0,1:T(8,128)} %copy.99) | copy-start | bytes 6291460
  325.5 72.7 %copy-start.27 = (bf16[2048,1024]{1,0:T(8,128)(2,1)S(1)}, bf16[2048,1024]{1,0:T(8,128)(2,1)}, u32[]{:S(2)}) copy-start(bf16[2048,1024]{1,0:T(8,128)(2,1)} %get-tuple-element.74) | copy-start | bytes 12582916
  398.1 9.2 %copy-start.28 = (bf16[2048,1024]{1,0:T(8,128)(2,1)S(1)}, bf16[2048,1024]{1,0:T(8,128)(2,1)}, u32[]{:S(2)}) copy-start(bf16[2048,1024]{1,0:T(8,128)(2,1)} %get-tuple-element.72) | copy-start | bytes 12582916
  398.1 9.2 %copy-start.30 = (bf16[2048,512]{1,0:T(8,128)(2,1)S(1)}, bf16[2048,512]{1,0:T(8,128)(2,1)}, u32[]{:S(2)}) copy-start(bf16[2048,512]{1,0:T(8,128)(2,1)} %get-tuple-element.73) | copy-start | bytes 6291460
  411.9 293.4 %reduce-scatter.3.cloned.1.call-start = ((), (), s32[]{:S(2)}) async-start(), calls=%async_computation.12 | async-start | bytes 4423680 | tf_op jit(solution)/shard_map/reduce_scatter | solution.py:715
  423.5 72.9 %copy-start.29 = (bf16[2048,512]{1,0:T(8,128)(2,1)S(1)}, bf16[2048,512]{1,0:T(8,128)(2,1)}, u32[]{:S(2)}) copy-start(bf16[2048,512]{1,0:T(8,128)(2,1)} %get-tuple-element.69) | copy-start | bytes 6291460
  515.7 5.5 copy-start.4
  516.7 18.2 %all-to-all-start.2 = ((bf16[512,4,256]{2,0,1:T(8,128)(2,1)}), bf16[512,4,256]{2,0,1:T(8,128)(2,1)S(1)}, u32[]{:S(2)}, u32[]{:S(2)}) async-start(bf16[512,4,256]{2,0,1:T(8,128)(2,1)} %bitcast.141), calls=%async_computation.2 | async-start | bytes 2097152 | tf_op jit(solution)/shard_map/all_to_all | solution.py:756
  534.9 18.0 %all-to-all-start.6 = ((bf16[512,4,256]{2,0,1:T(8,128)(2,1)}), bf16[512,4,256]{2,0,1:T(8,128)(2,1)S(1)}, u32[]{:S(2)}, u32[]{:S(2)}) async-start(bf16[512,4,256]{2,0,1:T(8,128)(2,1)} %bitcast.117), calls=%async_computation.6 | async-start | bytes 2097152 | tf_op jit(solution)/shard_map/all_to_all | solution.py:756
  623.3 8.5 %copy-start.20 = (f32[8,768]{1,0:T(8,128)S(1)}, f32[8,768]{1,0:T(8,128)}, u32[]{:S(2)}) copy-start(f32[8,768]{1,0:T(8,128)} %get-tuple-element.77) | copy-start | bytes 73732
  623.3 8.5 %copy-start.21 = (f32[8,768]{1,0:T(8,128)S(1)}, f32[8,768]{1,0:T(8,128)}, u32[]{:S(2)}) copy-start(f32[8,768]{1,0:T(8,128)} %get-tuple-element.76) | copy-start | bytes 73732
  623.3 80.2 %all-to-all-start.3 = ((bf16[8,3,128,256]{3,2,1,0:T(8,128)(2,1)}), bf16[8,3,128,256]{3,2,1,0:T(8,128)(2,1)S(1)}, u32[]{:S(2)}, u32[]{:S(2)}) async-start(bf16[8,3,128,256]{3,2,1,0:T(8,128)(2,1)} %get-tuple-element.155), calls=%async_computation.3 | async-start | bytes 3145728 | tf_op jit(solution)/shard_map/all_to_all | solution.py:758
  627.6 111.2 %all-reduce.14.cloned.1.call-start = ((), (), s32[]{:S(2)}) async-start(), calls=%async_computation.14 | async-start | bytes 524288 | tf_op jit(solution)/shard_map/psum | solution.py:739
  708.3 32.1 %copy-start.1 = (bf16[24,128,256]{2,1,0:T(8,128)(2,1)S(1)}, bf16[24,128,256]{2,1,0:T(8,128)(2,1)}, u32[]{:S(2)}) copy-start(bf16[24,128,256]{2,1,0:T(8,128)(2,1)} %param.15) | copy-start | bytes 4718596
  (11 other events, 22.3 us)
Sparse Core Ops, SparseCore 0:
  14.0 122.0 all-gather.2
  138.9 67.9 all-gather.4
  412.1 81.1 reduce-scatter.4
  514.1 105.4 reduce-scatter.2
  708.4 30.3 all-reduce.13

commit v3 on v2

--- a/solution.py
+++ b/solution.py
@@ -113,9 +113,9 @@
 
     def greet(self):
         barrier = pltpu.get_barrier_semaphore()
-        for other in (self.sibling, self.across):
+        for other in (self.sibling, self.across, self.beyond):
             pl.semaphore_signal(barrier, inc=1, device_id={"tensor": other}, device_id_type=pl.DeviceIdType.MESH)
-        pl.semaphore_wait(barrier, 2)
+        pl.semaphore_wait(barrier, greet_dp(barrier) + 3)
 
     def slot(self, owner):
         return ((self.low + owner % 2) % 2) * 2 + (self.high + owner // 2) % 2
@@ -128,13 +128,110 @@
         )
 
 
-def gather_copy(ring, kind, block, own, rows):
+def greet_dp(barrier):
+    count, me = lax.axis_size("dp"), lax.axis_index("dp")
+
+    @pl.loop(1, count)
+    def _(step):
+        pl.semaphore_signal(
+            barrier, inc=1, device_id={"dp": (me + step) % count}, device_id_type=pl.DeviceIdType.MESH
+        )
+
+    return count - 1
+
+
+class BinExchange:
+    def __init__(self, to_bins, source, target, sems):
+        self.to_bins, self.source, self.target, self.sems = to_bins, source, target, sems
+        self.count, self.me = lax.axis_size("dp"), lax.axis_index("dp")
+        self.span = source.shape[2] if to_bins else target.shape[2]
+
+    def pieces(self, other):
+        if self.to_bins:
+            return self.source.at[other], self.target.at[:, pl.ds(self.me * self.span, self.span), :]
+        return self.source.at[:, pl.ds(other * self.span, self.span), :], self.target.at[self.me]
+
+    def remote(self, step, other):
+        source, target = self.pieces(other)
+        return pltpu.make_async_remote_copy(
+            src_ref=source, dst_ref=target, send_sem=self.sems.at[step, 0], recv_sem=self.sems.at[step, 1],
+            device_id={"dp": other}, device_id_type=pl.DeviceIdType.MESH,
+        )
+
+    def local(self):
+        source, target = self.pieces(self.me)
+        return pltpu.make_async_copy(source, target, self.sems.at[0, 0])
+
+    def start(self):
+        self.local().start()
+
+        @pl.loop(1, self.count)
+        def _(step):
+            self.remote(step, (self.me + step) % self.count).start()
+
+    def wait(self):
+        self.local().wait()
+
+        @pl.loop(1, self.count)
+        def _(step):
+            self.remote(step, (self.me + step) % self.count).wait()
+
+
+class RowExchange:
+    def __init__(self, to_rows, source, target, sems):
+        self.to_rows, self.source, self.target, self.sems = to_rows, source, target, sems
+        self.me = lax.axis_index("tensor")
+        self.columns = source.shape[2] if to_rows else target.shape[2]
+
+    def pieces(self, other):
+        if self.to_rows:
+            return (
+                self.source.at[:, pl.ds(other * SHARE, SHARE), :],
+                self.target.at[:, :, pl.ds(pl.multiple_of(self.me * self.columns, LANES), self.columns)],
+            )
+        return (
+            self.source.at[:, :, pl.ds(pl.multiple_of(other * self.columns, LANES), self.columns)],
+            self.target.at[:, pl.ds(self.me * SHARE, SHARE), :],
+        )
+
+    def remote(self, step):
+        other = (self.me + step) % 4
+        source, target = self.pieces(other)
+        return pltpu.make_async_remote_copy(
+            src_ref=source, dst_ref=target, send_sem=self.sems.at[step, 0], recv_sem=self.sems.at[step, 1],
+            device_id={"tensor": other}, device_id_type=pl.DeviceIdType.MESH,
+        )
+
+    def local(self):
+        source, target = self.pieces(self.me)
+        return pltpu.make_async_copy(source, target, self.sems.at[0, 0])
+
+    def start(self):
+        self.local().start()
+        for step in range(1, 4):
+            self.remote(step).start()
+
+    def wait(self):
+        self.local().wait()
+        for step in range(1, 4):
+            self.remote(step).wait()
+
+
+def row_place(rows, member):
+    return rows.at[:, pl.ds(member * SHARE, SHARE), :]
+
+
+def column_place(rows, member):
+    columns = rows.shape[2] // 4
+    return rows.at[:, :, pl.ds(pl.multiple_of(member * columns, LANES), columns)]
+
+
+def gather_copy(ring, kind, block, own, rows, place):
     if kind == AG_PASS:
-        passed = rows.at[block, pl.ds(ring.across * SHARE, SHARE), :]
+        passed = place(rows, ring.across).at[block]
         return ring.copy(kind, block, passed, passed, ring.sibling)
-    mine = own.at[pl.ds(block * SHARE, SHARE), :]
-    place = rows.at[block, pl.ds(ring.me * SHARE, SHARE), :]
-    return ring.copy(kind, block, mine, place, ring.sibling if kind == AG_OWN else ring.across)
+    other = ring.sibling if kind == AG_OWN else ring.across
+    return ring.copy(kind, block, own.at[block], place(rows, ring.me).at[block], other)
 
 
 def pair_copy(ring, block, parts, from_pair):
@@ -171,10 +268,14 @@
 
 
 def forward_kernel(
-    off_ref, own_ref, hid_ref, w_ref, taps_ref, head_ref, wide_ref, spread_ref, next_ref,
+    from_columns, make_side,
+    off_ref, own_ref, hid_ref, w_ref, taps_ref, head_ref, wide_ref, spread_ref, gains_ref, side_in_ref,
     rows_ref, z_ref, in_ref, pre_ref, dt_ref, y_ref, gg_ref, st_ref, hnext_ref, tot_ref, scale_ref, normed_ref,
-    state, padded, rows, parts, from_pair, sums, from_across, sq_own, sq_pair, sq_sums, sq_across, sems,
+    side_out_ref,
+    state, padded, rows, parts, from_pair, sums, from_across, sq_own, sq_pair, sq_sums, sq_across, sems, *side_scratch,
 ):
+    place = column_place if from_columns else row_place
+    side = make_side(off_ref, side_in_ref, side_out_ref, *side_scratch)
     block = pl.program_id(0)
     inner = y_ref.shape[1]
     mixed = in_ref.shape[1]
@@ -188,30 +289,36 @@
     def sq_across_copy(at):
         return ring.copy(SM_ACROSS, at, sq_sums.at[at], sq_across.at[at], ring.across)
 
+    def own_copy():
+        return pltpu.make_async_copy(own_ref, place(rows, ring.me), sems.at[SM_PAIR, blocks, 0])
+
     @pl.when(block == 0)
     def _():
+        own_copy().start()
         ring.greet()
 
         @pl.loop(0, blocks)
         def _(at):
-            gather_copy(ring, AG_ACROSS, at, own_ref, rows).start()
-            gather_copy(ring, AG_OWN, at, own_ref, rows).start()
+            gather_copy(ring, AG_ACROSS, at, own_ref, rows, place).start()
+            gather_copy(ring, AG_OWN, at, own_ref, rows, place).start()
+
+        side.start()
 
         state[...] = jnp.zeros_like(state)
         padded[pl.ds(0, 8), :] = jnp.zeros((8, mixed), F32)
-
-        @pl.loop(0, blocks)
-        def _(at):
-            rows[at, pl.ds(ring.me * SHARE, SHARE), :] = own_ref[pl.ds(at * SHARE, SHARE), :]
-
-        gather_copy(ring, AG_ACROSS, 0, own_ref, rows).wait_recv()
-        gather_copy(ring, AG_PASS, 0, own_ref, rows).start()
-
-    gather_copy(ring, AG_OWN, block, own_ref, rows).wait_recv()
-    gather_copy(ring, AG_PASS, block, own_ref, rows).wait_recv()
+        own_copy().wait()
+        gather_copy(ring, AG_ACROSS, 0, own_ref, rows, place).wait_recv()
+        gather_copy(ring, AG_PASS, 0, own_ref, rows, place).start()
+
+    gather_copy(ring, AG_OWN, block, own_ref, rows, place).wait_recv()
+    gather_copy(ring, AG_PASS, block, own_ref, rows, place).wait_recv()
     here = rows[block]
+    gains = gains_ref[...]
+    if from_columns:
+        raw = here.astype(F32)
+        mean = jnp.sum(raw * raw, axis=1, keepdims=True) / raw.shape[1]
+        here = (raw * lax.rsqrt(mean + eps) * gains[1:2]).astype(BF16)
     rows_ref[...] = here
-
     row_col, row_row, seg_col, seg_row = block_frame(block, first, second)
     seg_start = jnp.where(seg_col == 0, 0, jnp.where(seg_col == 1, first, second))
     within = row_col - seg_start
@@ -287,48 +394,55 @@
         squares = own_column((sq_sums[at] + sq_across[at])[0:1], ring.me * SHARE)
         scale = lax.rsqrt(squares / INNER + eps)
         here = pl.ds(at * SHARE, SHARE)
-        hidden = hid_ref[here, :] + total * scale
+        if from_columns:
+            before = rows[at, pl.ds(ring.me * SHARE, SHARE), :].astype(F32)
+            hid_ref[here, :] = before
+        else:
+            before = hid_ref[here, :]
+        hidden = before + total * scale
         hnext_ref[here, :] = hidden
         tot_ref[here, :] = total
         scale_ref[here, :] = scale
         mean = jnp.sum(hidden * hidden, axis=1, keepdims=True) / hidden.shape[1]
-        normed_ref[here, :] = (hidden * lax.rsqrt(mean + eps) * next_ref[0:1]).astype(BF16)
+        normed_ref[here, :] = (hidden * lax.rsqrt(mean + eps) * gains[0:1]).astype(BF16)
+
+    side.during(block)
 
     @pl.when(block < blocks - 1)
     def _():
-        gather_copy(ring, AG_ACROSS, block + 1, own_ref, rows).wait_recv()
-        gather_copy(ring, AG_PASS, block + 1, own_ref, rows).start()
+        gather_copy(ring, AG_ACROSS, block + 1, own_ref, rows, place).wait_recv()
+        gather_copy(ring, AG_PASS, block + 1, own_ref, rows, place).start()
 
     @pl.when(block >= 1)
     def _():
         second_stage(block - 1)
 
-    @pl.when(block >= 2)
-    def _():
-        last_stage(block - 2)
-
     @pl.when(block == blocks - 1)
     def _():
         second_stage(block)
-        last_stage(block - 1)
-        last_stage(block)
 
         @pl.loop(0, blocks)
         def _(at):
+            last_stage(at)
             for kind in (AG_OWN, AG_ACROSS, AG_PASS):
-                gather_copy(ring, kind, at, own_ref, rows).wait_send()
+                gather_copy(ring, kind, at, own_ref, rows, place).wait_send()
             pair_copy(ring, at, parts, from_pair).wait_send()
             across_copy(ring, at, sums, from_across).wait_send()
             sq_pair_copy(at).wait_send()
             sq_across_copy(at).wait_send()
 
+        side.finish()
+
 
 def backward_kernel(
+    make_side,
     off_ref, own_ref, tw_ref, w_ref, taps_ref, head_ref, wide_ref, spread_ref,
-    z_ref, in_ref, pre_ref, dt_ref, y_ref, st_ref,
-    rows_ref, gnormed_ref, gproj_ref, gtaps_ref, ghead_ref, gwide_ref,
-    dstate, padded, rows, parts, from_pair, sums, from_across, twice, sems,
+    z_ref, in_ref, pre_ref, dt_ref, y_ref, st_ref, side_in_ref,
+    rows_ref, gnormed_ref, gproj_ref, gtaps_ref, ghead_ref, gwide_ref, side_out_ref,
+    dstate, padded, rows, parts, from_pair, sums, from_across, twice, sems, *side_scratch,
 ):
+    place = row_place
+    side = make_side(off_ref, side_in_ref, side_out_ref, *side_scratch)
     step = pl.program_id(0)
     block = pl.num_programs(0) - 1 - step
     inner = y_ref.shape[1]
@@ -344,8 +458,12 @@
             ring.copy(SM_PAIR, 1, twice.at[ring.across], twice.at[ring.across], ring.sibling),
         )
 
+    def own_copy():
+        return pltpu.make_async_copy(own_ref, place(rows, ring.me), sems.at[SM_PAIR, blocks, 0])
+
     @pl.when(step == 0)
     def _():
+        own_copy().start()
         ring.greet()
         to_sibling, to_across, onward = twice_copies()
         to_across.start()
@@ -353,18 +471,16 @@
 
         @pl.loop(0, blocks)
         def _(at):
-            gather_copy(ring, AG_ACROSS, blocks - 1 - at, own_ref, rows).start()
-            gather_copy(ring, AG_OWN, blocks - 1 - at, own_ref, rows).start()
-
-        @pl.loop(0, blocks)
-        def _(at):
-            rows[at, pl.ds(ring.me * SHARE, SHARE), :] = own_ref[pl.ds(at * SHARE, SHARE), :]
-
+            gather_copy(ring, AG_ACROSS, blocks - 1 - at, own_ref, rows, place).start()
+            gather_copy(ring, AG_OWN, blocks - 1 - at, own_ref, rows, place).start()
+
+        side.start()
         twice[ring.me] = tw_ref[...]
+        own_copy().wait()
         to_across.wait_recv()
         onward.start()
-        gather_copy(ring, AG_ACROSS, blocks - 1, own_ref, rows).wait_recv()
-        gather_copy(ring, AG_PASS, blocks - 1, own_ref, rows).start()
+        gather_copy(ring, AG_ACROSS, blocks - 1, own_ref, rows, place).wait_recv()
+        gather_copy(ring, AG_PASS, blocks - 1, own_ref, rows, place).start()
         to_sibling.wait_recv()
         onward.wait_recv()
         dstate[...] = jnp.zeros_like(dstate)
@@ -373,8 +489,8 @@
         ghead_ref[...] = jnp.zeros_like(ghead_ref)
         gwide_ref[...] = jnp.zeros_like(gwide_ref)
 
-    gather_copy(ring, AG_OWN, block, own_ref, rows).wait_recv()
-    gather_copy(ring, AG_PASS, block, own_ref, rows).wait_recv()
+    gather_copy(ring, AG_OWN, block, own_ref, rows, place).wait_recv()
+    gather_copy(ring, AG_PASS, block, own_ref, rows, place).wait_recv()
     here = rows[block]
     rows_ref[...] = here
     twice_here = jnp.concatenate([own_column(twice[owner, block][0:1], 0) for owner in range(4)], axis=0)
@@ -487,37 +603,37 @@
         across_copy(ring, at, sums, from_across).wait_recv()
         gnormed_ref[pl.ds(at * SHARE, SHARE), :] = add_all(at, parts, from_pair, from_across)
 
+    side.during(step)
+
     @pl.when(step < blocks - 1)
     def _():
-        gather_copy(ring, AG_ACROSS, block - 1, own_ref, rows).wait_recv()
-        gather_copy(ring, AG_PASS, block - 1, own_ref, rows).start()
+        gather_copy(ring, AG_ACROSS, block - 1, own_ref, rows, place).wait_recv()
+        gather_copy(ring, AG_PASS, block - 1, own_ref, rows, place).start()
 
     @pl.when(step >= 1)
     def _():
         second_stage(block + 1)
 
-    @pl.when(step >= 2)
-    def _():
-        last_stage(block + 2)
-
     @pl.when(step == blocks - 1)
     def _():
         second_stage(block)
-        last_stage(block + 1)
-        last_stage(block)
         for copy in twice_copies():
             copy.wait_send()
 
         @pl.loop(0, blocks)
-        def _(at):
+        def _(turn):
+            at = blocks - 1 - turn
+            last_stage(at)
             for kind in (AG_OWN, AG_ACROSS, AG_PASS):
-                gather_copy(ring, kind, at, own_ref, rows).wait_send()
+                gather_copy(ring, kind, at, own_ref, rows, place).wait_send()
             pair_copy(ring, at, parts, from_pair).wait_send()
             across_copy(ring, at, sums, from_across).wait_send()
 
+        side.finish()
+
 
 def whole(shape):
-    return pl.BlockSpec(shape, lambda b: (0,) * len(shape))
+    return pl.BlockSpec(shape, lambda *at: (0,) * len(shape))
 
 
 def exchange_scratch(blocks, width):
@@ -530,31 +646,45 @@
     ]
 
 
-def layer_forward(offsets, own, hidden, weights, taps, head, wide, spread, next_gain):
-    own_rows, width = own.shape
-    count = 4 * own_rows
+def layer_forward(offsets, own, hidden, weights, taps, head, wide, spread, gains, side, side_given):
+    from_columns = hidden is None
+    blocks, width = own.shape[0], gains.shape[1]
+    count = blocks * BLK
+    own_rows = count // 4
     inner, mixed = wide.shape[1], taps.shape[1]
-    blocks = count // BLK
     total = weights.shape[1]
 
     def by_block(columns):
         return pl.BlockSpec((BLK, columns), lambda b: (b, 0))
 
+    hidden_specs = [] if from_columns else [whole((own_rows, width))]
+    before_specs = [whole((own_rows, width))] if from_columns else []
+    before_shapes = [jax.ShapeDtypeStruct((own_rows, width), F32)] if from_columns else []
+
+    def kernel(*refs):
+        if from_columns:
+            refs = refs[:2] + (refs[9],) + refs[2:9] + refs[10:]
+        forward_kernel(from_columns, side.make, *refs)
+
     return pl.pallas_call(
-        forward_kernel,
+        kernel,
         grid=(blocks,),
-        in_specs=[
-            pl.BlockSpec(memory_space=pltpu.SMEM),
-            whole((own_rows, width)), whole((own_rows, width)), whole((width, total)), whole((8, mixed)),
-            whole((8, LANES)), whole((8, inner)), whole((2 * LANES, inner)), whole((8, width)),
+        in_specs=[pl.BlockSpec(memory_space=pltpu.SMEM), whole(own.shape)]
+        + hidden_specs
+        + [
+            whole((width, total)), whole((8, mixed)), whole((8, LANES)), whole((8, inner)),
+            whole((2 * LANES, inner)), whole((8, width)), side.given_spec,
         ],
-        out_specs=[
+        out_specs=before_specs
+        + [
             by_block(width), by_block(inner), by_block(mixed), by_block(mixed),
             by_block(LANES), by_block(inner), by_block(inner),
             pl.BlockSpec((1, STATE, inner), lambda b: (b, 0, 0)),
             whole((own_rows, width)), whole((own_rows, width)), whole((own_rows, 1)), whole((own_rows, width)),
+            side.result_spec,
         ],
-        out_shape=[
+        out_shape=before_shapes
+        + [
             jax.ShapeDtypeStruct((count, width), BF16),
             jax.ShapeDtypeStruct((count, inner), F32),
             jax.ShapeDtypeStruct((count, mixed), F32),
@@ -567,42 +697,46 @@
             jax.ShapeDtypeStruct((own_rows, width), F32),
             jax.ShapeDtypeStruct((own_rows, 1), F32),
             jax.ShapeDtypeStruct((own_rows, width), BF16),
+            side.result,
         ],
         scratch_shapes=[pltpu.VMEM((STATE, inner), F32), pltpu.VMEM((BLK + 8, mixed), F32)]
         + exchange_scratch(blocks, width)
         + [pltpu.VMEM((blocks, 8, BLK), F32)] * 4
-        + [pltpu.SemaphoreType.DMA((7, blocks, 2))],
+        + [pltpu.SemaphoreType.DMA((7, blocks + 1, 2))]
+        + side.scratch,
         compiler_params=pltpu.CompilerParams(
-            vmem_limit_bytes=56 * 1024 * 1024, collective_id=1, has_side_effects=True
+            vmem_limit_bytes=56 * 1024 * 1024, collective_id=side.collective_id, has_side_effects=True
         ),
+        cost_estimate=pl.CostEstimate(flops=6 * 10**10, bytes_accessed=6 * 10**7, transcendentals=10**7),
         name="layer_forward",
-    )(offsets, own, hidden, weights, taps, head, wide, spread, next_gain)
-
-
-def layer_backward(offsets, own, twice, weights, taps, head, wide, spread, saved):
+    )(offsets, own, *([] if from_columns else [hidden]), weights, taps, head, wide, spread, gains, side_given)
+
+
+def layer_backward(offsets, own, twice, weights, taps, head, wide, spread, saved, side, side_given):
     gate, mixed_in, conv, dt_raw, mixed_out, states = saved
-    own_rows, width = own.shape
-    count = 4 * own_rows
+    blocks, width = own.shape[0], own.shape[2]
+    count = blocks * BLK
+    own_rows = count // 4
     inner, mixed = wide.shape[1], taps.shape[1]
-    blocks = count // BLK
     total = weights.shape[1]
 
     def by_block(columns):
         return pl.BlockSpec((BLK, columns), lambda b: (blocks - 1 - b, 0))
 
     return pl.pallas_call(
-        backward_kernel,
+        functools.partial(backward_kernel, side.make),
         grid=(blocks,),
         in_specs=[
             pl.BlockSpec(memory_space=pltpu.SMEM),
-            whole((own_rows, width)), whole((blocks, 8, LANES)), whole((width, total)), whole((8, mixed)),
+            whole(own.shape), whole((blocks, 8, LANES)), whole((width, total)), whole((8, mixed)),
             whole((8, LANES)), whole((8, inner)), whole((2 * LANES, inner)),
             by_block(inner), by_block(mixed), by_block(mixed), by_block(LANES), by_block(inner),
             pl.BlockSpec((1, STATE, inner), lambda b: (blocks - 1 - b, 0, 0)),
+            side.given_spec,
         ],
         out_specs=[
             by_block(width), whole((own_rows, width)), by_block(total - inner),
-            whole((8, mixed)), whole((8, LANES)), whole((8, inner)),
+            whole((8, mixed)), whole((8, LANES)), whole((8, inner)), side.result_spec,
         ],
         out_shape=[
             jax.ShapeDtypeStruct((count, width), BF16),
@@ -611,22 +745,605 @@
             jax.ShapeDtypeStruct((8, mixed), F32),
             jax.ShapeDtypeStruct((8, LANES), F32),
             jax.ShapeDtypeStruct((8, inner), F32),
+            side.result,
         ],
         scratch_shapes=[pltpu.VMEM((STATE, inner), F32), pltpu.VMEM((BLK + 8, mixed), F32)]
         + exchange_scratch(blocks, width)
         + [pltpu.VMEM((4, blocks, 8, LANES), F32)]
-        + [pltpu.SemaphoreType.DMA((7, blocks, 2))],
+        + [pltpu.SemaphoreType.DMA((7, blocks + 1, 2))]
+        + side.scratch,
         compiler_params=pltpu.CompilerParams(
-            vmem_limit_bytes=56 * 1024 * 1024, collective_id=2, has_side_effects=True
+            vmem_limit_bytes=56 * 1024 * 1024, collective_id=side.collective_id, has_side_effects=True
         ),
+        cost_estimate=pl.CostEstimate(flops=6 * 10**10, bytes_accessed=6 * 10**7, transcendentals=10**7),
         name="layer_backward",
-    )(offsets, own, twice, weights, taps, head, wide, spread, gate, mixed_in, conv, dt_raw, mixed_out, states)
+    )(offsets, own, twice, weights, taps, head, wide, spread, gate, mixed_in, conv, dt_raw, mixed_out, states, side_given)
 
 
 def spread_matrix(inner, heads):
     lane_head = lax.broadcasted_iota(jnp.int32, (2 * LANES, inner), 1) // (inner // heads)
     row_head = lax.broadcasted_iota(jnp.int32, (2 * LANES, inner), 0) % LANES
     return jnp.where(lane_head == row_head, 1.0, 0.0).astype(BF16)
+
+
+SEQ_MIN = 512
+
+
+def choose_rows(wanted, valid, begin, end):
+    slots = begin + lax.broadcasted_iota(jnp.int32, (wanted.shape[0], end - begin), 1)
+    return jnp.where((slots == wanted) & valid, 1.0, 0.0).astype(BF16)
+
+
+def pick_all(off_ref, arrived, cols):
+    first, second = off_ref[0], off_ref[1]
+    length = arrived.shape[1]
+    for block in range(cols.shape[0]):
+        low, high = block * BLK, (block + 1) * BLK
+        row = low + lax.broadcasted_iota(jnp.int32, (BLK, 1), 0)
+        total = None
+        for member, begin, least, most in ((1, first, SEQ_MIN, length), (2, second, BIN - length, BIN - SEQ_MIN)):
+            reach = BIN - SEQ_MIN if member == 1 else BIN
+            start, end = max(low - most, 0), min(high - least, length)
+            if end <= 0 or start >= length or low >= reach:
+                continue
+            valid = (row >= first) & (row < second) if member == 1 else row >= second
+            term = dot_nn(choose_rows(row - begin, valid, start, end), arrived[member, start:end, :])
+            total = term if total is None else total + term
+        if high <= length:
+            own = arrived[0, low:high, :].astype(F32)
+            own = jnp.where(row < first, own, 0.0)
+            total = own if total is None else total + own
+        cols[block] = total.astype(BF16)
+
+
+def place_all(off_ref, cols, slots):
+    first, second = off_ref[0], off_ref[1]
+    length = slots.shape[1]
+    for chunk in range(length // BLK):
+        low, high = chunk * BLK, (chunk + 1) * BLK
+        position = low + lax.broadcasted_iota(jnp.int32, (BLK, 1), 0)
+        slots[0, low:high, :] = jnp.where(position < first, cols[low:high, :].astype(F32), 0.0).astype(BF16)
+        for member, begin, stop, least, most, reach in (
+            (1, first, second, SEQ_MIN, length, BIN - SEQ_MIN),
+            (2, second, BIN, BIN - length, BIN - SEQ_MIN, BIN),
+        ):
+            wanted = begin + position
+            start, end = least + low, min(most + high, reach)
+            choose = choose_rows(wanted, wanted < stop, start, end)
+            slots[member, low:high, :] = dot_nn(choose, cols[start:end, :]).astype(BF16)
+
+
+class LineGather:
+    def __init__(self, own, target, sems):
+        self.own, self.target, self.sems = own, target, sems
+        me = lax.axis_index("dp")
+        self.me, self.low, self.high = me, me % 2, me // 2
+        self.line = lax.axis_size("dp") // 2
+        self.span = own.shape[0]
+
+    def copy(self, kind, place, other, own):
+        here = self.target.at[pl.ds((place * 2 + self.low) * self.span, self.span), :]
+        arrival = 2 if kind == 2 else 3
+        return pltpu.make_async_remote_copy(
+            src_ref=self.own if own else here, dst_ref=here,
+            send_sem=self.sems.at[kind, place], recv_sem=self.sems.at[arrival + 1, place],
+            device_id={"dp": other}, device_id_type=pl.DeviceIdType.MESH,
+        )
+
+    def right(self, place, own=False):
+        return self.copy(0, place, (self.high + 1) * 2 + self.low, own)
+
+    def left(self, place, own=False):
+        return self.copy(1, place, (self.high - 1) * 2 + self.low, own)
+
+    def pair(self, place, own=False):
+        return self.copy(2, place, self.high * 2 + 1 - self.low, own)
+
+    def local(self):
+        here = self.target.at[pl.ds(self.me * self.span, self.span), :]
+        return pltpu.make_async_copy(self.own, here, self.sems.at[5, 0])
+
+    def start(self):
+        self.local().start()
+
+        @pl.when(self.high < self.line - 1)
+        def _():
+            self.right(self.high, True).start()
+
+        @pl.when(self.high > 0)
+        def _():
+            self.left(self.high, True).start()
+
+        self.pair(self.high, True).start()
+
+    def stage(self, step):
+        @pl.when(self.high - step >= 0)
+        def _():
+            self.right(self.high - step).wait_recv()
+
+            @pl.when(self.high < self.line - 1)
+            def _():
+                self.right(self.high - step).start()
+
+            self.pair(self.high - step).start()
+
+        @pl.when(self.high + step < self.line)
+        def _():
+            self.left(self.high + step).wait_recv()
+
+            @pl.when(self.high > 0)
+            def _():
+                self.left(self.high + step).start()
+
+            self.pair(self.high + step).start()
+
+    def finish(self):
+        self.local().wait()
+
+        @pl.loop(0, self.line)
+        def _(place):
+            self.pair(place).wait_recv()
+            self.pair(place).wait_send()
+
+            @pl.when((self.high < self.line - 1) & (place <= self.high))
+            def _():
+                self.right(place).wait_send()
+
+            @pl.when((self.high > 0) & (place >= self.high))
+            def _():
+                self.left(place).wait_send()
+
+
+class TileGather:
+    def __init__(self, own, target, sems):
+        self.own, self.target, self.sems = own, target, sems
+        self.count, self.me = lax.axis_size("dp"), lax.axis_index("dp")
+
+    def remote(self, step):
+        return pltpu.make_async_remote_copy(
+            src_ref=self.own, dst_ref=self.target.at[self.me],
+            send_sem=self.sems.at[step, 0], recv_sem=self.sems.at[step, 1],
+            device_id={"dp": (self.me + step) % self.count}, device_id_type=pl.DeviceIdType.MESH,
+        )
+
+    def start(self):
+        self.target[self.me] = self.own[...]
+
+        @pl.loop(1, self.count)
+        def _(step):
+            self.remote(step).start()
+
+    def wait(self):
+        @pl.loop(1, self.count)
+        def _(step):
+            self.remote(step).wait()
+
+
+def start_kernel(
+    off_ref, sorted_ref, own_ref, gain_ref, cols_ref, gains_ref, weights_ref, arrived, bin_sems, line_sems, tile_sems
+):
+    barrier = pltpu.get_barrier_semaphore()
+    pl.semaphore_wait(barrier, greet_dp(barrier))
+    line = LineGather(own_ref, weights_ref, line_sems)
+    bins = BinExchange(True, sorted_ref, arrived, bin_sems)
+    gains = TileGather(gain_ref, gains_ref, tile_sems)
+    gains.start()
+    line.start()
+    bins.start()
+
+    @pl.loop(1, line.line)
+    def _(step):
+        line.stage(step)
+
+    bins.wait()
+    pick_all(off_ref, arrived, cols_ref)
+    line.finish()
+    gains.wait()
+
+
+def start_exchange(offsets, given, own, gain):
+    count, members, span, columns = given.shape
+    return pl.pallas_call(
+        start_kernel,
+        in_specs=[
+            pl.BlockSpec(memory_space=pltpu.SMEM),
+            pl.BlockSpec(memory_space=pltpu.VMEM),
+            pl.BlockSpec(memory_space=pltpu.VMEM),
+            pl.BlockSpec(memory_space=pltpu.VMEM),
+        ],
+        out_specs=[
+            pl.BlockSpec(memory_space=pltpu.VMEM),
+            pl.BlockSpec(memory_space=pltpu.VMEM),
+            pl.BlockSpec(memory_space=pltpu.HBM),
+        ],
+        out_shape=[
+            jax.ShapeDtypeStruct((BIN // BLK, BLK, columns), BF16),
+            jax.ShapeDtypeStruct((count,) + gain.shape, F32),
+            jax.ShapeDtypeStruct((count * own.shape[0], own.shape[1]), BF16),
+        ],
+        scratch_shapes=[
+            pltpu.VMEM((members, count * span, columns), BF16),
+            pltpu.SemaphoreType.DMA((count, 2)),
+            pltpu.SemaphoreType.DMA((6, count // 2)),
+            pltpu.SemaphoreType.DMA((count, 2)),
+        ],
+        compiler_params=pltpu.CompilerParams(
+            vmem_limit_bytes=32 * 1024 * 1024, collective_id=5, has_side_effects=True
+        ),
+        cost_estimate=pl.CostEstimate(flops=6 * 10**10, bytes_accessed=6 * 10**7, transcendentals=0),
+        name="start_exchange",
+    )(offsets, given, own, gain)
+
+
+class LineReduce:
+    def __init__(self, given, out, pair_buf, from_left, from_right, sems):
+        self.given, self.out, self.pair_buf = given, out, pair_buf
+        self.from_left, self.from_right, self.sems = from_left, from_right, sems
+        me = lax.axis_index("dp")
+        self.low, self.high = me % 2, me // 2
+        self.line = lax.axis_size("dp") // 2
+        self.span = out.shape[0]
+
+    def chunk(self, place, low):
+        return pl.ds((place * 2 + low) * self.span, self.span)
+
+    def pair(self, place):
+        return pltpu.make_async_remote_copy(
+            src_ref=self.given.at[self.chunk(place, 1 - self.low), :], dst_ref=self.pair_buf.at[place],
+            send_sem=self.sems.at[0, place], recv_sem=self.sems.at[1, place],
+            device_id={"dp": self.high * 2 + 1 - self.low}, device_id_type=pl.DeviceIdType.MESH,
+        )
+
+    def onward(self, place, right):
+        target = self.from_left if right else self.from_right
+        other = (self.high + 1 if right else self.high - 1) * 2 + self.low
+        return pltpu.make_async_remote_copy(
+            src_ref=self.pair_buf.at[place], dst_ref=target.at[place],
+            send_sem=self.sems.at[2, place], recv_sem=self.sems.at[3 if right else 4, place],
+            device_id={"dp": other}, device_id_type=pl.DeviceIdType.MESH,
+        )
+
+    def by_distance(self, step, act):
+        distance = self.line - 1 - step
+
+        @pl.when(self.high + distance < self.line)
+        def _():
+            act(self.high + distance, True)
+
+        @pl.when(self.high - distance >= 0)
+        def _():
+            act(self.high - distance, False)
+
+    def send_pairs(self):
+        @pl.loop(0, self.line - 1)
+        def _(step):
+            self.by_distance(step, lambda place, right: self.pair(place).start())
+
+        self.pair(self.high).start()
+
+    def fold(self, place):
+        return self.given[self.chunk(place, self.low), :].astype(F32) + self.pair_buf[place].astype(F32)
+
+    def pass_on(self, place, right):
+        self.pair(place).wait_recv()
+        upstream = (self.high > 0) if right else (self.high < self.line - 1)
+        source = self.from_left if right else self.from_right
+
+        @pl.when(upstream)
+        def _():
+            self.onward(place, right).wait_recv()
+            self.pair_buf[place] = (self.fold(place) + source[place].astype(F32)).astype(BF16)
+
+        @pl.when(jnp.logical_not(upstream))
+        def _():
+            self.pair_buf[place] = self.fold(place).astype(BF16)
+
+        self.onward(place, right).start()
+
+    def stage(self, step):
+        self.by_distance(step, self.pass_on)
+
+    def finish(self):
+        here = self.high
+        self.pair(here).wait_recv()
+        self.out[...] = self.fold(here)
+
+        @pl.when(here > 0)
+        def _():
+            self.onward(here, True).wait_recv()
+            self.out[...] += self.from_left[here].astype(F32)
+
+        @pl.when(here < self.line - 1)
+        def _():
+            self.onward(here, False).wait_recv()
+            self.out[...] += self.from_right[here].astype(F32)
+
+        @pl.loop(0, self.line)
+        def _(place):
+            self.pair(place).wait_send()
+
+            @pl.when(place != here)
+            def _():
+                self.onward(place, True).wait_send()
+
+
+def line_scratch(count, span, columns):
+    line = count // 2
+    return [pltpu.VMEM((line, span, columns), BF16)] * 3 + [pltpu.SemaphoreType.DMA((5, line))]
+
+
+class WeightsSide:
+    collective_id = 1
+    given_spec = pl.BlockSpec(memory_space=pltpu.HBM)
+    result_spec = pl.BlockSpec(memory_space=pltpu.HBM)
+
+    def __init__(self, own):
+        self.count = lax.axis_size("dp")
+        self.result = jax.ShapeDtypeStruct((self.count * own.shape[0], own.shape[1]), BF16)
+        self.scratch = [pltpu.SemaphoreType.DMA((6, self.count // 2))]
+
+    def make(self, off_ref, given, result, sems):
+        line = LineGather(given, result, sems)
+        count = line.line
+
+        def during(step):
+            if count != 4:
+                return
+            for stage in (1, 2, 3):
+
+                @pl.when(step == 2 * stage - 1)
+                def _(stage=stage):
+                    line.stage(stage)
+
+        def finish():
+            if count != 4:
+
+                @pl.loop(1, count)
+                def _(stage):
+                    line.stage(stage)
+
+            line.finish()
+
+        return Side(line.start, during, finish)
+
+
+class Side:
+    def __init__(self, start, during, finish):
+        self.start, self.during, self.finish = start, during, finish
+
+
+class ArriveSide:
+    collective_id = 2
+    given_spec = pl.BlockSpec(memory_space=pltpu.HBM)
+    result_spec = pl.BlockSpec(memory_space=pltpu.HBM)
+
+    def __init__(self, given):
+        count, members, span, columns = given.shape
+        blocks = BIN // BLK
+        self.result = jax.ShapeDtypeStruct((blocks, SHARE, 4 * columns), BF16)
+        self.scratch = [
+            pltpu.VMEM((members, count * span, columns), BF16),
+            pltpu.VMEM((blocks, BLK, columns), BF16),
+            pltpu.SemaphoreType.DMA((count, 2)),
+            pltpu.SemaphoreType.DMA((4, 2)),
+        ]
+
+    def make(self, off_ref, given, result, arrived, cols, bin_sems, row_sems):
+        bins = BinExchange(True, given, arrived, bin_sems)
+        rows = RowExchange(True, cols, result, row_sems)
+
+        def during(step):
+            @pl.when(step == cols.shape[0] - 2)
+            def _():
+                bins.wait()
+                pick_all(off_ref, arrived, cols)
+                rows.start()
+
+        return Side(bins.start, during, rows.wait)
+
+
+class ReturnSide:
+    collective_id = 3
+    given_spec = pl.BlockSpec(memory_space=pltpu.HBM)
+    result_spec = pl.BlockSpec(memory_space=pltpu.HBM)
+
+    def __init__(self, count, span, columns):
+        blocks = BIN // BLK
+        self.result = jax.ShapeDtypeStruct((count, 3, span, columns), BF16)
+        self.scratch = [
+            pltpu.VMEM((BIN, columns), BF16),
+            pltpu.VMEM((3, count * span, columns), BF16),
+            pltpu.SemaphoreType.DMA((4, 2)),
+            pltpu.SemaphoreType.DMA((count, 2)),
+        ]
+
+    def make(self, off_ref, given, result, cols, slots, row_sems, bin_sems):
+        rows = RowExchange(False, given, cols.reshape(BIN // BLK, BLK, cols.shape[1]), row_sems)
+        bins = BinExchange(False, slots, result, bin_sems)
+
+        def during(step):
+            @pl.when(step == 2)
+            def _():
+                rows.wait()
+                place_all(off_ref, cols, slots)
+                bins.start()
+
+        return Side(rows.start, during, bins.wait)
+
+
+class GradientSide:
+    collective_id = 4
+    given_spec = pl.BlockSpec(memory_space=pltpu.VMEM)
+
+    def __init__(self, count, given):
+        span, columns = given.shape[0] // count, given.shape[1]
+        self.result = jax.ShapeDtypeStruct((span, columns), F32)
+        self.result_spec = whole((span, columns))
+        self.scratch = line_scratch(count, span, columns)
+
+    def make(self, off_ref, given, result, pair_buf, from_left, from_right, sems):
+        line = LineReduce(given, result, pair_buf, from_left, from_right, sems)
+        count = line.line
+
+        def during(step):
+            if count != 4:
+                return
+            for stage in (0, 1, 2):
+
+                @pl.when(step == 2 * stage + 2)
+                def _(stage=stage):
+                    line.stage(stage)
+
+        def finish():
+            if count != 4:
+
+                @pl.loop(0, count - 1)
+                def _(stage):
+                    line.stage(stage)
+
+            line.finish()
+
+        return Side(line.send_pairs, during, finish)
+
+
+class MemberGather:
+    def __init__(self, target, sems):
+        self.target, self.sems = target, sems
+        self.me = lax.axis_index("tensor")
+
+    def remote(self, step):
+        return pltpu.make_async_remote_copy(
+            src_ref=self.target.at[self.me], dst_ref=self.target.at[self.me],
+            send_sem=self.sems.at[step, 0], recv_sem=self.sems.at[step, 1],
+            device_id={"tensor": (self.me + step) % 4}, device_id_type=pl.DeviceIdType.MESH,
+        )
+
+    def start(self):
+        for step in range(1, 4):
+            self.remote(step).start()
+
+    def wait(self):
+        for step in range(1, 4):
+            self.remote(step).wait()
+
+
+def end_kernel(
+    off_ref, grad_ref, rows_ref, gproj_ref, sg_ref, gg_ref, tile_ref, later_ref,
+    back_ref, pack_ref, sum_ref, maps_ref,
+    cols, slots, packs, pair_buf, from_left, from_right, line_sems, tiles, shared, maps,
+    row_sems, bin_sems, tile_sems, shared_sems, maps_sems,
+):
+    ring = Ring(None)
+    ring.greet()
+    inner = gg_ref.shape[1]
+    first_map = 3 * inner
+    rows = RowExchange(False, grad_ref, cols.reshape(BIN // BLK, BLK, cols.shape[1]), row_sems)
+    bins = BinExchange(False, slots, back_ref, bin_sems)
+    line = LineReduce(packs, pack_ref, pair_buf, from_left, from_right, line_sems)
+    dp_tiles = TileGather(tile_ref, tiles, tile_sems)
+    shared_tiles = MemberGather(shared, shared_sems)
+    shared_maps = MemberGather(maps, maps_sems)
+    rows.start()
+    dp_tiles.start()
+
+    def compute(place):
+        width = 2 * line.span
+        lanes = pl.ds(pl.multiple_of(place * width, LANES), width)
+        here = pl.ds(place * width, width)
+        packs[here, :inner] = dot_tn(sg_ref[:, lanes], gg_ref[...]).astype(BF16)
+        packs[here, inner:] = dot_tn(rows_ref[:, lanes], gproj_ref[...]).astype(BF16)
+
+    if 2 * line.span % LANES == 0:
+
+        @pl.loop(0, line.line - 1)
+        def _(step):
+            def act(place, right):
+                compute(place)
+                line.pair(place).start()
+
+            line.by_distance(step, act)
+
+        compute(line.high)
+        line.pair(line.high).start()
+    else:
+
+        @pl.loop(0, packs.shape[0] // BLK)
+        def _(turn):
+            here = pl.ds(pl.multiple_of(turn * BLK, BLK), BLK)
+            packs[here, :inner] = dot_tn(sg_ref[:, here], gg_ref[...]).astype(BF16)
+            packs[here, inner:] = dot_tn(rows_ref[:, here], gproj_ref[...]).astype(BF16)
+
+        line.send_pairs()
+
+    rows.wait()
+    place_all(off_ref, cols, slots)
+    bins.start()
+
+    @pl.loop(0, line.line - 1)
+    def _(step):
+        line.stage(step)
+
+    dp_tiles.wait()
+    sum_ref[...] = tiles[0]
+
+    @pl.loop(1, tiles.shape[0])
+    def _(at):
+        sum_ref[...] += tiles[at]
+
+    shared[ring.me] = sum_ref[pl.ds(0, shared.shape[1]), :]
+    shared_tiles.start()
+    line.finish()
+    maps[ring.me, 0] = pack_ref[:, first_map : first_map + 2 * STATE].astype(BF16)
+    maps[ring.me, 1] = later_ref[...].astype(BF16)
+    shared_maps.start()
+    shared_tiles.wait()
+    sum_ref[pl.ds(0, shared.shape[1]), :] = shared[0] + shared[1] + shared[2] + shared[3]
+    shared_maps.wait()
+    for layer in range(LAYERS):
+        maps_ref[layer] = (maps[0, layer].astype(F32) + maps[1, layer].astype(F32)) + (
+            maps[2, layer].astype(F32) + maps[3, layer].astype(F32)
+        )
+    bins.wait()
+
+
+def end_exchange(offsets, grad_rows, rows, gproj, spread_grad, gained, tile, shared_rows, later_maps, span):
+    count = lax.axis_size("dp")
+    width, inner, total = rows.shape[1], gained.shape[1], gained.shape[1] + gproj.shape[1]
+    columns = width // 4
+    vmem = pl.BlockSpec(memory_space=pltpu.VMEM)
+    pack_rows = width // count
+    return pl.pallas_call(
+        end_kernel,
+        in_specs=[pl.BlockSpec(memory_space=pltpu.SMEM)] + [vmem] * 7,
+        out_specs=[pl.BlockSpec(memory_space=pltpu.HBM), vmem, vmem, vmem],
+        out_shape=[
+            jax.ShapeDtypeStruct((count, 3, span, columns), BF16),
+            jax.ShapeDtypeStruct((pack_rows, total), F32),
+            jax.ShapeDtypeStruct(tile.shape, F32),
+            jax.ShapeDtypeStruct((LAYERS, pack_rows, 2 * STATE), F32),
+        ],
+        scratch_shapes=[
+            pltpu.VMEM((BIN, columns), BF16),
+            pltpu.VMEM((3, count * span, columns), BF16),
+            pltpu.VMEM((width, total), BF16),
+        ]
+        + line_scratch(count, pack_rows, total)
+        + [
+            pltpu.VMEM((count,) + tile.shape, F32),
+            pltpu.VMEM((4, shared_rows, LANES), F32),
+            pltpu.VMEM((4, LAYERS, pack_rows, 2 * STATE), BF16),
+            pltpu.SemaphoreType.DMA((4, 2)),
+            pltpu.SemaphoreType.DMA((count, 2)),
+            pltpu.SemaphoreType.DMA((count, 2)),
+            pltpu.SemaphoreType.DMA((4, 2)),
+            pltpu.SemaphoreType.DMA((4, 2)),
+        ],
+        compiler_params=pltpu.CompilerParams(
+            vmem_limit_bytes=56 * 1024 * 1024, collective_id=6, has_side_effects=True
+        ),
+        cost_estimate=pl.CostEstimate(flops=6 * 10**10, bytes_accessed=6 * 10**7, transcendentals=0),
+        name="end_exchange",
+    )(offsets, grad_rows, rows, gproj, spread_grad, gained, tile, later_maps)
 
 
 def pre_norm(hidden, gain_full):
@@ -650,24 +1367,11 @@
     triples = lengths[packing].reshape(dp_count, 3)
     offsets = jnp.cumsum(triples, axis=1) - triples
     my_offsets = offsets[bin_index]
-    my_lengths = triples[bin_index]
     bounds = my_offsets[1:3]
-    bin_rows = jnp.arange(BIN, dtype=jnp.int32)
-    segment = segment_of(bin_rows, my_offsets[1], my_offsets[2])
-    seg_start = jnp.where(segment == 0, my_offsets[0], jnp.where(segment == 1, my_offsets[1], my_offsets[2]))
-    within = bin_rows - seg_start
-    pick_rows = (within // pos_here * 3 + segment) * pos_here + within % pos_here
+    groups = packing.reshape(dp_count, 3)
     blocks = BIN // BLK
-    pick_rows = jnp.swapaxes(pick_rows.reshape(blocks, 4, SHARE), 0, 1).reshape(-1)
-    groups = packing.reshape(dp_count, 3)
-
-    def to_bins(given):
-        arrived = lax.all_to_all(given[groups], "dp", split_axis=0, concat_axis=0, tiled=True)
-        flat = arrived.reshape(-1, cols_here)[pick_rows]
-        return lax.all_to_all(flat, "tensor", split_axis=0, concat_axis=1, tiled=True)
 
     spread = spread_matrix(inner_part, heads_here)
-    gains = lax.all_gather(pre_gain, "dp", axis=1, tiled=True).astype(F32)
     packs = []
     for layer in range(LAYERS):
         own = jnp.concatenate(
@@ -680,86 +1384,107 @@
         )
         packs.append((own, pad_to(taps, 8, mixed), pad_to(head, 8, LANES), pad_to(wide, 8, inner_part)))
 
-    row_tokens = to_bins(tokens)
-    hidden = row_tokens.astype(F32)
+    columns, gain_tiles, first_weights = start_exchange(
+        bounds, tokens[groups], packs[0][0], pad_to(pre_gain.astype(F32), 8, LANES)
+    )
+    gains = jnp.swapaxes(gain_tiles[:, :LAYERS, :dp_rows], 0, 1).reshape(LAYERS, dp_count * dp_rows)
+    given_cot = cotangent[groups]
+    own, hidden, weights = columns, None, first_weights
     records = []
     for layer in range(LAYERS):
-        own, taps, head, wide = packs[layer]
-        weights = lax.all_gather(own, "dp", axis=0, tiled=True)
-        before = hidden
-        if layer == 0:
-            normed = pre_norm(hidden, gains[layer]).astype(BF16)
-        rows, gate, mixed_in, conv, dt_raw, mixed_out, gained, states, hidden, total, scale, normed = layer_forward(
-            bounds, normed, hidden, weights, taps, head, wide, spread,
-            jnp.broadcast_to(gains[min(layer + 1, LAYERS - 1)], (8, gains.shape[1])),
-        )
+        _, taps, head, wide = packs[layer]
+        pair = pad_to(jnp.stack([gains[min(layer + 1, LAYERS - 1)], gains[layer]]), 8, gains.shape[1])
+        side_given = packs[1][0] if layer == 0 else given_cot
+        side = WeightsSide(side_given) if layer == 0 else ArriveSide(side_given)
+        results = layer_forward(bounds, own, hidden, weights, taps, head, wide, spread, pair, side, side_given)
+        before = results[0] if layer == 0 else hidden
+        (
+            rows, gate, mixed_in, conv, dt_raw, mixed_out, gained, states, hidden, total, scale, normed, side_out,
+        ) = results[1:] if layer == 0 else results
         saved = (gate, mixed_in, conv, dt_raw, mixed_out, states)
         records.append((before, rows, weights, gained, total, scale, saved))
-    final_rows = hidden.astype(BF16)
-
-    grad_hidden = to_bins(cotangent).astype(F32)
+        own = normed.reshape(blocks, SHARE, -1)
+        weights = side_out
+    grad_hidden = side_out.reshape(BIN // 4, -1).astype(F32)
+    side, side_given = ReturnSide(dp_count, pos_here, cols_here), hidden.astype(BF16).reshape(own.shape)
     collected = [None] * LAYERS
     for layer in reversed(range(LAYERS)):
-        own, taps, head, wide = packs[layer]
+        _, taps, head, wide = packs[layer]
         before, rows, weights, gained, total, scale, saved = records[layer]
         normed, norm_back = jax.vjp(pre_norm, before, gains[layer])
         grad_branch = grad_hidden.astype(BF16).astype(F32)
         twice = 2.0 * (-(scale**3) / (2 * INNER)) * jnp.sum(grad_branch * total, axis=1, keepdims=True)
         twice_rows = jnp.broadcast_to(pad_to(twice.reshape(blocks, SHARE), blocks, LANES)[:, None], (blocks, 8, LANES))
-        spread_grad, grad_normed, gproj, gtaps, ghead, gwide = layer_backward(
-            bounds, (grad_branch * scale).astype(BF16), twice_rows, weights, taps, head, wide, spread, saved
+        spread_grad, grad_normed, gproj, gtaps, ghead, gwide, side_out = layer_backward(
+            bounds, (grad_branch * scale).astype(BF16).reshape(own.shape), twice_rows, weights, taps, head, wide, spread,
+            saved, side, side_given,
         )
-        grad_weights = jnp.concatenate(
-            [dot_tn(spread_grad, gained).astype(BF16), dot_tn(rows, gproj).astype(BF16)], axis=1
-        )
-        own_weights = lax.psum_scatter(grad_weights, "dp", scatter_dimension=0, tiled=True)
         grad_before, grad_gain = norm_back(grad_normed)
         grad_hidden = grad_hidden + grad_before
-        collected[layer] = (own_weights, grad_gain, gtaps, ghead, gwide)
-
-    heads_first = (
-        jnp.stack([item[2][: CONV + 1, :inner_part] for item in collected]),
-        jnp.stack(
-            [
-                jnp.concatenate(
-                    [item[3][:2, :heads_here], jnp.sum(item[4][0:1].reshape(1, heads_here, -1), axis=2)], axis=0
-                )
-                for item in collected
-            ]
-        ),
-        jnp.stack([item[4][1] for item in collected]),
+        collected[layer] = (grad_gain, gtaps, ghead, gwide)
+        if layer == LAYERS - 1:
+            activations_back = side_out
+            side_given = jnp.concatenate(
+                [dot_tn(spread_grad, gained).astype(BF16), dot_tn(rows, gproj).astype(BF16)], axis=1
+            )
+            side = GradientSide(dp_count, side_given)
+
+    pieces = []
+    for grad_gain, gtaps, ghead, gwide in collected:
+        pieces += [gtaps[: CONV + 1, inner_part:].reshape(-1, LANES), grad_gain.reshape(-1, LANES)]
+    shared_rows = sum(piece.shape[0] for piece in pieces)
+    gap = -shared_rows % 8
+    pieces.append(jnp.zeros((gap, LANES), F32))
+    for grad_gain, gtaps, ghead, gwide in collected:
+        pieces += [gtaps[: CONV + 1, :inner_part].reshape(-1, LANES), ghead[:2], gwide[:2].reshape(-1, LANES)]
+    tile = jnp.concatenate(pieces, axis=0)
+    tile = pad_to(tile, tile.shape[0] + -tile.shape[0] % 8, LANES)
+    later_pack = side_out
+    first_map = 3 * inner_part
+    returned, first_pack, sums, maps = end_exchange(
+        bounds, grad_hidden.astype(BF16).reshape(own.shape), rows, gproj, spread_grad, gained, tile, shared_rows + gap,
+        later_pack[:, first_map : first_map + 2 * STATE], pos_here,
     )
-    shared = (
-        jnp.stack([item[2][: CONV + 1, inner_part:] for item in collected]),
-        jnp.stack([item[1] for item in collected]),
+    taken = 0
+
+    def take(shape):
+        nonlocal taken
+        rows_here = 1
+        for size in shape:
+            rows_here *= size
+        rows_here //= LANES
+        piece = sums[taken : taken + rows_here].reshape(shape)
+        taken += rows_here
+        return piece
+
+    convbc, pre = zip(*[(take((CONV + 1, 2 * STATE)), take((gains.shape[1],))) for _ in range(LAYERS)])
+    taken += gap
+    convx, heads, wides = zip(
+        *[(take((CONV + 1, inner_part)), take((2, LANES)), take((2, inner_part))) for _ in range(LAYERS)]
     )
-    grad_convx, grad_head, grad_norm, shared_convbc, shared_pre = lax.psum(heads_first + shared, "dp")
-    own_weights = jnp.stack([item[0] for item in collected])
-    shared_bc = own_weights[:, :, 3 * inner_part : 3 * inner_part + 2 * STATE].astype(F32)
-    grad_convbc, grad_pre, grad_bc = lax.psum((shared_convbc, shared_pre, shared_bc), "tensor")
-    shard_pre = lax.dynamic_slice_in_dim(grad_pre, bin_index * dp_rows, dp_rows, 1)
-    own_weights = own_weights.astype(F32)
+    grad_convbc, grad_convx = jnp.stack(convbc), jnp.stack(convx)
+    shard_pre = lax.dynamic_slice_in_dim(jnp.stack(pre), bin_index * dp_rows, dp_rows, 1)
+    grad_head = jnp.stack(
+        [
+            jnp.concatenate([head[:, :heads_here], jnp.sum(wide[0:1].reshape(1, heads_here, -1), axis=2)], axis=0)
+            for head, wide in zip(heads, wides)
+        ]
+    )
+    grad_norm = jnp.stack([wide[1] for wide in wides])
+    own_weights = jnp.stack([first_pack, later_pack])
+    grad_bc = maps
     grad_out = jnp.swapaxes(own_weights[:, :, :inner_part], 1, 2)
     grad_z = own_weights[:, :, inner_part : 2 * inner_part]
     grad_x = own_weights[:, :, 2 * inner_part : 3 * inner_part]
     grad_dt = own_weights[:, :, 3 * inner_part + 2 * STATE : 3 * inner_part + 2 * STATE + heads_here]
 
-    dev_grid = jnp.arange(dp_count, dtype=jnp.int32)[:, None, None]
-    pos_grid = jnp.arange(pos_here, dtype=jnp.int32)[None, None, :]
-    seq_pos = dev_grid * pos_here + pos_grid
-    live_slot = (seq_pos < my_lengths[None, :, None]).reshape(-1, 1)
-    source = jnp.minimum(my_offsets[None, :, None] + seq_pos, BIN - 1).reshape(-1)
-    source = (source % BLK // SHARE) * (BIN // 4) + source // BLK * SHARE + source % SHARE
     rank_of = jnp.zeros_like(packing).at[packing].set(jnp.arange(seq_total, dtype=jnp.int32))
 
-    def from_bins(rows):
-        columns = lax.all_to_all(rows, "tensor", split_axis=1, concat_axis=0, tiled=True)
-        slots = jnp.where(live_slot, columns[source], 0).reshape(dp_count, 3, pos_here, cols_here)
-        returned = lax.all_to_all(slots, "dp", split_axis=0, concat_axis=0, tiled=True)
+    def in_order(returned):
         return returned.reshape(seq_total, pos_here, cols_here)[rank_of]
 
-    activations = from_bins(final_rows)
-    input_grad = from_bins(grad_hidden.astype(BF16))
+    activations = in_order(activations_back)
+    input_grad = in_order(returned)
     return (
         activations, input_grad, shard_pre, grad_z, grad_x, grad_bc, grad_dt,
         grad_convx, grad_convbc, grad_head, grad_norm, grad_out,

time: 754 us -> 558 us (0.74)
  Pallas kernels: 281 us -> 472 us
  blocking collectives: 137 us -> 0 us
  waiting for transfers between devices: 130 us -> 0 us
  local copies, waits for them, and re-layouts: 85.7 us -> 38.3 us
  starting transfers between devices: 35.5 us -> 0 us
  matrix products: 26.3 us -> 12 us
  between operations: 14.7 us -> 1.68 us
  other arithmetic: 36.7 us -> 24.1 us
    pallas_call x4 -> x6, Pallas kernels: 281 us -> 472 us  [the longest x2 157 us: layer_backward(): pl.pallas_call(functools.partial(backward_kernel, side.make), grid=(block...]
    all_to_all x7 -> x0, waiting for transfers between devices: 105 us -> none  [the longest x2 94.1 us: to_bins(): lax.all_to_all(given[groups], 'dp', split_axis=0, concat_axis=0, tiled=True)]
    psum x2 -> x0, blocking collectives: 67.4 us -> none  [the longest x1 49 us: on_device(): lax.psum(heads_first + shared, 'dp')]
    all_to_all x1 -> x0, blocking collectives: 54.3 us -> none  [from_bins(): lax.all_to_all(slots, 'dp', split_axis=0, concat_axis=0, tiled=True)]
    gather x8 -> x4, local copies, waits for them, and re-layouts: 51.6 us -> 8.07 us  [the longest x2 5.58 us: in_order(): return returned.reshape(seq_total, pos_here, cols_here)[rank_of]]
    all_to_all x7 -> x0, starting transfers between devices: 35.3 us -> none  [the longest x2 13.3 us: to_bins(): lax.all_to_all(given[groups], 'dp', split_axis=0, concat_axis=0, tiled=True)]
    psum x1 -> x0, waiting for transfers between devices: 25 us -> none  [on_device(): lax.psum((shared_convbc, shared_pre, shared_bc), 'tensor')]
    all_gather x1 -> x0, blocking collectives: 15.1 us -> none  [on_device(): gains = lax.all_gather(pre_gain, 'dp', axis=1, tiled=True).astype(F32)]
  transfers between devices with their start and end apart: 12 -> 0, of which waited for: 6 -> 0; matrix products, arithmetic and copies ran while one was open for 15% -> 0% of each run, Pallas kernels for 19% -> 0%
where the time goes in v3:
time: 558 us; the launch traced here: 548 us
  Pallas kernels  472 us (85%)
  local copies, waits for them, and re-layouts  38.3 us (7%)
  other arithmetic  24.1 us (4%)
  matrix products  12 us (2%)
    pallas_call x2, Pallas kernels, layer_backward(): pl.pallas_call(functools.partial(backward_kernel, side.make), grid=(block...  157 us
    pallas_call x2, Pallas kernels, layer_forward(): pl.pallas_call(kernel, grid=(blocks,), in_specs=[pl.BlockSpec(memory_spac...  138 us
    pallas_call x1, Pallas kernels, end_exchange(): pl.pallas_call(end_kernel, in_specs=[pl.BlockSpec(memory_space=pltpu.SMEM...  94.2 us
    pallas_call x1, Pallas kernels, start_exchange(): pl.pallas_call(start_kernel, in_specs=[pl.BlockSpec(memory_space=pltpu.SM...  82.7 us
    unnamed x92, local copies, waits for them, and re-layouts  14.3 us
    dot_general x2, matrix products, dot_tn(): lax.dot_general(left, right, (((0,), (0,)), ((), ())), preferred_element_...  12 us

profile of v3, /device:TPU:1, one launch (start us, length us, event | category | flops | bytes accessed | tf_op | source)
XLA Modules:
  0.0 547.8 jit_solution(11169242845023057973)
XLA Ops:
  0.7 1.1 fusion.37
  2.1 1.0 bitcast_dynamic-update-slice_fusion.3
  3.2 0.7 copy-done.28
  7.3 1.0 copy-done.3
  8.4 82.7 %start_exchange.1 = (bf16[8,256,256]{2,1,0:T(8,128)(2,1)S(1)}, f32[8,8,128]{2,1,0:T(8,128)S(1)}, bf16[1024,1920]{1,0:T(8,128)(2,1)S(1)}) custom-call(s32[2]{0:T(128)S(1)} %slice_bitcast_fusion.5.off_ref.refs_0_, bf16[8,3,128,256]{3,2,1,0:T(8,128)(2,1)S(1)} %bitcast.90, bf16[128,1920]{1,0:T(8,128)(2,1)S(1)} %copy-done.3, f32[8,128]{1,0:T(8,128)S(1)} %pad_convert_fusion.gain_ref), custom_call_target="tpu_custom_call" | custom-call | flops 60000002048 | bytes 60000000 | tf_op jit(solution)/shard_map/start_exchange/pallas_call | solution.py:946
  91.1 2.0 copy-done.5
  93.1 1.0 copy-done.6
  97.7 0.9 select_convert_fusion.refs_6_.refs_7_.spread_ref
  99.2 66.6 %layer_forward.2 = (f32[512,1024]{1,0:T(8,128)}, bf16[2048,1024]{1,0:T(8,128)(2,1)}, f32[2048,512]{1,0:T(8,128)}, f32[2048,768]{1,0:T(8,128)}, f32[2048,768]{1,0...) custom-call(s32[2]{0:T(128)} %copy-done.4, ...), custom_call_target="tpu_custom_call" | custom-call | flops 60000002048 | bytes 60000000 | tf_op jit(solution)/shard_map/layer_forward/pallas_call | solution.py:669
  167.0 1.8 gather_fusion.2
  168.9 71.1 %layer_forward.3 = (bf16[2048,1024]{1,0:T(8,128)(2,1)}, f32[2048,512]{1,0:T(8,128)}, f32[2048,768]{1,0:T(8,128)}, f32[2048,768]{1,0:T(8,128)}, f32[2048,128]{1,0...) custom-call(s32[2]{0:T(128)} %copy-done.4, ...), custom_call_target="tpu_custom_call" | custom-call | flops 60000002048 | bytes 60000000 | tf_op jit(solution)/shard_map/layer_forward/pallas_call | solution.py:669
  240.0 2.2 fusion.6
  242.3 1.3 fusion.13
  243.7 1.2 fusion.5.own_ref
  244.9 1.1 convert_element_type.85
  246.8 83.9 %layer_backward.2 = (bf16[2048,1024]{1,0:T(8,128)(2,1)}, f32[512,1024]{1,0:T(8,128)}, bf16[2048,1408]{1,0:T(8,128)(2,1)}, f32[8,768]{1,0:T(8,128)}, f32[8,128]{1...) custom-call(s32[2]{0:T(128)} %copy-done.4, bf16[8,64,1024]{2,1,0:T(8,128)(2,1)} %fusion.5.own_ref, ...), custom_call_target="tpu_custom_call" | custom-call | flops 60000002048 | bytes 60000000 | tf_op jit(solution)/shard_map/layer_backward/pallas_call | solution.py:726
  330.7 4.7 convolution_convert_fusion.1
  335.4 7.3 %convolution_convert_fusion = bf16[1024,1408]{1,0:T(8,128)(2,1)S(1)} fusion(bf16[2048,1024]{1,0:T(8,128)(2,1)S(1)} %copy-done.38, bf16[2048,1408]{1,0:T(8,128)(2,1)S(1)} %copy-done.37), kind=kOutput, calls=%fused_computation.7 | convolution fusion | flops 5907021824 | bytes 12845056 | tf_op jit(solution)/shard_map/dot_general | solution.py:31
  342.7 2.2 pad_maximum_fusion.side_in_ref
  345.3 1.2 copy-done.13
  347.2 0.9 copy-done.17
  348.1 0.9 fusion.1
  349.4 1.3 fusion
  351.4 73.4 %layer_backward.3 = (bf16[2048,1024]{1,0:T(8,128)(2,1)}, f32[512,1024]{1,0:T(8,128)}, bf16[2048,1408]{1,0:T(8,128)(2,1)}, f32[8,768]{1,0:T(8,128)}, f32[8,128]{1...) custom-call(s32[2]{0:T(128)} %copy-done.4, bf16[8,64,1024]{2,1,0:T(8,128)(2,1)} %bitcast.99, ...), custom_call_target="tpu_custom_call" | custom-call | flops 60000002048 | bytes 60000000 | tf_op jit(solution)/shard_map/layer_backward/pallas_call | solution.py:726
  426.5 1.4 copy-done.12
  432.6 3.8 fusion.4
  437.0 94.2 %end_exchange.1 = (bf16[8,3,128,256]{3,2,1,0:T(8,128)(2,1)}, f32[128,1920]{1,0:T(8,128)}, f32[104,128]{1,0:T(8,128)}, f32[2,128,256]{2,1,0:T(8,128)}) custom-call(s32[2]{0:T(128)} %copy-done.4, bf16[8,64,1024]{2,1,0:T(8,128)(2,1)} %bitcast.100, bf16[2048,1024]{1,0:T(8,128)(2,1)} %get-tuple-element.91.rows_ref, ...), custom_call_target="tpu_custom_call" | custom-call | flops 60000002048 | bytes 60000000 | tf_op jit(solution)/shard_map/end_exchange/pallas_call | solution.py:1315
  531.2 0.8 fusion.38
  535.7 2.4 fusion.9
  538.1 1.0 copy.57
  541.1 3.5 gather_fusion.4
  544.5 2.1 gather_fusion.3
  (182 shorter events, 25.5 us)
Async XLA Ops:
  0.6 6.0 %copy-start = (bf16[24,128,256]{2,1,0:T(8,128)(2,1)S(1)}, bf16[24,128,256]{2,1,0:T(8,128)(2,1)}, u32[]{:S(2)}) copy-start(bf16[24,128,256]{2,1,0:T(8,128)(2,1)} %param.14) | copy-start | bytes 4718596
  0.7 2.4 copy-start.20
  0.7 2.5 copy-start.23
  0.7 2.5 copy-start.32
  0.7 3.4 copy-start.34
  0.7 3.5 copy-start.7
  3.1 4.2 copy-start.35
  4.1 2.5 copy-start.2
  5.2 85.9 %copy-start.4 = (s32[2]{0:T(128)}, s32[2]{0:T(128)S(1)}, u32[]{:S(2)}) copy-start(s32[2]{0:T(128)S(1)} %slice_bitcast_fusion.5.off_ref.refs_0_) | copy-start | bytes 28
  8.4 87.7 %copy-start.33 = (f32[2,3,8]{2,0,1:T(2,128)S(1)}, f32[2,3,8]{2,0,1:T(2,128)}, u32[]{:S(2)}) copy-start(f32[2,3,8]{2,0,1:T(2,128)} %param.25) | copy-start | bytes 580
  8.4 88.6 %copy-start.31 = (bf16[2,512]{1,0:T(2,128)(2,1)S(1)}, bf16[2,512]{1,0:T(2,128)(2,1)}, u32[]{:S(2)}) copy-start(bf16[2,512]{1,0:T(2,128)(2,1)} %param.26) | copy-start | bytes 6148
  8.4 90.2 %copy-start.25 = (bf16[2,5,512]{2,0,1:T(2,128)(2,1)S(1)}, bf16[2,5,512]{2,0,1:T(2,128)(2,1)}, u32[]{:S(2)}) copy-start(bf16[2,5,512]{2,0,1:T(2,128)(2,1)} %param.23) | copy-start | bytes 30724
  8.4 90.2 %copy-start.30 = (bf16[2,5,256]{2,0,1:T(2,128)(2,1)S(1)}, bf16[2,5,256]{2,0,1:T(2,128)(2,1)}, u32[]{:S(2)}) copy-start(bf16[2,5,256]{2,0,1:T(2,128)(2,1)} %param.24) | copy-start | bytes 15364
  91.1 2.0 copy-start.5
  99.2 67.8 %copy-start.18 = (bf16[24,128,256]{2,1,0:T(8,128)(2,1)S(1)}, bf16[24,128,256]{2,1,0:T(8,128)(2,1)}, u32[]{:S(2)}) copy-start(bf16[24,128,256]{2,1,0:T(8,128)(2,1)} %param.15) | copy-start | bytes 4718596
  240.0 3.8 copy-start.11
  242.2 2.7 copy-start.16
  246.8 83.9 %copy-start.36 = (bf16[2048,512]{1,0:T(8,128)(2,1)S(1)}, bf16[2048,512]{1,0:T(8,128)(2,1)}, u32[]{:S(2)}) copy-start(bf16[2048,512]{1,0:T(8,128)(2,1)} %get-tuple-element.86) | copy-start | bytes 6291460
  246.8 88.6 %copy-start.38 = (bf16[2048,1024]{1,0:T(8,128)(2,1)S(1)}, bf16[2048,1024]{1,0:T(8,128)(2,1)}, u32[]{:S(2)}) copy-start(bf16[2048,1024]{1,0:T(8,128)(2,1)} %get-tuple-element.87) | copy-start | bytes 12582916
  330.6 4.7 copy-start.37
  342.7 2.4 copy-start.9
  344.9 1.6 copy-start.27
  349.0 2.4 copy-start.10
  351.4 74.8 %copy-start.8 = (f32[512,1024]{1,0:T(8,128)S(1)}, f32[512,1024]{1,0:T(8,128)}, u32[]{:S(2)}) copy-start(f32[512,1024]{1,0:T(8,128)} %get-tuple-element.90) | copy-start | bytes 6291460
  424.8 1.7 copy-start.26
  427.8 2.1 copy-start.29
  432.6 3.8 copy-start.14
  535.7 3.4 copy-start.24
  535.7 4.0 copy-start.15
  539.7 4.8 copy-start.19
  541.0 6.3 %copy-start.1 = (bf16[24,128,256]{2,1,0:T(8,128)(2,1)S(1)}, bf16[24,128,256]{2,1,0:T(8,128)(2,1)}, u32[]{:S(2)}) copy-start(bf16[24,128,256]{2,1,0:T(8,128)(2,1)} %param.14) | copy-start | bytes 4718596
  544.5 2.1 copy-start.22
  (7 other events, 8.7 us)

commit v4 on v3

v4 whole, which is shorter than its diff:
```python
import functools
import jax
import jax.numpy as jnp
from jax import lax
from jax.experimental import pallas as pl
from jax.experimental.pallas import tpu as pltpu
from jax.sharding import PartitionSpec as P

CONV = 4
INNER = 2048
LAYERS = 2
BIN = 2048
eps = 1e-05
STATE = 128
BLK = 256
LANES = 128
LOG2E = 1.4426950408889634
F32 = jnp.float32
BF16 = jnp.bfloat16


def dot_nn(left, right):
    return lax.dot_general(left, right, (((1,), (0,)), ((), ())), preferred_element_type=F32)


def dot_nt(left, right):
    return lax.dot_general(left, right, (((1,), (1,)), ((), ())), preferred_element_type=F32)


def dot_tn(left, right):
    return lax.dot_general(left, right, (((0,), (0,)), ((), ())), preferred_element_type=F32)


def split_two(values):
    high = values.astype(BF16)
    return high, (values - high.astype(F32)).astype(BF16)


def split_three(values):
    high = values.astype(BF16)
    rest = values - high.astype(F32)
    middle = rest.astype(BF16)
    return high, middle, (rest - middle.astype(F32)).astype(BF16)


def spread_heads(values, spread):
    high, low = split_two(values)
    return dot_nn(jnp.concatenate([high, low], axis=1), spread)


def gather_heads(values, spread):
    high, low = split_two(values)
    half = spread[:LANES]
    return dot_nt(high, half) + dot_nt(low, half)


def sigmoid(values):
    return 0.5 * jnp.tanh(0.5 * values) + 0.5


def softplus(values):
    return jnp.maximum(values, 0.0) + jnp.log1p(jnp.exp(-jnp.abs(values)))


def segment_of(rows, first, second):
    return (rows >= first).astype(jnp.int32) + (rows >= second).astype(jnp.int32)


def block_frame(block, first, second):
    row_col = block * BLK + lax.broadcasted_iota(jnp.int32, (BLK, 1), 0)
    row_row = block * BLK + lax.broadcasted_iota(jnp.int32, (1, BLK), 1)
    return row_col, row_row, segment_of(row_col, first, second), segment_of(row_row, first, second)


def decay_parts(block, dt_raw, head, seg_col, first, second):
    shifted = dt_raw + head[0:1]
    steps = softplus(shifted)
    log_decay = steps * head[1:2]
    above = lax.broadcasted_iota(jnp.int32, (BLK, BLK), 0)
    below = lax.broadcasted_iota(jnp.int32, (BLK, BLK), 1)
    lower = jnp.where(above >= below, 1.0, 0.0).astype(BF16)
    parts = dot_nn(lower, jnp.concatenate(split_three(log_decay), axis=1))
    cumulative = parts[:, :LANES] + parts[:, LANES : 2 * LANES] + parts[:, 2 * LANES :]
    cum2 = cumulative * LOG2E
    final2 = cum2[BLK - 1 : BLK]
    last_seg = segment_of(block * BLK + BLK - 1, first, second)
    prior_seg = jnp.where(block == 0, -1, segment_of(block * BLK - 1, first, second))
    entering = jnp.where(seg_col == prior_seg, jnp.exp2(cum2), 0.0)
    tail = jnp.where(seg_col == last_seg, jnp.exp2(final2 - cum2), 0.0)
    retained = jnp.where(last_seg == prior_seg, jnp.exp2(final2), 0.0)
    return shifted, steps, cum2, entering, tail, retained


def head_half(pair, head):
    lanes = lax.broadcasted_iota(jnp.int32, pair.shape, 1)
    keep = (lanes < LANES // 2) if head % 2 == 0 else (lanes >= LANES // 2)
    return jnp.where(keep, pair, jnp.zeros_like(pair))


SHARE = BLK // 4
AG_OWN, AG_ACROSS, AG_PASS, RS_PAIR, RS_ACROSS, SM_PAIR, SM_ACROSS = range(7)


class Ring:
    def __init__(self, sems):
        me = lax.axis_index("tensor")
        self.low, self.high = me % 2, me // 2
        self.me = me
        self.sibling = self.high * 2 + (1 - self.low)
        self.across = (1 - self.high) * 2 + self.low
        self.beyond = (1 - self.high) * 2 + (1 - self.low)
        self.sems = sems

    def greet(self):
        barrier = pltpu.get_barrier_semaphore()
        for other in (self.sibling, self.across, self.beyond):
            pl.semaphore_signal(barrier, inc=1, device_id={"tensor": other}, device_id_type=pl.DeviceIdType.MESH)
        pl.semaphore_wait(barrier, greet_dp(barrier) + 3)

    def slot(self, owner):
        return ((self.low + owner % 2) % 2) * 2 + (self.high + owner // 2) % 2

    def copy(self, kind, block, source, target, other):
        return pltpu.make_async_remote_copy(
            src_ref=source, dst_ref=target,
            send_sem=self.sems.at[kind, block, 0], recv_sem=self.sems.at[kind, block, 1],
            device_id={"tensor": other}, device_id_type=pl.DeviceIdType.MESH,
        )


def greet_dp(barrier):
    count, me = lax.axis_size("dp"), lax.axis_index("dp")

    @pl.loop(1, count)
    def _(step):
        pl.semaphore_signal(
            barrier, inc=1, device_id={"dp": (me + step) % count}, device_id_type=pl.DeviceIdType.MESH
        )

    return count - 1


class BinExchange:
    def __init__(self, to_bins, source, target, sems):
        self.to_bins, self.source, self.target, self.sems = to_bins, source, target, sems
        self.count, self.me = lax.axis_size("dp"), lax.axis_index("dp")
        self.span = source.shape[2] if to_bins else target.shape[2]

    def pieces(self, other):
        if self.to_bins:
            return self.source.at[other], self.target.at[:, pl.ds(self.me * self.span, self.span), :]
        return self.source.at[:, pl.ds(other * self.span, self.span), :], self.target.at[self.me]

    def remote(self, step, other):
        source, target = self.pieces(other)
        return pltpu.make_async_remote_copy(
            src_ref=source, dst_ref=target, send_sem=self.sems.at[step, 0], recv_sem=self.sems.at[step, 1],
            device_id={"dp": other}, device_id_type=pl.DeviceIdType.MESH,
        )

    def local(self):
        source, target = self.pieces(self.me)
        return pltpu.make_async_copy(source, target, self.sems.at[0, 0])

    def start(self):
        self.local().start()

        @pl.loop(1, self.count)
        def _(step):
            self.remote(step, (self.me + step) % self.count).start()

    def wait(self):
        self.local().wait()

        @pl.loop(1, self.count)
        def _(step):
            self.remote(step, (self.me + step) % self.count).wait()


class RowExchange:
    def __init__(self, to_rows, source, target, sems):
        self.to_rows, self.source, self.target, self.sems = to_rows, source, target, sems
        self.me = lax.axis_index("tensor")
        self.columns = source.shape[2] if to_rows else target.shape[2]

    def pieces(self, other):
        if self.to_rows:
            return (
                self.source.at[:, pl.ds(other * SHARE, SHARE), :],
                self.target.at[:, :, pl.ds(pl.multiple_of(self.me * self.columns, LANES), self.columns)],
            )
        return (
            self.source.at[:, :, pl.ds(pl.multiple_of(other * self.columns, LANES), self.columns)],
            self.target.at[:, pl.ds(self.me * SHARE, SHARE), :],
        )

    def remote(self, step):
        other = (self.me + step) % 4
        source, target = self.pieces(other)
        return pltpu.make_async_remote_copy(
            src_ref=source, dst_ref=target, send_sem=self.sems.at[step, 0], recv_sem=self.sems.at[step, 1],
            device_id={"tensor": other}, device_id_type=pl.DeviceIdType.MESH,
        )

    def local(self):
        source, target = self.pieces(self.me)
        return pltpu.make_async_copy(source, target, self.sems.at[0, 0])

    def start(self):
        self.local().start()
        for step in range(1, 4):
            self.remote(step).start()

    def wait(self):
        self.local().wait()
        for step in range(1, 4):
            self.remote(step).wait()


def row_place(rows, member):
    return rows.at[:, pl.ds(member * SHARE, SHARE), :]


def column_place(rows, member):
    columns = rows.shape[2] // 4
    return rows.at[:, :, pl.ds(pl.multiple_of(member * columns, LANES), columns)]


def gather_copy(ring, kind, block, own, rows, place):
    if kind == AG_PASS:
        passed = place(rows, ring.across).at[block]
        return ring.copy(kind, block, passed, passed, ring.sibling)
    other = ring.sibling if kind == AG_OWN else ring.across
    target = place(rows, ring.me).at[block]
    return ring.copy(kind, block, target if own is None else own.at[block], target, other)


def pair_copy(ring, block, parts, from_pair):
    return ring.copy(RS_PAIR, block, parts.at[block, pl.ds(2 * SHARE, 2 * SHARE), :], from_pair.at[block], ring.sibling)


def across_copy(ring, block, parts, from_across):
    return ring.copy(RS_ACROSS, block, parts.at[block, pl.ds(SHARE, SHARE), :], from_across.at[block], ring.across)


def store_parts(ring, block, part, parts):
    for owner in range(4):
        parts[block, pl.ds(ring.slot(owner) * SHARE, SHARE), :] = part[owner * SHARE : (owner + 1) * SHARE].astype(BF16)


def add_pair(block, parts, from_pair):
    parts[block, pl.ds(SHARE, SHARE), :] = (
        parts[block, pl.ds(SHARE, SHARE), :].astype(F32) + from_pair[block, pl.ds(SHARE, SHARE), :].astype(F32)
    ).astype(BF16)


def add_all(block, parts, from_pair, from_across):
    return (
        parts[block, pl.ds(0, SHARE), :].astype(F32)
        + from_pair[block, pl.ds(0, SHARE), :].astype(F32)
        + from_across[block].astype(F32)
    )


def own_column(line, first_lane):
    lanes = lax.broadcasted_iota(jnp.int32, (SHARE, line.shape[1]), 1)
    rows = lax.broadcasted_iota(jnp.int32, (SHARE, line.shape[1]), 0)
    return jnp.sum(jnp.where(lanes == rows + first_lane, line, 0.0), axis=1, keepdims=True)


LAG = 4
DEFER = 2
PASS_AHEAD = 2


def forward_kernel(
    off_ref, tok_ref, packs_ref, own_gains_ref, cot_ref, taps_ref, head_ref, wide_ref, spread_ref,
    rows_ref, z_ref, in_ref, pre_ref, dt_ref, y_ref, gg_ref, st_ref,
    before_ref, middle_ref, tot_ref, scale_ref, final_ref, gains_ref, cot_cols_ref, weights_ref,
    state, padded, rows, parts, from_pair, from_across, sq_own, sq_pair, sq_sums, sq_across,
    weights, arrived, cols, cot_arrived, all_gains, middle, kept,
    sems, copy_sems, line_sems, bin_sems, cot_sems, gain_sems,
):
    step = pl.program_id(0)
    inner = y_ref.shape[1]
    mixed = in_ref.shape[1]
    first, second = off_ref[0], off_ref[1]
    blocks = rows.shape[0]
    layer, block = step // blocks, step % blocks
    rings = (Ring(sems.at[0]), Ring(sems.at[1]))
    ring = rings[0]
    total_columns = weights.shape[2]
    out_part, in_part = pl.ds(0, inner), pl.ds(inner, total_columns - inner)
    line = LineGather(packs_ref.at[1], weights.at[1], line_sems.at[1])
    in_line = LineGather(packs_ref.at[0, :, in_part], weights.at[0, :, in_part], line_sems.at[0])
    out_line = LineGather(packs_ref.at[0, :, out_part], weights.at[0, :, out_part], line_sems.at[2])
    bins = BinExchange(True, tok_ref, arrived, bin_sems)
    cot_bins = BinExchange(True, cot_ref, cot_arrived, cot_sems)
    gain_tiles = TileGather(own_gains_ref, all_gains, gain_sems)
    four = line.line == 4

    def gather(at_layer, kind, at):
        own, place = ((cols, column_place), (None, row_place))[at_layer]
        return gather_copy(rings[at_layer], kind, at, own, rows, place)

    def sq_pair_copy(at_ring, slot):
        return at_ring.copy(SM_PAIR, slot % blocks, sq_own.at[slot], sq_pair.at[slot], at_ring.sibling)

    def sq_across_copy(at_ring, slot):
        return at_ring.copy(SM_ACROSS, slot % blocks, sq_sums.at[slot], sq_across.at[slot], at_ring.across)

    def own_copy():
        return pltpu.make_async_copy(cols, column_place(rows, ring.me), copy_sems.at[LAYERS])

    def keep_weights(at):
        return pltpu.make_async_copy(weights.at[at], weights_ref.at[at], copy_sems.at[at])

    def clear():
        state[...] = jnp.zeros_like(state)
        padded[pl.ds(0, 8), :] = jnp.zeros((8, mixed), F32)

    @pl.when(step == 0)
    def _():
        ring.greet()
        bins.start()
        in_line.start_pair()
        gain_tiles.start()
        clear()
        bins.wait()
        in_line.start_line()
        pick_all(off_ref, arrived, cols)
        own_copy().start()

        @pl.loop(0, blocks)
        def _(at):
            gather(0, AG_ACROSS, at).start()
            gather(0, AG_OWN, at).start()

        gain_tiles.wait()
        gains_ref[...] = all_gains[0]

        @pl.loop(1, all_gains.shape[0])
        def _(at):
            gains_ref[...] += all_gains[at]

        own_copy().wait()

        def pass_rows(begin, end):
            @pl.loop(begin, end)
            def _(at):
                gather(0, AG_ACROSS, at).wait_recv()
                gather(0, AG_PASS, at).start()

        if four:
            in_line.stage(1)
            pass_rows(0, blocks // 2)
            in_line.stage(2)
            pass_rows(blocks // 2, blocks)
            in_line.stage(3)
            out_line.start()
            line.start()
        else:
            pass_rows(0, blocks)

            @pl.loop(1, line.line)
            def _(stage):
                in_line.stage(stage)

        in_line.finish()
        if not four:
            out_line.start()
            line.start()

    @pl.when(step == blocks)
    def _():
        clear()

    for at_layer in range(LAYERS):

        @pl.when(layer == at_layer)
        def _(at_layer=at_layer):
            gather(at_layer, AG_OWN, block).wait_recv()
            gather(at_layer, AG_PASS, block).wait_recv()

    gains = gains_ref[...]
    raw = rows[block].astype(F32)
    mean = jnp.sum(raw * raw, axis=1, keepdims=True) / raw.shape[1]
    normed = raw * lax.rsqrt(mean + eps) * gains[0:1]
    here = jnp.where(layer == 0, normed, raw).astype(BF16)
    rows_ref[...] = here
    row_col, row_row, seg_col, seg_row = block_frame(block, first, second)
    seg_start = jnp.where(seg_col == 0, 0, jnp.where(seg_col == 1, first, second))
    within = row_col - seg_start
    product = dot_nn(here, weights[layer, :, inner:])
    gate = product[:, :inner]
    mixed_in = product[:, inner : inner + mixed]
    dt_raw = product[:, inner + mixed :]
    z_ref[...] = gate.astype(BF16)
    in_ref[...] = mixed_in.astype(BF16)
    dt_ref[...] = dt_raw
    padded[pl.ds(8, BLK), :] = mixed_in
    taps = taps_ref[layer]
    conv = taps[CONV : CONV + 1] + taps[CONV - 1 : CONV] * mixed_in
    for delay in range(1, CONV):
        shifted_in = padded[pl.ds(8 - delay, BLK), :]
        conv = conv + taps[CONV - 1 - delay : CONV - delay] * jnp.where(within >= delay, shifted_in, 0.0)
    padded[pl.ds(0, 8), :] = padded[pl.ds(BLK, 8), :]
    pre_ref[...] = conv
    mixed_low = (conv * sigmoid(conv)).astype(BF16)
    x_low = mixed_low[:, :inner]
    b_low = mixed_low[:, inner : inner + STATE]
    c_low = mixed_low[:, inner + STATE :]
    head = head_ref[layer]
    spread = spread_ref[...]
    shifted, steps, cum2, entering, tail, retained = decay_parts(block, dt_raw, head, seg_col, first, second)
    cum_row = jnp.transpose(cum2)
    x_in = x_low.astype(F32)
    x_steps = spread_heads(steps, spread) * x_in
    x_steps_low = x_steps.astype(BF16)
    allowed = (seg_col == seg_row) & (row_col >= row_row)
    scores = jnp.where(allowed, dot_nt(c_low, b_low), 0.0)
    old_state = state[...]
    st_ref[0] = old_state
    carried = spread_heads(entering, spread) * dot_nn(c_low, old_state.astype(BF16))
    wide = wide_ref[layer]
    pieces = []
    for pair in range(inner // LANES):
        columns = slice(pair * LANES, (pair + 1) * LANES)
        total = None
        for head_index in (2 * pair, 2 * pair + 1):
            gaps = cum2[:, head_index : head_index + 1] - cum_row[head_index : head_index + 1, :]
            coupling = (jnp.exp2(jnp.minimum(gaps, 0.0)) * scores).astype(BF16)
            term = dot_nn(coupling, head_half(x_steps_low[:, columns], head_index))
            total = term if total is None else total + term
        pieces.append(total)
    mixed_out = jnp.concatenate(pieces, axis=1) + carried + wide[0:1] * x_in
    tailed = (spread_heads(tail, spread) * x_steps).astype(BF16)
    keep = spread_heads(jnp.broadcast_to(retained, (8, LANES)), spread)[0:1]
    state[...] = old_state * keep + dot_tn(b_low, tailed)
    y_ref[...] = mixed_out
    gated = mixed_out * (gate * sigmoid(gate))
    gained = (gated * wide[1:2]).astype(BF16)
    gg_ref[...] = gained
    now = Ring(sems.at[layer])
    high, low = split_two(gated * gated)
    ones = jnp.ones((8, inner), BF16)
    sq_own[step] = dot_nt(ones, high) + dot_nt(ones, low)
    sq_pair_copy(now, step).start()

    def send_parts(at_ring, at, values, out_weights):
        store_parts(at_ring, at, dot_nt(values, out_weights), parts)
        pair_copy(at_ring, at, parts, from_pair).start()

    @pl.when(step < DEFER)
    def _():
        kept[step] = gained

    if four:
        for stage in (1, 2, 3):

            @pl.when(step == min(stage - 1, DEFER))
            def _(stage=stage):
                out_line.stage(stage)

    @pl.when(step == DEFER)
    def _():
        if not four:

            @pl.loop(1, line.line)
            def _(stage):
                out_line.stage(stage)

        out_line.finish()
        keep_weights(0).start()

        @pl.loop(0, DEFER)
        def _(at):
            gather(0, AG_PASS, at).wait_send()
            send_parts(ring, at, kept[at], weights[0, :, :inner])

    @pl.when(layer > 0)
    def _():
        pair_copy(ring, block, parts, from_pair).wait_send()
        across_copy(ring, block, parts, from_across).wait_send()

    @pl.when((step >= DEFER) & (layer == 0))
    def _():
        gather(0, AG_PASS, block).wait_send()

    @pl.when(step >= DEFER)
    def _():
        send_parts(now, block, gained, weights[layer, :, :inner])

    def second_stage(slot):
        at_layer, at = slot // blocks, slot % blocks
        at_ring = Ring(sems.at[at_layer])
        pair_copy(at_ring, at, parts, from_pair).wait_recv()
        sq_pair_copy(at_ring, slot).wait_recv()

        add_pair(at, parts, from_pair)
        sq_sums[slot] = sq_own[slot] + sq_pair[slot]
        across_copy(at_ring, at, parts, from_across).start()
        sq_across_copy(at_ring, slot).start()

    def last_stage(at_layer, at):
        at_ring, slot = rings[at_layer], at_layer * blocks + at
        across_copy(at_ring, at, parts, from_across).wait_recv()
        sq_across_copy(at_ring, slot).wait_recv()
        total = add_all(at, parts, from_pair, from_across)
        squares = own_column((sq_sums[slot] + sq_across[slot])[0:1], ring.me * SHARE)
        scale = lax.rsqrt(squares / INNER + eps)
        here = pl.ds(at * SHARE, SHARE)
        mine = pl.ds(ring.me * SHARE, SHARE)
        tot_ref[slot] = total.astype(BF16)
        scale_ref[slot] = scale
        if at_layer == 0:
            before = rows[at, mine, :]
            before_ref[at] = before
            hidden = before.astype(F32) + total * scale
            middle[at] = hidden
            middle_ref[at] = hidden.astype(BF16)
            mean = jnp.sum(hidden * hidden, axis=1, keepdims=True) / hidden.shape[1]
            later = (hidden * lax.rsqrt(mean + eps) * gains[1:2]).astype(BF16)
            rows[at, mine, :] = later
            gather(1, AG_ACROSS, at).start()
            gather(1, AG_OWN, at).start()
        else:
            final_ref[at] = (middle[at] + total * scale).astype(BF16)

    @pl.when((step >= LAG) & (step < blocks + LAG))
    def _():
        last_stage(0, step - LAG)

    @pl.when(step >= blocks + LAG)
    def _():
        last_stage(1, step - LAG - blocks)

    if four:
        for stage, when in ((1, 0), (2, 2), (3, 4)):

            @pl.when(step == when)
            def _(stage=stage):
                line.stage(stage)

    @pl.when(step == 2)
    def _():
        cot_bins.start()

    @pl.when((step >= blocks - PASS_AHEAD) & (step < 2 * blocks - PASS_AHEAD))
    def _():
        gather(1, AG_ACROSS, (step + PASS_AHEAD) % blocks).wait_recv()
        gather(1, AG_PASS, (step + PASS_AHEAD) % blocks).start()

    @pl.when(step == DEFER + 1)
    def _():
        @pl.loop(0, DEFER)
        def _(at):
            second_stage(at)

    @pl.when(step > DEFER)
    def _():
        second_stage(step - 1)

    @pl.when(step == blocks - 1)
    def _():
        if not four:

            @pl.loop(1, line.line)
            def _(stage):
                line.stage(stage)

        line.finish()
        keep_weights(1).start()

    @pl.when(step == 2 * blocks - 1)
    def _():
        second_stage(step)
        cot_bins.wait()
        pick_all(off_ref, cot_arrived, cot_cols_ref)

        @pl.loop(blocks - LAG, blocks)
        def _(at):
            last_stage(1, at)

        @pl.loop(0, blocks)
        def _(at):
            gather(0, AG_OWN, at).wait_send()
            gather(0, AG_ACROSS, at).wait_send()
            for kind in (AG_OWN, AG_ACROSS, AG_PASS):
                gather(1, kind, at).wait_send()
            pair_copy(rings[1], at, parts, from_pair).wait_send()
            across_copy(rings[1], at, parts, from_across).wait_send()
            for at_layer in range(LAYERS):
                sq_pair_copy(rings[at_layer], at_layer * blocks + at).wait_send()
                sq_across_copy(rings[at_layer], at_layer * blocks + at).wait_send()

        for at in range(LAYERS):
            keep_weights(at).wait()


def own_line(column):
    lanes = lax.broadcasted_iota(jnp.int32, (SHARE, LANES), 1)
    rows = lax.broadcasted_iota(jnp.int32, (SHARE, LANES), 0)
    return jnp.sum(jnp.where(lanes == rows, column, 0.0), axis=0, keepdims=True)


TILE_KINDS = (5, 6, 7)
AHEAD = 2
QUEUED = 4
BACK_LAG = 4


def backward_kernel(
    off_ref, cot_ref, tot_ref, scale_ref, before_ref, middle_ref, gains_ref, taps_ref, head_ref, wide_ref, spread_ref,
    weights_ref, final_ref,
    z_ref, in_ref, pre_ref, dt_ref, y_ref, st_ref, normed_ref, gg_ref,
    ginput_ref, small_ref, pack_ref, packs_ref, back_ref,
    dstate, padded, rows, parts, from_pair, from_across, tiles, held, running, weights, acc_out, acc_in,
    packs, pair_buf, arrivals, cols, slots,
    sems, copy_sems, line_sems, row_sems, bin_sems,
):
    step = pl.program_id(0)
    inner = y_ref.shape[1]
    mixed = in_ref.shape[1]
    first, second = off_ref[0], off_ref[1]
    blocks = rows.shape[0]
    phase, block = step // blocks, blocks - 1 - step % blocks
    layer = LAYERS - 1 - phase
    rings = (Ring(sems.at[0]), Ring(sems.at[1]))
    ring = rings[0]
    line = LineReduce(packs, pack_ref, pair_buf, arrivals, line_sems)
    four = line.line == 4
    final_rows = RowExchange(False, final_ref, cols.reshape(blocks, BLK, cols.shape[1]), row_sems)
    bins = BinExchange(False, slots, back_ref, bin_sems)
    mine = pl.ds(ring.me * SHARE, SHARE)

    def gather(at_phase, kind, at):
        own, place = ((cot_ref, column_place), (None, row_place))[at_phase]
        return gather_copy(rings[at_phase], kind, at, own, rows, place)

    def tile_copies(at_phase, at):
        at_ring = rings[at_phase]
        here = tiles.at[at_phase, ring.me, at]
        return [
            at_ring.copy(kind, at, here, here, other)
            for kind, other in zip(TILE_KINDS, (ring.sibling, ring.across, ring.beyond))
        ]

    def make_tile(at_phase, at, grad_low):
        slot = (LAYERS - 1 - at_phase) * blocks + at
        scale = scale_ref[slot]
        weighted = jnp.sum(grad_low.astype(F32) * tot_ref[slot].astype(F32), axis=1, keepdims=True)
        twice = -(scale * scale * scale) / INNER * weighted
        row = lax.broadcasted_iota(jnp.int32, (8, LANES), 0)
        tiles[at_phase, ring.me, at] = jnp.where(row == 0, own_line(twice), own_line(scale))
        for copy in tile_copies(at_phase, at):
            copy.start()

    def prepare(at):
        gather(0, AG_OWN, at).wait_recv()
        gather(0, AG_PASS, at).wait_recv()
        make_tile(0, at, rows[at, mine, :])

    def pass_rows(at_phase, at):
        gather(at_phase, AG_ACROSS, at).wait_recv()
        gather(at_phase, AG_PASS, at).start()

    def send_rows(at):
        gather(0, AG_ACROSS, at).start()
        gather(0, AG_OWN, at).start()

    def own_copy():
        return pltpu.make_async_copy(cot_ref, column_place(rows, ring.me), copy_sems.at[0])

    def load_weights(at_layer):
        return pltpu.make_async_copy(weights_ref.at[at_layer], weights, copy_sems.at[1])

    def load_held(at_phase):
        return pltpu.make_async_copy((middle_ref, before_ref)[at_phase], held, copy_sems.at[3 + at_phase])

    def store_packs():
        return pltpu.make_async_copy(packs, packs_ref, copy_sems.at[2])

    def clear():
        dstate[...] = jnp.zeros_like(dstate)
        padded[pl.ds(BLK, 8), :] = jnp.zeros((8, mixed), F32)
        acc_out[...] = jnp.zeros_like(acc_out)
        acc_in[...] = jnp.zeros_like(acc_in)

    @pl.when(step == 0)
    def _():
        own_copy().start()
        load_weights(LAYERS - 1).start()
        load_held(0).start()
        ring.greet()

        send_rows(blocks - 1)
        clear()
        small_ref[...] = jnp.zeros_like(small_ref)
        own_copy().wait()
        pass_rows(0, blocks - 1)
        for at in range(1, QUEUED):
            send_rows(blocks - 1 - at)
        prepare(blocks - 1)
        for at in range(1, AHEAD + 1):
            pass_rows(0, blocks - 1 - at)
        for at in range(1, AHEAD):
            prepare(blocks - 1 - at)
        load_weights(LAYERS - 1).wait()

    @pl.when(step == blocks)
    def _():
        load_weights(0).start()
        clear()
        load_weights(0).wait()

    @pl.when(phase > 0)
    def _():
        gather(1, AG_OWN, block).wait_recv()
        gather(1, AG_PASS, block).wait_recv()

    for at_phase in range(LAYERS):

        @pl.when(phase == at_phase)
        def _(at_phase=at_phase):
            for copy in tile_copies(at_phase, block):
                copy.wait_recv()

    here = rows[block]
    tile_rows = [tiles[phase, owner, block] for owner in range(4)]
    twice_here = jnp.concatenate([own_column(tile[0:1], 0) for tile in tile_rows], axis=0)
    scale_here = jnp.concatenate([own_column(tile[1:2], 0) for tile in tile_rows], axis=0)
    row_col, row_row, seg_col, seg_row = block_frame(block, first, second)
    seg_end = jnp.where(seg_col == 0, first, jnp.where(seg_col == 1, second, BIN))
    remaining = seg_end - row_col
    head = head_ref[layer]
    wide = wide_ref[layer]
    spread = spread_ref[...]
    skip, gain = wide[0:1], wide[1:2]
    gate = z_ref[...].astype(F32)
    mixed_out = y_ref[...]
    conv = pre_ref[...]
    gate_sig = sigmoid(gate)
    gate_silu = gate * gate_sig
    gated = mixed_out * gate_silu
    grad_scaled = dot_nn(here, weights[:, :inner]) * scale_here
    grad_gated = grad_scaled * gain + twice_here * gated
    grad_out = grad_gated * gate_silu
    grad_gate = grad_gated * mixed_out * (gate_sig * (1.0 + gate * (1.0 - gate_sig)))
    grad_out_low = grad_out.astype(BF16)

    conv_sig = sigmoid(conv)
    mixed_low = (conv * conv_sig).astype(BF16)
    x_low = mixed_low[:, :inner]
    b_low = mixed_low[:, inner : inner + STATE]
    c_low = mixed_low[:, inner + STATE :]
    x_in = x_low.astype(F32)
    shifted, steps, cum2, entering, tail, retained = decay_parts(block, dt_ref[...], head, seg_col, first, second)
    cum_row = jnp.transpose(cum2)
    steps_wide = spread_heads(steps, spread)
    x_steps_low = (steps_wide * x_in).astype(BF16)
    x_steps = x_steps_low.astype(F32)

    allowed = (seg_col == seg_row) & (row_col <= row_row)
    scores = jnp.where(allowed, dot_nt(b_low, c_low), 0.0)
    grad_scores = jnp.zeros((BLK, BLK), F32)
    pieces = []
    for pair in range(inner // LANES):
        columns = slice(pair * LANES, (pair + 1) * LANES)
        total = None
        for head_index in (2 * pair, 2 * pair + 1):
            gaps = cum_row[head_index : head_index + 1, :] - cum2[:, head_index : head_index + 1]
            decays = jnp.exp2(jnp.minimum(gaps, 0.0))
            coupling = (decays * scores).astype(BF16)
            term = dot_nn(coupling, head_half(grad_out_low[:, columns], head_index))
            total = term if total is None else total + term
            grad_scores = grad_scores + decays * dot_nt(
                head_half(x_steps_low[:, columns], head_index), grad_out_low[:, columns]
            )
        pieces.append(total)
    grad_scores_low = jnp.where(allowed, grad_scores, 0.0).astype(BF16)
    old_dstate = dstate[...]
    old_dstate_low = old_dstate.astype(BF16)
    old_state = st_ref[0]
    tail_wide = spread_heads(tail, spread)
    from_state = tail_wide * dot_nn(b_low, old_dstate_low)
    grad_unit = jnp.concatenate(pieces, axis=1) + from_state
    entered = (spread_heads(entering, spread) * grad_out).astype(BF16)
    tailed = (tail_wide * x_steps).astype(BF16)
    grad_c = dot_tn(grad_scores_low, b_low) + dot_nt(entered, old_state.astype(BF16))
    grad_b = dot_nn(grad_scores_low, c_low) + dot_nt(tailed, old_dstate_low)
    keep = spread_heads(jnp.broadcast_to(retained, (8, LANES)), spread)[0:1]
    dstate[...] = old_dstate * keep + dot_tn(c_low, entered)

    balance = gather_heads(grad_out_low.astype(F32) * (mixed_out - skip * x_in) - x_steps * grad_unit, spread)
    direct = gather_heads(x_in * grad_unit, spread)
    final_wide = jnp.sum(x_steps * from_state, axis=0, keepdims=True) + keep * jnp.sum(
        old_dstate * old_state, axis=0, keepdims=True
    )
    final = gather_heads(jnp.broadcast_to(final_wide, (8, inner)), spread)[0:1]
    above = lax.broadcasted_iota(jnp.int32, (BLK, BLK), 0)
    below = lax.broadcasted_iota(jnp.int32, (BLK, BLK), 1)
    upper = jnp.where(above <= below, 1.0, 0.0).astype(BF16)
    thirds = dot_nn(upper, jnp.concatenate(split_three(balance), axis=1))
    grad_log = thirds[:, :LANES] + thirds[:, LANES : 2 * LANES] + thirds[:, 2 * LANES :] + final
    grad_steps = direct + grad_log * head[1:2]
    grad_dt = grad_steps * sigmoid(shifted)
    small_ref[layer, 7:8, :LANES] += jnp.sum(grad_dt, axis=0, keepdims=True)
    small_ref[layer, 7:8, LANES : 2 * LANES] += jnp.sum(grad_log * steps, axis=0, keepdims=True) * head[1:2]
    small_ref[layer, 6:7, :inner] += jnp.sum(grad_out * x_in, axis=0, keepdims=True)
    small_ref[layer, 6:7, inner : 2 * inner] += jnp.sum(grad_scaled * gated, axis=0, keepdims=True)

    grad_x = steps_wide * grad_unit + skip * grad_out
    grad_conv = jnp.concatenate([grad_x, grad_b, grad_c], axis=1) * (
        conv_sig * (1.0 + conv * (1.0 - conv_sig))
    )
    padded[pl.ds(0, BLK), :] = grad_conv
    mixed_in = in_ref[...].astype(F32)
    taps = taps_ref[layer]
    grad_in = taps[CONV - 1 : CONV] * grad_conv
    small_ref[layer, CONV : CONV + 1, :mixed] += jnp.sum(grad_conv, axis=0, keepdims=True)
    small_ref[layer, CONV - 1 : CONV, :mixed] += jnp.sum(mixed_in * grad_conv, axis=0, keepdims=True)
    for delay in range(1, CONV):
        later = jnp.where(remaining > delay, padded[pl.ds(delay, BLK), :], 0.0)
        grad_in = grad_in + taps[CONV - 1 - delay : CONV - delay] * later
        small_ref[layer, CONV - 1 - delay : CONV - delay, :mixed] += jnp.sum(mixed_in * later, axis=0, keepdims=True)
    padded[pl.ds(BLK, 8), :] = padded[pl.ds(0, 8), :]
    gproj = jnp.concatenate([grad_gate.astype(BF16), grad_in.astype(BF16), grad_dt.astype(BF16)], axis=1)
    acc_out[...] += dot_tn(here, (gg_ref[...].astype(F32) * scale_here).astype(BF16))
    acc_in[...] += dot_tn(normed_ref[...], gproj)
    part = dot_nt(gproj, weights[:, inner:])

    @pl.when(phase > 0)
    def _():
        pair_copy(ring, block, parts, from_pair).wait_send()
        across_copy(ring, block, parts, from_across).wait_send()

    @pl.when(phase == 0)
    def _():
        gather(0, AG_PASS, block).wait_send()

    now = Ring(sems.at[phase])
    store_parts(now, block, part, parts)
    pair_copy(now, block, parts, from_pair).start()

    def second_stage(turn):
        at_phase, at = turn // blocks, blocks - 1 - turn % blocks
        at_ring = Ring(sems.at[at_phase])
        pair_copy(at_ring, at, parts, from_pair).wait_recv()

        add_pair(at, parts, from_pair)
        across_copy(at_ring, at, parts, from_across).start()

    def last_stage(at_phase, at):
        at_layer = LAYERS - 1 - at_phase
        across_copy(rings[at_phase], at, parts, from_across).wait_recv()
        grad_normed = add_all(at, parts, from_pair, from_across)
        hidden = held[at].astype(F32)
        width = hidden.shape[1]
        root = lax.rsqrt(jnp.sum(hidden * hidden, axis=1, keepdims=True) / width + eps)
        gained = grad_normed * gains_ref[at_layer : at_layer + 1, :]
        small_ref[at_layer, 5:6, :] += jnp.sum(grad_normed * hidden * root, axis=0, keepdims=True)
        along = jnp.sum(gained * hidden, axis=1, keepdims=True) * (root * root * root) / width
        change = gained * root - hidden * along
        if at_phase == 0:
            grad = rows[at, mine, :].astype(F32) + change
            running[at] = grad
            grad_low = grad.astype(BF16)
            rows[at, mine, :] = grad_low
            gather(1, AG_ACROSS, at).start()
            gather(1, AG_OWN, at).start()
            make_tile(1, at, grad_low)
        else:
            ginput_ref[at] = (running[at] + change).astype(BF16)

    @pl.when(step == BACK_LAG)
    def _():
        load_held(0).wait()

    @pl.when(step == blocks + BACK_LAG)
    def _():
        load_held(1).start()
        load_held(1).wait()

    @pl.when((step >= BACK_LAG) & (step < blocks + BACK_LAG))
    def _():
        last_stage(0, blocks - 1 - (step - BACK_LAG))

    @pl.when(step >= blocks + BACK_LAG)
    def _():
        last_stage(1, blocks - 1 - (step - BACK_LAG - blocks))

    @pl.when(step + QUEUED < blocks)
    def _():
        send_rows(blocks - 1 - (step + QUEUED))

    @pl.when(step + AHEAD + 1 < blocks)
    def _():
        pass_rows(0, blocks - 1 - (step + AHEAD + 1))

    @pl.when(step + AHEAD < blocks)
    def _():
        prepare(blocks - 1 - (step + AHEAD))

    @pl.when((step >= blocks - PASS_AHEAD) & (step < 2 * blocks - PASS_AHEAD))
    def _():
        pass_rows(1, blocks - 1 - (step + PASS_AHEAD) % blocks)

    @pl.when(step >= 1)
    def _():
        second_stage(step - 1)

    @pl.when(step == 1)
    def _():
        final_rows.start()

    @pl.when(step == 4)
    def _():
        final_rows.wait()
        place_all(off_ref, cols, slots)
        bins.start()

    @pl.when(step == blocks - 1)
    def _():
        packs[:, :inner] = acc_out[...].astype(BF16)
        packs[:, inner:] = acc_in[...].astype(BF16)
        line.send_pairs()

    if four:
        for stage in (0, 1, 2):

            @pl.when(step == blocks + 1 + 2 * stage)
            def _(stage=stage):
                line.stage(stage)

    @pl.when(step == 2 * blocks - 1)
    def _():
        second_stage(step)
        if not four:

            @pl.loop(0, line.line - 1)
            def _(stage):
                line.stage(stage)

        line.finish()
        packs[:, :inner] = acc_out[...].astype(BF16)
        packs[:, inner:] = acc_in[...].astype(BF16)
        store_packs().start()

        @pl.loop(0, BACK_LAG)
        def _(turn):
            last_stage(1, BACK_LAG - 1 - turn)

        @pl.loop(0, blocks)
        def _(at):
            gather(0, AG_OWN, at).wait_send()
            gather(0, AG_ACROSS, at).wait_send()
            for kind in (AG_OWN, AG_ACROSS, AG_PASS):
                gather(1, kind, at).wait_send()
            pair_copy(rings[1], at, parts, from_pair).wait_send()
            across_copy(rings[1], at, parts, from_across).wait_send()
            for at_phase in range(LAYERS):
                for copy in tile_copies(at_phase, at):
                    copy.wait_send()

        store_packs().wait()
        bins.wait()


def whole(shape):
    return pl.BlockSpec(shape, lambda *at: (0,) * len(shape))


def exchange_scratch(blocks, width):
    return [
        pltpu.VMEM((blocks, BLK, width), BF16),
        pltpu.VMEM((blocks, BLK, width), BF16),
        pltpu.VMEM((blocks, 2 * SHARE, width), BF16),
        pltpu.VMEM((blocks, SHARE, width), BF16),
    ]


def layers_forward(offsets, given, packs, own_gains, given_cot, taps, head, wide, spread):
    blocks, width = BIN // BLK, own_gains.shape[1]
    inner, mixed = wide.shape[2], taps.shape[2]
    dp_count, members, span, columns = given_cot.shape
    total = packs.shape[2]
    steps = LAYERS * blocks
    vmem, hbm = pl.BlockSpec(memory_space=pltpu.VMEM), pl.BlockSpec(memory_space=pltpu.HBM)

    def by_block(size):
        return pl.BlockSpec((BLK, size), lambda s: (s, 0))

    return pl.pallas_call(
        forward_kernel,
        grid=(steps,),
        in_specs=[pl.BlockSpec(memory_space=pltpu.SMEM), hbm, vmem, vmem, hbm] + [vmem] * 4,
        out_specs=[
            by_block(width), by_block(inner), by_block(mixed), by_block(mixed),
            by_block(LANES), by_block(inner), by_block(inner),
            pl.BlockSpec((1, STATE, inner), lambda s: (s, 0, 0)),
            vmem, vmem, vmem, vmem, vmem, vmem, vmem, hbm,
        ],
        out_shape=[
            jax.ShapeDtypeStruct((steps * BLK, width), BF16),
            jax.ShapeDtypeStruct((steps * BLK, inner), BF16),
            jax.ShapeDtypeStruct((steps * BLK, mixed), BF16),
            jax.ShapeDtypeStruct((steps * BLK, mixed), F32),
            jax.ShapeDtypeStruct((steps * BLK, LANES), F32),
            jax.ShapeDtypeStruct((steps * BLK, inner), F32),
            jax.ShapeDtypeStruct((steps * BLK, inner), BF16),
            jax.ShapeDtypeStruct((steps, STATE, inner), F32),
            jax.ShapeDtypeStruct((blocks, SHARE, width), BF16),
            jax.ShapeDtypeStruct((blocks, SHARE, width), BF16),
            jax.ShapeDtypeStruct((steps, SHARE, width), BF16),
            jax.ShapeDtypeStruct((steps, SHARE, 1), F32),
            jax.ShapeDtypeStruct((blocks, SHARE, width), BF16),
            jax.ShapeDtypeStruct(own_gains.shape, F32),
            jax.ShapeDtypeStruct((blocks, BLK, columns), BF16),
            jax.ShapeDtypeStruct((LAYERS, width, total), BF16),
        ],
        scratch_shapes=[pltpu.VMEM((STATE, inner), F32), pltpu.VMEM((BLK + 8, mixed), F32)]
        + exchange_scratch(blocks, width)
        + [pltpu.VMEM((steps, 8, BLK), F32)] * 4
        + [
            pltpu.VMEM((LAYERS, width, total), BF16),
            pltpu.VMEM((members, dp_count * span, columns), BF16),
            pltpu.VMEM((blocks, BLK, columns), BF16),
            pltpu.VMEM((members, dp_count * span, columns), BF16),
            pltpu.VMEM((dp_count,) + own_gains.shape, F32),
            pltpu.VMEM((blocks, SHARE, width), F32),
            pltpu.VMEM((DEFER, BLK, inner), BF16),
            pltpu.SemaphoreType.DMA((LAYERS, 7, blocks, 2)),
            pltpu.SemaphoreType.DMA((LAYERS + 1,)),
            pltpu.SemaphoreType.DMA((LAYERS + 1, 6, dp_count // 2)),
            pltpu.SemaphoreType.DMA((dp_count, 2)),
            pltpu.SemaphoreType.DMA((dp_count, 2)),
            pltpu.SemaphoreType.DMA((dp_count, 2)),
        ],
        compiler_params=pltpu.CompilerParams(
            vmem_limit_bytes=48 * 1024 * 1024, collective_id=1, has_side_effects=True
        ),
        cost_estimate=pl.CostEstimate(flops=6 * 10**10, bytes_accessed=6 * 10**7, transcendentals=10**7),
        name="layers_forward",
    )(offsets, given, packs, own_gains, given_cot, taps, head, wide, spread)


def layers_backward(offsets, cot, totals, scales, before, middle, gains, taps, head, wide, spread, weights, final, saved, span):
    gate, mixed_in, conv, dt_raw, mixed_out, states, normed, gained = saved
    blocks, _, columns = cot.shape
    width = gains.shape[1]
    inner, mixed = wide.shape[2], taps.shape[2]
    total = weights.shape[2]
    steps = LAYERS * blocks
    count = lax.axis_size("dp")
    vmem, hbm = pl.BlockSpec(memory_space=pltpu.VMEM), pl.BlockSpec(memory_space=pltpu.HBM)

    def by_block(size):
        return pl.BlockSpec((BLK, size), lambda s: (steps - 1 - s, 0))

    return pl.pallas_call(
        backward_kernel,
        grid=(steps,),
        in_specs=[pl.BlockSpec(memory_space=pltpu.SMEM)]
        + [vmem] * 3
        + [hbm, hbm]
        + [vmem] * 5
        + [hbm, hbm]
        + [
            by_block(inner), by_block(mixed), by_block(mixed), by_block(LANES), by_block(inner),
            pl.BlockSpec((1, STATE, inner), lambda s: (steps - 1 - s, 0, 0)),
            by_block(width), by_block(inner),
        ],
        out_specs=[vmem, vmem, vmem, hbm, hbm],
        out_shape=[
            jax.ShapeDtypeStruct((blocks, SHARE, width), BF16),
            jax.ShapeDtypeStruct((LAYERS, 8, width), F32),
            jax.ShapeDtypeStruct((width // count, total), F32),
            jax.ShapeDtypeStruct((width, total), BF16),
            jax.ShapeDtypeStruct((count, 3, span, columns), BF16),
        ],
        scratch_shapes=[pltpu.VMEM((STATE, inner), F32), pltpu.VMEM((BLK + 8, mixed), F32)]
        + exchange_scratch(blocks, width)
        + [
            pltpu.VMEM((LAYERS, 4, blocks, 8, LANES), F32),
            pltpu.VMEM((blocks, SHARE, width), BF16),
            pltpu.VMEM((blocks, SHARE, width), F32),
            pltpu.VMEM((width, total), BF16),
            pltpu.VMEM((width, inner), F32),
            pltpu.VMEM((width, total - inner), F32),
            pltpu.VMEM((width, total), BF16),
        ]
        + [
            pltpu.VMEM((count // 2, width // count, total), BF16),
            pltpu.VMEM((count // 2 + 1, width // count, total), BF16),
            pltpu.VMEM((BIN, columns), BF16),
            pltpu.VMEM((3, count * span, columns), BF16),
            pltpu.SemaphoreType.DMA((LAYERS, 8, blocks, 2)),
            pltpu.SemaphoreType.DMA((3 + LAYERS,)),
            pltpu.SemaphoreType.DMA((5, count // 2)),
            pltpu.SemaphoreType.DMA((4, 2)),
            pltpu.SemaphoreType.DMA((count, 2)),
        ],
        compiler_params=pltpu.CompilerParams(
            vmem_limit_bytes=61 * 1024 * 1024, collective_id=2, has_side_effects=True
        ),
        cost_estimate=pl.CostEstimate(flops=6 * 10**10, bytes_accessed=6 * 10**7, transcendentals=10**7),
        name="layers_backward",
    )(
        offsets, cot, totals, scales, before, middle, gains, taps, head, wide, spread, weights, final,
        gate, mixed_in, conv, dt_raw, mixed_out, states, normed, gained,
    )


def spread_matrix(inner, heads):
    lane_head = lax.broadcasted_iota(jnp.int32, (2 * LANES, inner), 1) // (inner // heads)
    row_head = lax.broadcasted_iota(jnp.int32, (2 * LANES, inner), 0) % LANES
    return jnp.where(lane_head == row_head, 1.0, 0.0).astype(BF16)


SEQ_MIN = 512


def choose_rows(wanted, valid, begin, end):
    slots = begin + lax.broadcasted_iota(jnp.int32, (wanted.shape[0], end - begin), 1)
    return jnp.where((slots == wanted) & valid, 1.0, 0.0).astype(BF16)


def pick_all(off_ref, arrived, cols):
    first, second = off_ref[0], off_ref[1]
    length = arrived.shape[1]
    for block in range(cols.shape[0]):
        low, high = block * BLK, (block + 1) * BLK
        row = low + lax.broadcasted_iota(jnp.int32, (BLK, 1), 0)
        total = None
        for member, begin, least, most in ((1, first, SEQ_MIN, length), (2, second, BIN - length, BIN - SEQ_MIN)):
            reach = BIN - SEQ_MIN if member == 1 else BIN
            start, end = max(low - most, 0), min(high - least, length)
            if end <= 0 or start >= length or low >= reach:
                continue
            valid = (row >= first) & (row < second) if member == 1 else row >= second
            term = dot_nn(choose_rows(row - begin, valid, start, end), arrived[member, start:end, :])
            total = term if total is None else total + term
        if high <= length:
            own = arrived[0, low:high, :].astype(F32)
            own = jnp.where(row < first, own, 0.0)
            total = own if total is None else total + own
        cols[block] = total.astype(BF16)


def place_all(off_ref, cols, slots):
    first, second = off_ref[0], off_ref[1]
    length = slots.shape[1]
    for chunk in range(length // BLK):
        low, high = chunk * BLK, (chunk + 1) * BLK
        position = low + lax.broadcasted_iota(jnp.int32, (BLK, 1), 0)
        slots[0, low:high, :] = jnp.where(position < first, cols[low:high, :].astype(F32), 0.0).astype(BF16)
        for member, begin, stop, least, most, reach in (
            (1, first, second, SEQ_MIN, length, BIN - SEQ_MIN),
            (2, second, BIN, BIN - length, BIN - SEQ_MIN, BIN),
        ):
            wanted = begin + position
            start, end = least + low, min(most + high, reach)
            choose = choose_rows(wanted, wanted < stop, start, end)
            slots[member, low:high, :] = dot_nn(choose, cols[start:end, :]).astype(BF16)


class LineGather:
    def __init__(self, own, target, sems):
        self.own, self.target, self.sems = own, target, sems
        me = lax.axis_index("dp")
        self.me, self.low, self.high = me, me % 2, me // 2
        self.line = lax.axis_size("dp") // 2
        self.span = own.shape[0]

    def copy(self, kind, place, other, own):
        here = self.target.at[pl.ds((place * 2 + self.low) * self.span, self.span), :]
        arrival = 2 if kind == 2 else 3
        return pltpu.make_async_remote_copy(
            src_ref=self.own if own else here, dst_ref=here,
            send_sem=self.sems.at[kind, place], recv_sem=self.sems.at[arrival + 1, place],
            device_id={"dp": other}, device_id_type=pl.DeviceIdType.MESH,
        )

    def right(self, place, own=False):
        return self.copy(0, place, (self.high + 1) * 2 + self.low, own)

    def left(self, place, own=False):
        return self.copy(1, place, (self.high - 1) * 2 + self.low, own)

    def pair(self, place, own=False):
        return self.copy(2, place, self.high * 2 + 1 - self.low, own)

    def local(self):
        here = self.target.at[pl.ds(self.me * self.span, self.span), :]
        return pltpu.make_async_copy(self.own, here, self.sems.at[5, 0])

    def start_pair(self):
        self.local().start()
        self.pair(self.high, True).start()

    def start_line(self):
        @pl.when(self.high < self.line - 1)
        def _():
            self.right(self.high, True).start()

        @pl.when(self.high > 0)
        def _():
            self.left(self.high, True).start()

    def start(self):
        self.start_line()
        self.start_pair()

    def stage(self, step):
        @pl.when(self.high - step >= 0)
        def _():
            self.right(self.high - step).wait_recv()

            @pl.when(self.high < self.line - 1)
            def _():
                self.right(self.high - step).start()

            self.pair(self.high - step).start()

        @pl.when(self.high + step < self.line)
        def _():
            self.left(self.high + step).wait_recv()

            @pl.when(self.high > 0)
            def _():
                self.left(self.high + step).start()

            self.pair(self.high + step).start()

    def finish(self):
        self.local().wait()

        @pl.loop(0, self.line)
        def _(place):
            self.pair(place).wait_recv()
            self.pair(place).wait_send()

            @pl.when((self.high < self.line - 1) & (place <= self.high))
            def _():
                self.right(place).wait_send()

            @pl.when((self.high > 0) & (place >= self.high))
            def _():
                self.left(place).wait_send()


class TileGather:
    def __init__(self, own, target, sems):
        self.own, self.target, self.sems = own, target, sems
        self.count, self.me = lax.axis_size("dp"), lax.axis_index("dp")

    def remote(self, step):
        return pltpu.make_async_remote_copy(
            src_ref=self.own, dst_ref=self.target.at[self.me],
            send_sem=self.sems.at[step, 0], recv_sem=self.sems.at[step, 1],
            device_id={"dp": (self.me + step) % self.count}, device_id_type=pl.DeviceIdType.MESH,
        )

    def start(self):
        self.target[self.me] = self.own[...]

        @pl.loop(1, self.count)
        def _(step):
            self.remote(step).start()

    def wait(self):
        @pl.loop(1, self.count)
        def _(step):
            self.remote(step).wait()


class LineReduce:
    def __init__(self, given, out, pair_buf, arrivals, sems):
        self.given, self.out, self.pair_buf = given, out, pair_buf
        self.arrivals, self.sems = arrivals, sems
        me = lax.axis_index("dp")
        self.low, self.high = me % 2, me // 2
        self.line = lax.axis_size("dp") // 2
        self.span = out.shape[0]

    def chunk(self, place, low):
        return pl.ds((place * 2 + low) * self.span, self.span)

    def pair(self, place):
        return pltpu.make_async_remote_copy(
            src_ref=self.given.at[self.chunk(place, 1 - self.low), :], dst_ref=self.pair_buf.at[place],
            send_sem=self.sems.at[0, place], recv_sem=self.sems.at[1, place],
            device_id={"dp": self.high * 2 + 1 - self.low}, device_id_type=pl.DeviceIdType.MESH,
        )

    def onward(self, place, right):
        slot = place + 1 if right else place
        other = (self.high + 1 if right else self.high - 1) * 2 + self.low
        return pltpu.make_async_remote_copy(
            src_ref=self.pair_buf.at[place], dst_ref=self.arrivals.at[slot],
            send_sem=self.sems.at[2, place], recv_sem=self.sems.at[3 if right else 4, place],
            device_id={"dp": other}, device_id_type=pl.DeviceIdType.MESH,
        )

    def by_distance(self, step, act):
        distance = self.line - 1 - step

        @pl.when(self.high + distance < self.line)
        def _():
            act(self.high + distance, True)

        @pl.when(self.high - distance >= 0)
        def _():
            act(self.high - distance, False)

    def send_pairs(self):
        @pl.loop(0, self.line - 1)
        def _(step):
            self.by_distance(step, lambda place, right: self.pair(place).start())

        self.pair(self.high).start()

    def fold(self, place):
        return self.given[self.chunk(place, self.low), :].astype(F32) + self.pair_buf[place].astype(F32)

    def pass_on(self, place, right):
        self.pair(place).wait_recv()
        upstream = (self.high > 0) if right else (self.high < self.line - 1)
        slot = place + 1 if right else place

        @pl.when(upstream)
        def _():
            self.onward(place, right).wait_recv()
            self.pair_buf[place] = (self.fold(place) + self.arrivals[slot].astype(F32)).astype(BF16)

        @pl.when(jnp.logical_not(upstream))
        def _():
            self.pair_buf[place] = self.fold(place).astype(BF16)

        self.onward(place, right).start()

    def stage(self, step):
        self.by_distance(step, self.pass_on)

    def finish(self):
        here = self.high
        self.pair(here).wait_recv()
        self.out[...] = self.fold(here)

        @pl.when(here > 0)
        def _():
            self.onward(here, True).wait_recv()
            self.out[...] += self.arrivals[here + 1].astype(F32)

        @pl.when(here < self.line - 1)
        def _():
            self.onward(here, False).wait_recv()
            self.out[...] += self.arrivals[here].astype(F32)

        @pl.loop(0, self.line)
        def _(place):
            self.pair(place).wait_send()

            @pl.when(place != here)
            def _():
                self.onward(place, True).wait_send()


def line_scratch(count, span, columns):
    line = count // 2
    return [
        pltpu.VMEM((line, span, columns), BF16),
        pltpu.VMEM((line + 1, span, columns), BF16),
        pltpu.SemaphoreType.DMA((5, line)),
    ]


class MemberGather:
    def __init__(self, target, sems):
        self.target, self.sems = target, sems
        self.me = lax.axis_index("tensor")

    def remote(self, step):
        return pltpu.make_async_remote_copy(
            src_ref=self.target.at[self.me], dst_ref=self.target.at[self.me],
            send_sem=self.sems.at[step, 0], recv_sem=self.sems.at[step, 1],
            device_id={"tensor": (self.me + step) % 4}, device_id_type=pl.DeviceIdType.MESH,
        )

    def start(self):
        for step in range(1, 4):
            self.remote(step).start()

    def wait(self):
        for step in range(1, 4):
            self.remote(step).wait()


def end_kernel(
    off_ref, grad_ref, packs_ref, small_ref, later_ref,
    back_ref, pack_ref, sum_ref, shared_ref, maps_ref,
    cols, slots, pair_buf, arrivals, line_sems, smalls, shared, maps,
    row_sems, bin_sems, small_sems, shared_sems, maps_sems,
):
    ring = Ring(None)
    ring.greet()
    inner = (pack_ref.shape[1] - 2 * STATE - LANES) // 3
    first_map = 3 * inner
    rows = RowExchange(False, grad_ref, cols.reshape(BIN // BLK, BLK, cols.shape[1]), row_sems)
    bins = BinExchange(False, slots, back_ref, bin_sems)
    line = LineReduce(packs_ref, pack_ref, pair_buf, arrivals, line_sems)
    dp_smalls = TileGather(small_ref, smalls, small_sems)
    shared_smalls = MemberGather(shared, shared_sems)
    shared_maps = MemberGather(maps, maps_sems)
    rows.start()
    line.send_pairs()
    dp_smalls.start()
    rows.wait()
    place_all(off_ref, cols, slots)
    bins.start()

    @pl.loop(0, line.line - 1)
    def _(step):
        line.stage(step)

    dp_smalls.wait()
    sum_ref[...] = smalls[0]

    @pl.loop(1, smalls.shape[0])
    def _(at):
        sum_ref[...] += smalls[at]

    shared[ring.me] = sum_ref[...]
    shared_smalls.start()
    line.finish()
    maps[ring.me, 0] = pack_ref[:, first_map : first_map + 2 * STATE].astype(BF16)
    maps[ring.me, 1] = later_ref[:, first_map : first_map + 2 * STATE].astype(BF16)
    shared_maps.start()
    shared_smalls.wait()
    shared_ref[...] = (shared[0] + shared[1]) + (shared[2] + shared[3])
    shared_maps.wait()
    for layer in range(LAYERS):
        maps_ref[layer] = (maps[0, layer].astype(F32) + maps[1, layer].astype(F32)) + (
            maps[2, layer].astype(F32) + maps[3, layer].astype(F32)
        )
    bins.wait()


def end_exchange(offsets, grad_rows, packs, small, later_pack, span):
    count = lax.axis_size("dp")
    width, total = packs.shape
    columns = width // 4
    vmem = pl.BlockSpec(memory_space=pltpu.VMEM)
    pack_rows = width // count
    return pl.pallas_call(
        end_kernel,
        in_specs=[pl.BlockSpec(memory_space=pltpu.SMEM)] + [vmem] * 4,
        out_specs=[pl.BlockSpec(memory_space=pltpu.HBM), vmem, vmem, vmem, vmem],
        out_shape=[
            jax.ShapeDtypeStruct((count, 3, span, columns), BF16),
            jax.ShapeDtypeStruct((pack_rows, total), F32),
            jax.ShapeDtypeStruct(small.shape, F32),
            jax.ShapeDtypeStruct(small.shape, F32),
            jax.ShapeDtypeStruct((LAYERS, pack_rows, 2 * STATE), F32),
        ],
        scratch_shapes=[
            pltpu.VMEM((BIN, columns), BF16),
            pltpu.VMEM((3, count * span, columns), BF16),
        ]
        + line_scratch(count, pack_rows, total)
        + [
            pltpu.VMEM((count,) + small.shape, F32),
            pltpu.VMEM((4,) + small.shape, F32),
            pltpu.VMEM((4, LAYERS, pack_rows, 2 * STATE), BF16),
            pltpu.SemaphoreType.DMA((4, 2)),
            pltpu.SemaphoreType.DMA((count, 2)),
            pltpu.SemaphoreType.DMA((count, 2)),
            pltpu.SemaphoreType.DMA((4, 2)),
            pltpu.SemaphoreType.DMA((4, 2)),
        ],
        compiler_params=pltpu.CompilerParams(
            vmem_limit_bytes=56 * 1024 * 1024, collective_id=3, has_side_effects=True
        ),
        cost_estimate=pl.CostEstimate(flops=6 * 10**10, bytes_accessed=6 * 10**7, transcendentals=0),
        name="end_exchange",
    )(offsets, grad_rows, packs, small, later_pack)


def pad_to(values, rows, columns):
    return jnp.pad(values, ((0, rows - values.shape[0]), (0, columns - values.shape[1])))


def on_device(
    tokens, cotangent, lengths, packing, pre_gain, w_z, w_x, w_bc, w_dt, conv_x, conv_bc, head_params, norm_gain, w_out,
):
    dp_count = lax.axis_size("dp")
    bin_index = lax.axis_index("dp")
    seq_total, pos_here, cols_here = tokens.shape
    inner_part = conv_x.shape[2]
    heads_here = head_params.shape[2]
    dp_rows = w_z.shape[1]
    mixed = inner_part + 2 * STATE
    triples = lengths[packing].reshape(dp_count, 3)
    offsets = jnp.cumsum(triples, axis=1) - triples
    my_offsets = offsets[bin_index]
    bounds = my_offsets[1:3]
    groups = packing.reshape(dp_count, 3)

    spread = spread_matrix(inner_part, heads_here)
    packs = []
    for layer in range(LAYERS):
        own = jnp.concatenate(
            [w_out[layer].T, w_z[layer], w_x[layer], w_bc[layer], pad_to(w_dt[layer], dp_rows, LANES)], axis=1
        )
        taps = jnp.concatenate([conv_x[layer], conv_bc[layer]], axis=1).astype(F32)
        head = jnp.stack([head_params[layer, 0], -jnp.exp(head_params[layer, 1])])
        wide = jnp.stack(
            [jnp.repeat(head_params[layer, 2], inner_part // heads_here), norm_gain[layer].astype(F32)]
        )
        packs.append((own, pad_to(taps, 8, mixed), pad_to(head, 8, LANES), pad_to(wide, 8, inner_part)))

    own_gains = lax.dynamic_update_slice(
        jnp.zeros((8, dp_count * dp_rows), F32), pre_gain.astype(F32), (0, bin_index * dp_rows)
    )
    taps_all, head_all, wide_all = (jnp.stack([pack[at] for pack in packs]) for at in (1, 2, 3))
    (
        rows_all, gate, mixed_in, conv, dt_raw, mixed_out, gained_all, states, first_before, middle, totals, scales,
        final_rows, gains, cot_columns, all_weights,
    ) = layers_forward(
        bounds, tokens[groups], jnp.stack([pack[0] for pack in packs]), own_gains, cotangent[groups],
        taps_all, head_all, wide_all, spread,
    )
    grad_rows, small, later_pack, first_packs, activations_back = layers_backward(
        bounds, cot_columns, totals, scales, first_before, middle, gains, taps_all, head_all, wide_all, spread,
        all_weights, final_rows, (gate, mixed_in, conv, dt_raw, mixed_out, states, rows_all, gained_all), pos_here,
    )
    returned, first_pack, sums, shared, maps = end_exchange(bounds, grad_rows, first_packs, small, later_pack, pos_here)
    grad_convx = sums[:, : CONV + 1, :inner_part]
    grad_convbc = shared[:, : CONV + 1, inner_part:mixed]
    shard_pre = lax.dynamic_slice_in_dim(shared[:, 5], bin_index * dp_rows, dp_rows, 1)
    skips = jnp.sum(sums[:, 6, :inner_part].reshape(LAYERS, heads_here, -1), axis=2)
    grad_head = jnp.stack([sums[:, 7, :heads_here], sums[:, 7, LANES : LANES + heads_here], skips], axis=1)
    grad_norm = sums[:, 6, inner_part : 2 * inner_part]
    own_weights = jnp.stack([first_pack, later_pack])
    grad_bc = maps
    grad_out = jnp.swapaxes(own_weights[:, :, :inner_part], 1, 2)
    grad_z = own_weights[:, :, inner_part : 2 * inner_part]
    grad_x = own_weights[:, :, 2 * inner_part : 3 * inner_part]
    grad_dt = own_weights[:, :, 3 * inner_part + 2 * STATE : 3 * inner_part + 2 * STATE + heads_here]

    rank_of = jnp.zeros_like(packing).at[packing].set(jnp.arange(seq_total, dtype=jnp.int32))

    def in_order(returned):
        return returned.reshape(seq_total, pos_here, cols_here)[rank_of]

    activations = in_order(activations_back)
    input_grad = in_order(returned)
    return (
        activations, input_grad, shard_pre, grad_z, grad_x, grad_bc, grad_dt,
        grad_convx, grad_convbc, grad_head, grad_norm, grad_out,
    )


def solution(mesh):
    placed = (
        P(None, "dp", "tensor"), P(None, "dp", "tensor"), P(), P(), P(None, "dp"),
        P(None, "dp", "tensor"), P(None, "dp", "tensor"), P(None, "dp", None), P(None, "dp", "tensor"),
        P(None, None, "tensor"), P(), P(None, None, "tensor"), P(None, "tensor"), P(None, "tensor", "dp"),
    )
    results = (
        P(None, "dp", "tensor"), P(None, "dp", "tensor"), P(None, "dp"),
        P(None, "dp", "tensor"), P(None, "dp", "tensor"), P(None, "dp", None), P(None, "dp", "tensor"),
        P(None, None, "tensor"), P(), P(None, None, "tensor"), P(None, "tensor"), P(None, "tensor", "dp"),
    )
    return jax.shard_map(on_device, mesh=mesh, in_specs=placed, out_specs=results, check_vma=False)
```

time: 558 us -> 505 us (0.905); the launches traced: 548 us -> 504 us
  other arithmetic: 24.1 us -> 5.51 us
  matrix products: 12 us -> 0 us
  Pallas kernels: 472 us -> 464 us
    dot_general x2 -> x0, matrix products: 12 us -> none  [dot_tn(): lax.dot_general(left, right, (((0,), (0,)), ((), ())), preferred_element_...]
    convert_element_type x4 -> x0, other arithmetic: 7.4 us -> none  [the longest x1 3.78 us: on_device(): grad_hidden.astype(BF16).reshape(own.shape)]
    pallas_call x5 -> x2, Pallas kernels: 378 us -> 370 us  [the longest x1 207 us: layers_forward(): pl.pallas_call(forward_kernel, grid=(steps,), in_specs=[pl.BlockSpec(memo...]
    slice x15 -> x5, local copies, waits for them, and re-layouts: 7.7 us -> 1.6 us  [the longest x1 0.85 us: on_device(): shared[:, 5]]
    unnamed x92 -> x55, local copies, waits for them, and re-layouts: 14.3 us -> 13.6 us
where the time goes in v4:
time: 505 us; the launch traced here: 504 us
  Pallas kernels  464 us (92%)
  local copies, waits for them, and re-layouts  33.2 us (7%)
  other arithmetic  5.51 us (1%)
    pallas_call x1, Pallas kernels, layers_forward(): pl.pallas_call(forward_kernel, grid=(steps,), in_specs=[pl.BlockSpec(memo...  207 us
    pallas_call x1, Pallas kernels, layers_backward(): pl.pallas_call(backward_kernel, grid=(steps,), in_specs=[pl.BlockSpec(mem...  163 us
    pallas_call x1, Pallas kernels, end_exchange(): pl.pallas_call(end_kernel, in_specs=[pl.BlockSpec(memory_space=pltpu.SMEM...  94 us
    unnamed x55, local copies, waits for them, and re-layouts  13.6 us

profile of v4, /device:TPU:1, one launch (start us, length us, event | category | flops | bytes accessed | tf_op | source)
XLA Modules:
  0.0 504.0 jit_solution(7782899573693353007)
XLA Ops:
  0.7 0.8 compare_select_fusion.2
  1.5 0.6 scatter_custom_fusion
  2.2 0.8 slice_bitcast_fusion.1
  3.1 1.4 gather_fusion
  5.0 0.7 reshape.97
  5.8 0.7 fusion.27
  6.5 0.8 slice_convert_fusion.1
  7.3 0.8 fusion.26
  8.1 0.8 fusion.25
  9.3 0.7 convert_dynamic-update-slice_fusion.own_gains_ref
  10.7 1.8 gather_fusion.2
  12.6 3.2 gather_fusion.1
  15.9 206.9 %layers_forward.1 = (bf16[4096,1024]{1,0:T(8,128)(2,1)}, bf16[4096,512]{1,0:T(8,128)(2,1)}, bf16[4096,768]{1,0:T(8,128)(2,1)}, f32[4096,768]{1,0:T(8,128)}, f32[...) custom-call(s32[2]{0:T(128)S(1)} %slice_bitcast_fusion.4.off_ref, ...), custom_call_target="tpu_custom_call" | custom-call | flops 60000002048 | bytes 60000000 | tf_op jit(solution)/shard_map/layers_forward/pallas_call | solution.py:994
  222.8 1.0 copy-done.7
  223.8 1.0 copy-done.8
  224.8 1.0 copy-done.9
  225.8 1.0 copy-done.10
  226.8 0.8 copy-done.11
  227.6 0.6 copy-done.12
  228.2 163.3 %layers_backward.1 = (bf16[8,64,1024]{2,1,0:T(8,128)(2,1)}, f32[2,8,1024]{2,1,0:T(8,128)}, f32[128,1920]{1,0:T(8,128)}, bf16[1024,1920]{1,0:T(8,128)(2,1)}, bf16[8,3,128,256]{3,2,1,0:T(8,128)(2,1)}) custom-call(s32[2]{0:T(128)} %copy-done.6, bf16[8,256,256]{2,1,0:T(8,128)(2,1)} %copy-done.10, bf16[16,64,1024]{2,1,0:T(8,128)(2,1)} %get-tuple-element.39.tot_ref, ...), custom_call_target="tpu_custom_call" | custom-call | flops 60000002048 | bytes 60000000 | tf_op jit(solution)/shard_map/layers_backward/pallas_call | solution.py:1061
  391.5 3.2 gather_fusion.3
  394.7 94.0 %end_exchange.1 = (bf16[8,3,128,256]{3,2,1,0:T(8,128)(2,1)}, f32[128,1920]{1,0:T(8,128)}, f32[2,8,1024]{2,1,0:T(8,128)}, f32[2,8,1024]{2,1,0:T(8,128)}, f32[2,128,256]{2,1,0:T(8,128)}) custom-call(s32[2]{0:T(128)} %copy-done.6, bf16[8,64,1024]{2,1,0:T(8,128)(2,1)} %get-tuple-element.55.grad_ref, bf16[1024,1920]{1,0:T(8,128)(2,1)} %get-tuple-element.56.packs_ref, ...), custom_call_target="tpu_custom_call" | custom-call | flops 60000002048 | bytes 60000000 | tf_op jit(solution)/shard_map/end_exchange/pallas_call | solution.py:1456
  488.7 3.4 gather_fusion.4
  492.1 0.8 slice.129
  493.0 0.7 slice.134
  494.3 0.6 copy.51
  494.9 0.6 copy.50
  496.9 0.7 fusion.3
  497.6 1.2 fusion.2
  498.8 1.6 copy.49
  500.3 2.0 copy.53
  502.4 1.7 copy.79
  (85 shorter events, 3.7 us)
Async XLA Ops:
  0.6 10.1 %copy-start = (bf16[24,128,256]{2,1,0:T(8,128)(2,1)S(1)}, bf16[24,128,256]{2,1,0:T(8,128)(2,1)}, u32[]{:S(2)}) copy-start(bf16[24,128,256]{2,1,0:T(8,128)(2,1)} %param.15) | copy-start | bytes 4718596
  0.7 9.5 %copy-start.15 = (bf16[2,512,128]{2,1,0:T(8,128)(2,1)S(1)}, bf16[2,512,128]{2,1,0:T(8,128)(2,1)}, u32[]{:S(2)}) copy-start(bf16[2,512,128]{2,1,0:T(8,128)(2,1)} %param.27) | copy-start | bytes 786436
  0.7 9.8 %copy-start.16 = (bf16[2,128,512]{2,1,0:T(8,128)(2,1)S(1)}, bf16[2,128,512]{2,1,0:T(8,128)(2,1)}, u32[]{:S(2)}) copy-start(bf16[2,128,512]{2,1,0:T(8,128)(2,1)} %param.19) | copy-start | bytes 786436
  4.5 6.0 %copy-start.17 = (bf16[2,128,512]{2,1,0:T(8,128)(2,1)S(1)}, bf16[2,128,512]{2,1,0:T(8,128)(2,1)}, u32[]{:S(2)}) copy-start(bf16[2,128,512]{2,1,0:T(8,128)(2,1)} %param.20) | copy-start | bytes 786436
  4.8 11.0 %copy-start.6 = (s32[2]{0:T(128)}, s32[2]{0:T(128)S(1)}, u32[]{:S(2)}) copy-start(s32[2]{0:T(128)S(1)} %slice_bitcast_fusion.4.off_ref) | copy-start | bytes 28
  7.3 8.5 %copy-start.5 = (f32[2,8,128]{2,1,0:T(8,128)}, f32[2,8,128]{2,1,0:T(8,128)S(1)}, u32[]{:S(2)}) copy-start(f32[2,8,128]{2,1,0:T(8,128)S(1)} %pad_maximum_fusion.3.head_ref) | copy-start | bytes 24580
  9.0 6.9 %copy-start.3 = (f32[2,8,768]{2,1,0:T(8,128)}, f32[2,8,768]{2,1,0:T(8,128)S(1)}, u32[]{:S(2)}) copy-start(f32[2,8,768]{2,1,0:T(8,128)S(1)} %maximum_convert_fusion.taps_ref) | copy-start | bytes 147460
  9.0 1.6 copy-start.18
  9.0 6.8 %copy-start.4 = (f32[2,8,512]{2,1,0:T(8,128)}, f32[2,8,512]{2,1,0:T(8,128)S(1)}, u32[]{:S(2)}) copy-start(f32[2,8,512]{2,1,0:T(8,128)S(1)} %pad_maximum_fusion.2.wide_ref) | copy-start | bytes 98308
  10.2 5.7 %copy-start.2 = (bf16[256,512]{1,0:T(8,128)(2,1)}, bf16[256,512]{1,0:T(8,128)(2,1)S(1)}, u32[]{:S(2)}) copy-start(bf16[256,512]{1,0:T(8,128)(2,1)S(1)} %select_convert_fusion.spread_ref) | copy-start | bytes 786436
  222.8 1.0 copy-start.7
  223.8 1.0 copy-start.8
  224.8 1.0 copy-start.9
  225.8 1.0 copy-start.10
  226.8 0.8 copy-start.11
  227.6 0.6 copy-start.12
  488.7 3.4 copy-start.19
  488.7 8.2 %copy-start.13 = (f32[128,1920]{1,0:T(8,128)S(1)}, f32[128,1920]{1,0:T(8,128)}, u32[]{:S(2)}) copy-start(f32[128,1920]{1,0:T(8,128)} %get-tuple-element.58.later_ref) | copy-start | bytes 2949124
  488.7 8.2 %copy-start.14 = (f32[128,1920]{1,0:T(8,128)S(1)}, f32[128,1920]{1,0:T(8,128)}, u32[]{:S(2)}) copy-start(f32[128,1920]{1,0:T(8,128)} %get-tuple-element.61) | copy-start | bytes 2949124
  497.6 6.5 %copy-start.1 = (bf16[24,128,256]{2,1,0:T(8,128)(2,1)S(1)}, bf16[24,128,256]{2,1,0:T(8,128)(2,1)}, u32[]{:S(2)}) copy-start(bf16[24,128,256]{2,1,0:T(8,128)(2,1)} %param.15) | copy-start | bytes 4718596

commit v5 on v4

--- a/solution.py
+++ b/solution.py
@@ -164,15 +164,19 @@
 
     def start(self):
         self.local().start()
-
-        @pl.loop(1, self.count)
+        self.start_steps(1, self.count)
+
+    def wait(self):
+        self.local().wait()
+        self.wait_steps(1, self.count)
+
+    def start_steps(self, begin, end):
+        @pl.loop(begin, end)
         def _(step):
             self.remote(step, (self.me + step) % self.count).start()
 
-    def wait(self):
-        self.local().wait()
-
-        @pl.loop(1, self.count)
+    def wait_steps(self, begin, end):
+        @pl.loop(begin, end)
         def _(step):
             self.remote(step, (self.me + step) % self.count).wait()
 
@@ -279,6 +283,7 @@
     before_ref, middle_ref, tot_ref, scale_ref, final_ref, gains_ref, cot_cols_ref, weights_ref,
     state, padded, rows, parts, from_pair, from_across, sq_own, sq_pair, sq_sums, sq_across,
     weights, arrived, cols, cot_arrived, all_gains, middle, kept,
+    before_buf, middle_buf, tot_buf, scale_buf, final_buf, cot_cols, keep_sems,
     sems, copy_sems, line_sems, bin_sems, cot_sems, gain_sems,
 ):
     step = pl.program_id(0)
@@ -290,10 +295,15 @@
     rings = (Ring(sems.at[0]), Ring(sems.at[1]))
     ring = rings[0]
     total_columns = weights.shape[2]
-    out_part, in_part = pl.ds(0, inner), pl.ds(inner, total_columns - inner)
-    line = LineGather(packs_ref.at[1], weights.at[1], line_sems.at[1])
-    in_line = LineGather(packs_ref.at[0, :, in_part], weights.at[0, :, in_part], line_sems.at[0])
-    out_line = LineGather(packs_ref.at[0, :, out_part], weights.at[0, :, out_part], line_sems.at[2])
+
+    def line_of(at_layer, begin, end, slot):
+        part = pl.ds(begin, end - begin)
+        return LineGather(packs_ref.at[at_layer, :, part], weights.at[at_layer, :, part], line_sems.at[slot])
+
+    cut = inner + (total_columns - inner) // (2 * LANES) * LANES
+    in_lines = [Lines([line_of(at, inner, cut, 3 * at), line_of(at, cut, total_columns, 3 * at + 1)]) for at in range(LAYERS)]
+    out_lines = [line_of(at, 0, inner, 3 * at + 2) for at in range(LAYERS)]
+    in_line, line = in_lines
     bins = BinExchange(True, tok_ref, arrived, bin_sems)
     cot_bins = BinExchange(True, cot_ref, cot_arrived, cot_sems)
     gain_tiles = TileGather(own_gains_ref, all_gains, gain_sems)
@@ -315,6 +325,13 @@
     def keep_weights(at):
         return pltpu.make_async_copy(weights.at[at], weights_ref.at[at], copy_sems.at[at])
 
+    def keep_copies():
+        kept_pairs = (
+            (before_buf, before_ref), (middle_buf, middle_ref), (tot_buf, tot_ref),
+            (scale_buf, scale_ref), (final_buf, final_ref), (cot_cols, cot_cols_ref),
+        )
+        return [pltpu.make_async_copy(a, b, keep_sems.at[at]) for at, (a, b) in enumerate(kept_pairs)]
+
     def clear():
         state[...] = jnp.zeros_like(state)
         padded[pl.ds(0, 8), :] = jnp.zeros((8, mixed), F32)
@@ -322,12 +339,21 @@
     @pl.when(step == 0)
     def _():
         ring.greet()
-        bins.start()
+        half = bins.count // 2
+        bins.local().start()
+        bins.start_steps(half - 1, half + 2)
         in_line.start_pair()
+        for part in (out_lines[0], line, out_lines[1]):
+            part.start_pair()
         gain_tiles.start()
         clear()
-        bins.wait()
+        bins.wait_steps(half - 1, half + 2)
         in_line.start_line()
+        bins.start_steps(1, half - 1)
+        bins.start_steps(half + 2, bins.count)
+        bins.local().wait()
+        bins.wait_steps(1, half - 1)
+        bins.wait_steps(half + 2, bins.count)
         pick_all(off_ref, arrived, cols)
         own_copy().start()
 
@@ -357,8 +383,8 @@
             in_line.stage(2)
             pass_rows(blocks // 2, blocks)
             in_line.stage(3)
-            out_line.start()
-            line.start()
+            for part in (out_lines[0], line, out_lines[1]):
+                part.start_line()
         else:
             pass_rows(0, blocks)
 
@@ -368,8 +394,8 @@
 
         in_line.finish()
         if not four:
-            out_line.start()
-            line.start()
+            for part in (out_lines[0], line, out_lines[1]):
+                part.start_line()
 
     @pl.when(step == blocks)
     def _():
@@ -447,48 +473,55 @@
     sq_own[step] = dot_nt(ones, high) + dot_nt(ones, low)
     sq_pair_copy(now, step).start()
 
+    def free_parts(at_layer, at):
+        if at_layer == 0:
+            gather(0, AG_PASS, at).wait_send()
+        else:
+            pair_copy(ring, at, parts, from_pair).wait_send()
+            across_copy(ring, at, parts, from_across).wait_send()
+
     def send_parts(at_ring, at, values, out_weights):
         store_parts(at_ring, at, dot_nt(values, out_weights), parts)
         pair_copy(at_ring, at, parts, from_pair).start()
 
-    @pl.when(step < DEFER)
-    def _():
-        kept[step] = gained
-
-    if four:
-        for stage in (1, 2, 3):
-
-            @pl.when(step == min(stage - 1, DEFER))
-            def _(stage=stage):
-                out_line.stage(stage)
-
-    @pl.when(step == DEFER)
-    def _():
-        if not four:
-
-            @pl.loop(1, line.line)
-            def _(stage):
-                out_line.stage(stage)
-
-        out_line.finish()
-        keep_weights(0).start()
-
-        @pl.loop(0, DEFER)
-        def _(at):
-            gather(0, AG_PASS, at).wait_send()
-            send_parts(ring, at, kept[at], weights[0, :, :inner])
-
-    @pl.when(layer > 0)
-    def _():
-        pair_copy(ring, block, parts, from_pair).wait_send()
-        across_copy(ring, block, parts, from_across).wait_send()
-
-    @pl.when((step >= DEFER) & (layer == 0))
-    def _():
-        gather(0, AG_PASS, block).wait_send()
-
-    @pl.when(step >= DEFER)
-    def _():
+    @pl.when(block < DEFER)
+    def _():
+        kept[block] = gained
+
+    for at_layer in range(LAYERS):
+        first_step = at_layer * blocks
+        if four:
+            for stage in (1, 2, 3):
+                when = min(stage - 1, DEFER) if at_layer == 0 else 2 * stage + 2
+
+                @pl.when(step == when)
+                def _(at_layer=at_layer, stage=stage):
+                    out_lines[at_layer].stage(stage)
+
+        @pl.when(step == first_step + DEFER)
+        def _(at_layer=at_layer):
+            if not four:
+
+                @pl.loop(1, line.line)
+                def _(stage):
+                    out_lines[at_layer].stage(stage)
+
+            out_lines[at_layer].finish()
+            keep_weights(at_layer).start()
+
+            @pl.loop(0, DEFER)
+            def _(at):
+                free_parts(at_layer, at)
+                send_parts(rings[at_layer], at, kept[at], weights[at_layer, :, :inner])
+
+    @pl.when(block >= DEFER)
+    def _():
+        for at_layer in range(LAYERS):
+
+            @pl.when(layer == at_layer)
+            def _(at_layer=at_layer):
+                free_parts(at_layer, block)
+
         send_parts(now, block, gained, weights[layer, :, :inner])
 
     def second_stage(slot):
@@ -511,21 +544,21 @@
         scale = lax.rsqrt(squares / INNER + eps)
         here = pl.ds(at * SHARE, SHARE)
         mine = pl.ds(ring.me * SHARE, SHARE)
-        tot_ref[slot] = total.astype(BF16)
-        scale_ref[slot] = scale
+        tot_buf[slot] = total.astype(BF16)
+        scale_buf[slot] = scale
         if at_layer == 0:
             before = rows[at, mine, :]
-            before_ref[at] = before
+            before_buf[at] = before
             hidden = before.astype(F32) + total * scale
             middle[at] = hidden
-            middle_ref[at] = hidden.astype(BF16)
+            middle_buf[at] = hidden.astype(BF16)
             mean = jnp.sum(hidden * hidden, axis=1, keepdims=True) / hidden.shape[1]
             later = (hidden * lax.rsqrt(mean + eps) * gains[1:2]).astype(BF16)
             rows[at, mine, :] = later
             gather(1, AG_ACROSS, at).start()
             gather(1, AG_OWN, at).start()
         else:
-            final_ref[at] = (middle[at] + total * scale).astype(BF16)
+            final_buf[at] = (middle[at] + total * scale).astype(BF16)
 
     @pl.when((step >= LAG) & (step < blocks + LAG))
     def _():
@@ -536,13 +569,13 @@
         last_stage(1, step - LAG - blocks)
 
     if four:
-        for stage, when in ((1, 0), (2, 2), (3, 4)):
+        for stage, when in ((1, 1), (2, 3), (3, 5)):
 
             @pl.when(step == when)
             def _(stage=stage):
                 line.stage(stage)
 
-    @pl.when(step == 2)
+    @pl.when(step == blocks)
     def _():
         cot_bins.start()
 
@@ -551,13 +584,13 @@
         gather(1, AG_ACROSS, (step + PASS_AHEAD) % blocks).wait_recv()
         gather(1, AG_PASS, (step + PASS_AHEAD) % blocks).start()
 
-    @pl.when(step == DEFER + 1)
+    @pl.when((step % blocks == DEFER + 1) & (step > 0))
     def _():
         @pl.loop(0, DEFER)
         def _(at):
-            second_stage(at)
-
-    @pl.when(step > DEFER)
+            second_stage(layer * blocks + at)
+
+    @pl.when((step > 0) & ((step - 1 + blocks) % blocks >= DEFER))
     def _():
         second_stage(step - 1)
 
@@ -570,17 +603,23 @@
                 line.stage(stage)
 
         line.finish()
-        keep_weights(1).start()
 
     @pl.when(step == 2 * blocks - 1)
     def _():
         second_stage(step)
         cot_bins.wait()
-        pick_all(off_ref, cot_arrived, cot_cols_ref)
+        pick_all(off_ref, cot_arrived, cot_cols)
+
+        before_keep, middle_keep, *late_keep, cot_keep = keep_copies()
+        for copy in (before_keep, middle_keep, cot_keep):
+            copy.start()
 
         @pl.loop(blocks - LAG, blocks)
         def _(at):
             last_stage(1, at)
+
+        for copy in late_keep:
+            copy.start()
 
         @pl.loop(0, blocks)
         def _(at):
@@ -596,6 +635,8 @@
 
         for at in range(LAYERS):
             keep_weights(at).wait()
+        for copy in (before_keep, middle_keep, *late_keep, cot_keep):
+            copy.wait()
 
 
 def own_line(column):
@@ -611,13 +652,13 @@
 
 
 def backward_kernel(
-    off_ref, cot_ref, tot_ref, scale_ref, before_ref, middle_ref, gains_ref, taps_ref, head_ref, wide_ref, spread_ref,
+    off_ref, cot_in, tot_in, scale_in, before_ref, middle_ref, gains_ref, taps_ref, head_ref, wide_ref, spread_ref,
     weights_ref, final_ref,
     z_ref, in_ref, pre_ref, dt_ref, y_ref, st_ref, normed_ref, gg_ref,
-    ginput_ref, small_ref, pack_ref, packs_ref, back_ref,
+    gcols_out, small_ref, pack_ref, packs_ref, back_ref,
     dstate, padded, rows, parts, from_pair, from_across, tiles, held, running, weights, acc_out, acc_in,
     packs, pair_buf, arrivals, cols, slots,
-    sems, copy_sems, line_sems, row_sems, bin_sems,
+    cot_ref, tot_ref, scale_ref, ginput, gcols_ref, sems, copy_sems, line_sems, row_sems, bin_sems, load_sems, col_sems,
 ):
     step = pl.program_id(0)
     inner = y_ref.shape[1]
@@ -665,6 +706,22 @@
         gather(at_phase, AG_ACROSS, at).wait_recv()
         gather(at_phase, AG_PASS, at).start()
 
+    def load_inputs():
+        pairs = ((cot_in, cot_ref), (tot_in, tot_ref), (scale_in, scale_ref))
+        return [pltpu.make_async_copy(a, b, load_sems.at[at]) for at, (a, b) in enumerate(pairs)]
+
+    def column_copy(at, hop):
+        other = (ring.me + hop) % 4
+        columns = gcols_ref.shape[2]
+        source = ginput.at[at, :, pl.ds(pl.multiple_of(other * columns, LANES), columns)]
+        target = gcols_ref.at[at, mine, :]
+        if hop == 0:
+            return pltpu.make_async_copy(source, target, col_sems.at[at, 0, 0])
+        return pltpu.make_async_remote_copy(
+            src_ref=source, dst_ref=target, send_sem=col_sems.at[at, hop, 0], recv_sem=col_sems.at[at, hop, 1],
+            device_id={"tensor": other}, device_id_type=pl.DeviceIdType.MESH,
+        )
+
     def send_rows(at):
         gather(0, AG_ACROSS, at).start()
         gather(0, AG_OWN, at).start()
@@ -689,9 +746,13 @@
 
     @pl.when(step == 0)
     def _():
-        own_copy().start()
+        cot_load, *loads = load_inputs()
+        for copy in (cot_load, *loads):
+            copy.start()
         load_weights(LAYERS - 1).start()
         load_held(0).start()
+        cot_load.wait()
+        own_copy().start()
         ring.greet()
 
         send_rows(blocks - 1)
@@ -701,6 +762,8 @@
         pass_rows(0, blocks - 1)
         for at in range(1, QUEUED):
             send_rows(blocks - 1 - at)
+        for copy in loads:
+            copy.wait()
         prepare(blocks - 1)
         for at in range(1, AHEAD + 1):
             pass_rows(0, blocks - 1 - at)
@@ -871,7 +934,9 @@
             gather(1, AG_OWN, at).start()
             make_tile(1, at, grad_low)
         else:
-            ginput_ref[at] = (running[at] + change).astype(BF16)
+            ginput[at] = (running[at] + change).astype(BF16)
+            for hop in range(4):
+                column_copy(at, hop).start()
 
     @pl.when(step == BACK_LAG)
     def _():
@@ -963,6 +1028,14 @@
                 for copy in tile_copies(at_phase, at):
                     copy.wait_send()
 
+        @pl.loop(0, blocks)
+        def _(at):
+            for hop in range(4):
+                column_copy(at, hop).wait()
+
+        keep_columns = pltpu.make_async_copy(gcols_ref, gcols_out, load_sems.at[0])
+        keep_columns.start()
+        keep_columns.wait()
         store_packs().wait()
         bins.wait()
 
@@ -999,7 +1072,7 @@
             by_block(width), by_block(inner), by_block(mixed), by_block(mixed),
             by_block(LANES), by_block(inner), by_block(inner),
             pl.BlockSpec((1, STATE, inner), lambda s: (s, 0, 0)),
-            vmem, vmem, vmem, vmem, vmem, vmem, vmem, hbm,
+            hbm, hbm, hbm, hbm, hbm, vmem, hbm, hbm,
         ],
         out_shape=[
             jax.ShapeDtypeStruct((steps * BLK, width), BF16),
@@ -1030,9 +1103,16 @@
             pltpu.VMEM((dp_count,) + own_gains.shape, F32),
             pltpu.VMEM((blocks, SHARE, width), F32),
             pltpu.VMEM((DEFER, BLK, inner), BF16),
+            pltpu.VMEM((blocks, SHARE, width), BF16),
+            pltpu.VMEM((blocks, SHARE, width), BF16),
+            pltpu.VMEM((steps, SHARE, width), BF16),
+            pltpu.VMEM((steps, SHARE, 1), F32),
+            pltpu.VMEM((blocks, SHARE, width), BF16),
+            pltpu.VMEM((blocks, BLK, columns), BF16),
+            pltpu.SemaphoreType.DMA((6,)),
             pltpu.SemaphoreType.DMA((LAYERS, 7, blocks, 2)),
             pltpu.SemaphoreType.DMA((LAYERS + 1,)),
-            pltpu.SemaphoreType.DMA((LAYERS + 1, 6, dp_count // 2)),
+            pltpu.SemaphoreType.DMA((3 * LAYERS, 6, dp_count // 2)),
             pltpu.SemaphoreType.DMA((dp_count, 2)),
             pltpu.SemaphoreType.DMA((dp_count, 2)),
             pltpu.SemaphoreType.DMA((dp_count, 2)),
@@ -1062,8 +1142,7 @@
         backward_kernel,
         grid=(steps,),
         in_specs=[pl.BlockSpec(memory_space=pltpu.SMEM)]
-        + [vmem] * 3
-        + [hbm, hbm]
+        + [hbm] * 5
         + [vmem] * 5
         + [hbm, hbm]
         + [
@@ -1071,9 +1150,9 @@
             pl.BlockSpec((1, STATE, inner), lambda s: (steps - 1 - s, 0, 0)),
             by_block(width), by_block(inner),
         ],
-        out_specs=[vmem, vmem, vmem, hbm, hbm],
+        out_specs=[hbm, vmem, vmem, hbm, hbm],
         out_shape=[
-            jax.ShapeDtypeStruct((blocks, SHARE, width), BF16),
+            jax.ShapeDtypeStruct((blocks, BLK, columns), BF16),
             jax.ShapeDtypeStruct((LAYERS, 8, width), F32),
             jax.ShapeDtypeStruct((width // count, total), F32),
             jax.ShapeDtypeStruct((width, total), BF16),
@@ -1095,11 +1174,18 @@
             pltpu.VMEM((count // 2 + 1, width // count, total), BF16),
             pltpu.VMEM((BIN, columns), BF16),
             pltpu.VMEM((3, count * span, columns), BF16),
+            pltpu.VMEM(cot.shape, BF16),
+            pltpu.VMEM(totals.shape, BF16),
+            pltpu.VMEM(scales.shape, F32),
+            pltpu.VMEM((blocks, SHARE, width), BF16),
+            pltpu.VMEM((blocks, BLK, columns), BF16),
             pltpu.SemaphoreType.DMA((LAYERS, 8, blocks, 2)),
             pltpu.SemaphoreType.DMA((3 + LAYERS,)),
             pltpu.SemaphoreType.DMA((5, count // 2)),
             pltpu.SemaphoreType.DMA((4, 2)),
             pltpu.SemaphoreType.DMA((count, 2)),
+            pltpu.SemaphoreType.DMA((3,)),
+            pltpu.SemaphoreType.DMA((blocks, 4, 2)),
         ],
         compiler_params=pltpu.CompilerParams(
             vmem_limit_bytes=61 * 1024 * 1024, collective_id=2, has_side_effects=True
@@ -1250,6 +1336,30 @@
                 self.left(place).wait_send()
 
 
+class Lines:
+    def __init__(self, parts):
+        self.parts, self.line = parts, parts[0].line
+
+    def each(self, name, *given):
+        for part in self.parts:
+            getattr(part, name)(*given)
+
+    def start(self):
+        self.each("start")
+
+    def start_pair(self):
+        self.each("start_pair")
+
+    def start_line(self):
+        self.each("start_line")
+
+    def stage(self, step):
+        self.each("stage", step)
+
+    def finish(self):
+        self.each("finish")
+
+
 class TileGather:
     def __init__(self, own, target, sems):
         self.own, self.target, self.sems = own, target, sems
@@ -1398,27 +1508,32 @@
 
 
 def end_kernel(
-    off_ref, grad_ref, packs_ref, small_ref, later_ref,
+    off_ref, cols_ref, packs_ref, small_ref, later_ref,
     back_ref, pack_ref, sum_ref, shared_ref, maps_ref,
-    cols, slots, pair_buf, arrivals, line_sems, smalls, shared, maps,
-    row_sems, bin_sems, small_sems, shared_sems, maps_sems,
+    slots, pair_buf, arrivals, line_sems, smalls, shared, maps,
+    bin_sems, small_sems, shared_sems, maps_sems,
 ):
     ring = Ring(None)
     ring.greet()
     inner = (pack_ref.shape[1] - 2 * STATE - LANES) // 3
     first_map = 3 * inner
-    rows = RowExchange(False, grad_ref, cols.reshape(BIN // BLK, BLK, cols.shape[1]), row_sems)
     bins = BinExchange(False, slots, back_ref, bin_sems)
-    line = LineReduce(packs_ref, pack_ref, pair_buf, arrivals, line_sems)
+    cut = pack_ref.shape[1] // (2 * LANES) * LANES
+    line = Lines(
+        [
+            LineReduce(
+                packs_ref.at[:, part], pack_ref.at[:, part], pair_buf.at[:, :, part], arrivals.at[:, :, part], line_sems.at[at]
+            )
+            for at, part in enumerate((pl.ds(0, cut), pl.ds(cut, pack_ref.shape[1] - cut)))
+        ]
+    )
     dp_smalls = TileGather(small_ref, smalls, small_sems)
     shared_smalls = MemberGather(shared, shared_sems)
     shared_maps = MemberGather(maps, maps_sems)
-    rows.start()
-    line.send_pairs()
+    line.each("send_pairs")
+    place_all(off_ref, cols_ref, slots)
+    bins.start()
     dp_smalls.start()
-    rows.wait()
-    place_all(off_ref, cols, slots)
-    bins.start()
 
     @pl.loop(0, line.line - 1)
     def _(step):
@@ -1447,7 +1562,7 @@
     bins.wait()
 
 
-def end_exchange(offsets, grad_rows, packs, small, later_pack, span):
+def end_exchange(offsets, grad_columns, packs, small, later_pack, span):
     count = lax.axis_size("dp")
     width, total = packs.shape
     columns = width // 4
@@ -1464,16 +1579,13 @@
             jax.ShapeDtypeStruct(small.shape, F32),
             jax.ShapeDtypeStruct((LAYERS, pack_rows, 2 * STATE), F32),
         ],
-        scratch_shapes=[
-            pltpu.VMEM((BIN, columns), BF16),
-            pltpu.VMEM((3, count * span, columns), BF16),
-        ]
-        + line_scratch(count, pack_rows, total)
+        scratch_shapes=[pltpu.VMEM((3, count * span, columns), BF16)]
+        + line_scratch(count, pack_rows, total)[:2]
         + [
+            pltpu.SemaphoreType.DMA((2, 5, count // 2)),
             pltpu.VMEM((count,) + small.shape, F32),
             pltpu.VMEM((4,) + small.shape, F32),
             pltpu.VMEM((4, LAYERS, pack_rows, 2 * STATE), BF16),
-            pltpu.SemaphoreType.DMA((4, 2)),
             pltpu.SemaphoreType.DMA((count, 2)),
             pltpu.SemaphoreType.DMA((count, 2)),
             pltpu.SemaphoreType.DMA((4, 2)),
@@ -1484,7 +1596,7 @@
         ),
         cost_estimate=pl.CostEstimate(flops=6 * 10**10, bytes_accessed=6 * 10**7, transcendentals=0),
         name="end_exchange",
-    )(offsets, grad_rows, packs, small, later_pack)
+    )(offsets, grad_columns.reshape(BIN, columns), packs, small, later_pack)
 
 
 def pad_to(values, rows, columns):
@@ -1505,7 +1617,8 @@
     offsets = jnp.cumsum(triples, axis=1) - triples
     my_offsets = offsets[bin_index]
     bounds = my_offsets[1:3]
-    groups = packing.reshape(dp_count, 3)
+    by_bin = (dp_count, 3, pos_here, cols_here)
+    given_tokens, given_cot = (array[packing].reshape(by_bin) for array in (tokens, cotangent))
 
     spread = spread_matrix(inner_part, heads_here)
     packs = []
@@ -1528,14 +1641,14 @@
         rows_all, gate, mixed_in, conv, dt_raw, mixed_out, gained_all, states, first_before, middle, totals, scales,
         final_rows, gains, cot_columns, all_weights,
     ) = layers_forward(
-        bounds, tokens[groups], jnp.stack([pack[0] for pack in packs]), own_gains, cotangent[groups],
+        bounds, given_tokens, jnp.stack([pack[0] for pack in packs]), own_gains, given_cot,
         taps_all, head_all, wide_all, spread,
     )
-    grad_rows, small, later_pack, first_packs, activations_back = layers_backward(
+    grad_columns, small, later_pack, first_packs, activations_back = layers_backward(
         bounds, cot_columns, totals, scales, first_before, middle, gains, taps_all, head_all, wide_all, spread,
         all_weights, final_rows, (gate, mixed_in, conv, dt_raw, mixed_out, states, rows_all, gained_all), pos_here,
     )
-    returned, first_pack, sums, shared, maps = end_exchange(bounds, grad_rows, first_packs, small, later_pack, pos_here)
+    returned, first_pack, sums, shared, maps = end_exchange(bounds, grad_columns, first_packs, small, later_pack, pos_here)
     grad_convx = sums[:, : CONV + 1, :inner_part]
     grad_convbc = shared[:, : CONV + 1, inner_part:mixed]
     shard_pre = lax.dynamic_slice_in_dim(shared[:, 5], bin_index * dp_rows, dp_rows, 1)

time: 505 us -> 478 us (0.947)
  Pallas kernels: 464 us -> 438 us
    pallas_call x1, Pallas kernels: 207 us -> 194 us  [layers_forward(): pl.pallas_call(forward_kernel, grid=(steps,), in_specs=[pl.BlockSpec(memo...]
    pallas_call x1, Pallas kernels: 94 us -> 85.4 us  [end_exchange(): pl.pallas_call(end_kernel, in_specs=[pl.BlockSpec(memory_space=pltpu.SMEM...]
where the time goes in v5:
time: 478 us; the launch traced here: 477 us
  Pallas kernels  438 us (92%)
  local copies, waits for them, and re-layouts  32.4 us (7%)
  other arithmetic  5.5 us (1%)
    pallas_call x1, Pallas kernels, layers_forward(): pl.pallas_call(forward_kernel, grid=(steps,), in_specs=[pl.BlockSpec(memo...  194 us
    pallas_call x1, Pallas kernels, layers_backward(): pl.pallas_call(backward_kernel, grid=(steps,), in_specs=[pl.BlockSpec(mem...  159 us
    pallas_call x1, Pallas kernels, end_exchange(): pl.pallas_call(end_kernel, in_specs=[pl.BlockSpec(memory_space=pltpu.SMEM...  85.4 us
    unnamed x55, local copies, waits for them, and re-layouts  13.6 us

profile of v5, /device:TPU:1, one launch (start us, length us, event | category | flops | bytes accessed | tf_op | source)
XLA Modules:
  0.0 477.3 jit_solution(6373648818396593558)
XLA Ops:
  0.7 0.8 compare_select_fusion.1
  1.5 0.6 scatter_custom_fusion
  2.2 0.8 slice_bitcast_fusion.1
  3.3 0.7 fusion.27
  4.0 0.8 slice_convert_fusion.1
  4.7 1.4 gather_fusion
  6.5 0.8 fusion.26
  7.3 0.8 fusion.25
  8.5 0.7 convert_dynamic-update-slice_fusion.own_gains_ref
  9.9 1.8 gather_fusion.2
  11.7 3.2 gather_fusion.1
  15.0 193.9 %layers_forward.1 = (bf16[4096,1024]{1,0:T(8,128)(2,1)}, bf16[4096,512]{1,0:T(8,128)(2,1)}, bf16[4096,768]{1,0:T(8,128)(2,1)}, f32[4096,768]{1,0:T(8,128)}, f32[...) custom-call(s32[2]{0:T(128)S(1)} %slice_bitcast_fusion.4.off_ref, ...), custom_call_target="tpu_custom_call" | custom-call | flops 60000002048 | bytes 60000000 | tf_op jit(solution)/shard_map/layers_forward/pallas_call | solution.py:1067
  209.0 1.0 copy-done.7
  210.0 1.0 copy-done.8
  210.9 1.0 copy-done.9
  212.0 1.0 copy-done.10
  212.9 0.8 copy-done.11
  213.7 0.6 copy-done.12
  214.3 159.0 %layers_backward.1 = (bf16[8,256,256]{2,1,0:T(8,128)(2,1)}, f32[2,8,1024]{2,1,0:T(8,128)}, f32[128,1920]{1,0:T(8,128)}, bf16[1024,1920]{1,0:T(8,128)(2,1)}, bf16[8,3,128,256]{3,2,1,0:T(8,128)(2,1)}) custom-call(s32[2]{0:T(128)} %copy-done.6, bf16[8,256,256]{2,1,0:T(8,128)(2,1)} %copy-done.10, bf16[16,64,1024]{2,1,0:T(8,128)(2,1)} %get-tuple-element.39.tot_in, ...), custom_call_target="tpu_custom_call" | custom-call | flops 60000002048 | bytes 60000000 | tf_op jit(solution)/shard_map/layers_backward/pallas_call | solution.py:1141
  373.3 3.2 gather_fusion.3
  376.6 85.4 %end_exchange.1 = (bf16[8,3,128,256]{3,2,1,0:T(8,128)(2,1)}, f32[128,1920]{1,0:T(8,128)}, f32[2,8,1024]{2,1,0:T(8,128)}, f32[2,8,1024]{2,1,0:T(8,128)}, f32[2,128,256]{2,1,0:T(8,128)}) custom-call(s32[2]{0:T(128)} %copy-done.6, bf16[2048,256]{1,0:T(8,128)(2,1)} %bitcast.90, bf16[1024,1920]{1,0:T(8,128)(2,1)} %get-tuple-element.56.packs_ref, ...), custom_call_target="tpu_custom_call" | custom-call | flops 60000002048 | bytes 60000000 | tf_op jit(solution)/shard_map/end_exchange/pallas_call | solution.py:1571
  462.0 3.4 gather_fusion.4
  465.4 0.8 slice.129
  466.3 0.7 slice.134
  467.5 0.6 copy.51
  468.2 0.6 copy.50
  468.8 0.6 copy.68
  470.2 0.7 fusion.3
  470.8 1.2 fusion.2
  472.0 1.6 copy.49
  473.6 2.0 copy.53
  475.6 1.7 copy.79
  (81 shorter events, 3.1 us)
Async XLA Ops:
  0.6 9.3 %copy-start = (bf16[24,128,256]{2,1,0:T(8,128)(2,1)S(1)}, bf16[24,128,256]{2,1,0:T(8,128)(2,1)}, u32[]{:S(2)}) copy-start(bf16[24,128,256]{2,1,0:T(8,128)(2,1)} %param.15) | copy-start | bytes 4718596
  0.7 8.7 %copy-start.15 = (bf16[2,512,128]{2,1,0:T(8,128)(2,1)S(1)}, bf16[2,512,128]{2,1,0:T(8,128)(2,1)}, u32[]{:S(2)}) copy-start(bf16[2,512,128]{2,1,0:T(8,128)(2,1)} %param.27) | copy-start | bytes 786436
  0.7 9.0 %copy-start.16 = (bf16[2,128,512]{2,1,0:T(8,128)(2,1)S(1)}, bf16[2,128,512]{2,1,0:T(8,128)(2,1)}, u32[]{:S(2)}) copy-start(bf16[2,128,512]{2,1,0:T(8,128)(2,1)} %param.19) | copy-start | bytes 786436
  6.1 3.6 copy-start.17
  6.4 8.6 %copy-start.6 = (s32[2]{0:T(128)}, s32[2]{0:T(128)S(1)}, u32[]{:S(2)}) copy-start(s32[2]{0:T(128)S(1)} %slice_bitcast_fusion.4.off_ref) | copy-start | bytes 28
  6.5 8.5 %copy-start.5 = (f32[2,8,128]{2,1,0:T(8,128)}, f32[2,8,128]{2,1,0:T(8,128)S(1)}, u32[]{:S(2)}) copy-start(f32[2,8,128]{2,1,0:T(8,128)S(1)} %pad_maximum_fusion.3.head_ref) | copy-start | bytes 24580
  8.1 6.9 %copy-start.3 = (f32[2,8,768]{2,1,0:T(8,128)}, f32[2,8,768]{2,1,0:T(8,128)S(1)}, u32[]{:S(2)}) copy-start(f32[2,8,768]{2,1,0:T(8,128)S(1)} %maximum_convert_fusion.taps_ref) | copy-start | bytes 147460
  8.2 1.6 copy-start.18
  8.2 6.8 %copy-start.4 = (f32[2,8,512]{2,1,0:T(8,128)}, f32[2,8,512]{2,1,0:T(8,128)S(1)}, u32[]{:S(2)}) copy-start(f32[2,8,512]{2,1,0:T(8,128)S(1)} %pad_maximum_fusion.2.wide_ref) | copy-start | bytes 98308
  9.3 5.7 %copy-start.2 = (bf16[256,512]{1,0:T(8,128)(2,1)}, bf16[256,512]{1,0:T(8,128)(2,1)S(1)}, u32[]{:S(2)}) copy-start(bf16[256,512]{1,0:T(8,128)(2,1)S(1)} %select_convert_fusion.spread_ref) | copy-start | bytes 786436
  209.0 1.0 copy-start.7
  210.0 1.0 copy-start.8
  210.9 1.0 copy-start.9
  212.0 1.0 copy-start.10
  212.9 0.8 copy-start.11
  213.7 0.6 copy-start.12
  462.0 3.4 copy-start.19
  462.0 8.2 %copy-start.13 = (f32[128,1920]{1,0:T(8,128)S(1)}, f32[128,1920]{1,0:T(8,128)}, u32[]{:S(2)}) copy-start(f32[128,1920]{1,0:T(8,128)} %get-tuple-element.58.later_ref) | copy-start | bytes 2949124
  462.0 8.2 %copy-start.14 = (f32[128,1920]{1,0:T(8,128)S(1)}, f32[128,1920]{1,0:T(8,128)}, u32[]{:S(2)}) copy-start(f32[128,1920]{1,0:T(8,128)} %get-tuple-element.61) | copy-start | bytes 2949124
  470.8 6.5 %copy-start.1 = (bf16[24,128,256]{2,1,0:T(8,128)(2,1)S(1)}, bf16[24,128,256]{2,1,0:T(8,128)(2,1)}, u32[]{:S(2)}) copy-start(bf16[24,128,256]{2,1,0:T(8,128)(2,1)} %param.15) | copy-start | bytes 4718596

commit v6 on v5

--- a/solution.py
+++ b/solution.py
@@ -278,13 +278,13 @@
 
 
 def forward_kernel(
-    off_ref, tok_ref, packs_ref, own_gains_ref, cot_ref, taps_ref, head_ref, wide_ref, spread_ref,
+    off_ref, tok_ref, packs_ref, cot_ref, taps_ref, head_ref, wide_ref, spread_ref,
     rows_ref, z_ref, in_ref, pre_ref, dt_ref, y_ref, gg_ref, st_ref,
     before_ref, middle_ref, tot_ref, scale_ref, final_ref, gains_ref, cot_cols_ref, weights_ref,
     state, padded, rows, parts, from_pair, from_across, sq_own, sq_pair, sq_sums, sq_across,
-    weights, arrived, cols, cot_arrived, all_gains, middle, kept,
+    weights, arrived, cols, cot_arrived, middle, kept,
     before_buf, middle_buf, tot_buf, scale_buf, final_buf, cot_cols, keep_sems,
-    sems, copy_sems, line_sems, bin_sems, cot_sems, gain_sems,
+    sems, copy_sems, line_sems, bin_sems, cot_sems,
 ):
     step = pl.program_id(0)
     inner = y_ref.shape[1]
@@ -306,7 +306,6 @@
     in_line, line = in_lines
     bins = BinExchange(True, tok_ref, arrived, bin_sems)
     cot_bins = BinExchange(True, cot_ref, cot_arrived, cot_sems)
-    gain_tiles = TileGather(own_gains_ref, all_gains, gain_sems)
     four = line.line == 4
 
     def gather(at_layer, kind, at):
@@ -345,7 +344,6 @@
         in_line.start_pair()
         for part in (out_lines[0], line, out_lines[1]):
             part.start_pair()
-        gain_tiles.start()
         clear()
         bins.wait_steps(half - 1, half + 2)
         in_line.start_line()
@@ -362,13 +360,6 @@
             gather(0, AG_ACROSS, at).start()
             gather(0, AG_OWN, at).start()
 
-        gain_tiles.wait()
-        gains_ref[...] = all_gains[0]
-
-        @pl.loop(1, all_gains.shape[0])
-        def _(at):
-            gains_ref[...] += all_gains[at]
-
         own_copy().wait()
 
         def pass_rows(begin, end):
@@ -393,6 +384,8 @@
                 in_line.stage(stage)
 
         in_line.finish()
+        last_columns = weights[0, :, total_columns - LANES :].astype(F32)
+        gains_ref[...] = jnp.transpose(last_columns)[8:16]
         if not four:
             for part in (out_lines[0], line, out_lines[1]):
                 part.start_line()
@@ -1053,8 +1046,8 @@
     ]
 
 
-def layers_forward(offsets, given, packs, own_gains, given_cot, taps, head, wide, spread):
-    blocks, width = BIN // BLK, own_gains.shape[1]
+def layers_forward(offsets, given, packs, given_cot, taps, head, wide, spread):
+    blocks, width = BIN // BLK, given_cot.shape[0] * packs.shape[1]
     inner, mixed = wide.shape[2], taps.shape[2]
     dp_count, members, span, columns = given_cot.shape
     total = packs.shape[2]
@@ -1067,7 +1060,7 @@
     return pl.pallas_call(
         forward_kernel,
         grid=(steps,),
-        in_specs=[pl.BlockSpec(memory_space=pltpu.SMEM), hbm, vmem, vmem, hbm] + [vmem] * 4,
+        in_specs=[pl.BlockSpec(memory_space=pltpu.SMEM), hbm, vmem, hbm] + [vmem] * 4,
         out_specs=[
             by_block(width), by_block(inner), by_block(mixed), by_block(mixed),
             by_block(LANES), by_block(inner), by_block(inner),
@@ -1088,7 +1081,7 @@
             jax.ShapeDtypeStruct((steps, SHARE, width), BF16),
             jax.ShapeDtypeStruct((steps, SHARE, 1), F32),
             jax.ShapeDtypeStruct((blocks, SHARE, width), BF16),
-            jax.ShapeDtypeStruct(own_gains.shape, F32),
+            jax.ShapeDtypeStruct((8, width), F32),
             jax.ShapeDtypeStruct((blocks, BLK, columns), BF16),
             jax.ShapeDtypeStruct((LAYERS, width, total), BF16),
         ],
@@ -1100,7 +1093,6 @@
             pltpu.VMEM((members, dp_count * span, columns), BF16),
             pltpu.VMEM((blocks, BLK, columns), BF16),
             pltpu.VMEM((members, dp_count * span, columns), BF16),
-            pltpu.VMEM((dp_count,) + own_gains.shape, F32),
             pltpu.VMEM((blocks, SHARE, width), F32),
             pltpu.VMEM((DEFER, BLK, inner), BF16),
             pltpu.VMEM((blocks, SHARE, width), BF16),
@@ -1115,14 +1107,13 @@
             pltpu.SemaphoreType.DMA((3 * LAYERS, 6, dp_count // 2)),
             pltpu.SemaphoreType.DMA((dp_count, 2)),
             pltpu.SemaphoreType.DMA((dp_count, 2)),
-            pltpu.SemaphoreType.DMA((dp_count, 2)),
         ],
         compiler_params=pltpu.CompilerParams(
             vmem_limit_bytes=48 * 1024 * 1024, collective_id=1, has_side_effects=True
         ),
         cost_estimate=pl.CostEstimate(flops=6 * 10**10, bytes_accessed=6 * 10**7, transcendentals=10**7),
         name="layers_forward",
-    )(offsets, given, packs, own_gains, given_cot, taps, head, wide, spread)
+    )(offsets, given, packs, given_cot, taps, head, wide, spread)
 
 
 def layers_backward(offsets, cot, totals, scales, before, middle, gains, taps, head, wide, spread, weights, final, saved, span):
@@ -1360,31 +1351,6 @@
         self.each("finish")
 
 
-class TileGather:
-    def __init__(self, own, target, sems):
-        self.own, self.target, self.sems = own, target, sems
-        self.count, self.me = lax.axis_size("dp"), lax.axis_index("dp")
-
-    def remote(self, step):
-        return pltpu.make_async_remote_copy(
-            src_ref=self.own, dst_ref=self.target.at[self.me],
-            send_sem=self.sems.at[step, 0], recv_sem=self.sems.at[step, 1],
-            device_id={"dp": (self.me + step) % self.count}, device_id_type=pl.DeviceIdType.MESH,
-        )
-
-    def start(self):
-        self.target[self.me] = self.own[...]
-
-        @pl.loop(1, self.count)
-        def _(step):
-            self.remote(step).start()
-
-    def wait(self):
-        @pl.loop(1, self.count)
-        def _(step):
-            self.remote(step).wait()
-
-
 class LineReduce:
     def __init__(self, given, out, pair_buf, arrivals, sems):
         self.given, self.out, self.pair_buf = given, out, pair_buf
@@ -1524,40 +1490,44 @@
             LineReduce(
                 packs_ref.at[:, part], pack_ref.at[:, part], pair_buf.at[:, :, part], arrivals.at[:, :, part], line_sems.at[at]
             )
-            for at, part in enumerate((pl.ds(0, cut), pl.ds(cut, pack_ref.shape[1] - cut)))
+            for at, part in enumerate((pl.ds(cut, pack_ref.shape[1] - cut), pl.ds(0, cut)))
         ]
     )
-    dp_smalls = TileGather(small_ref, smalls, small_sems)
+    dp_smalls = LineGather(small_ref, smalls, small_sems)
     shared_smalls = MemberGather(shared, shared_sems)
-    shared_maps = MemberGather(maps, maps_sems)
+    shared_maps = [MemberGather(maps.at[at], maps_sems.at[at]) for at in range(LAYERS)]
+    maps[1, ring.me] = later_ref[:, first_map : first_map + 2 * STATE].astype(BF16)
+    dp_smalls.start()
     line.each("send_pairs")
+    shared_maps[1].start()
     place_all(off_ref, cols_ref, slots)
     bins.start()
-    dp_smalls.start()
 
     @pl.loop(0, line.line - 1)
     def _(step):
+        dp_smalls.stage(step + 1)
         line.stage(step)
 
-    dp_smalls.wait()
-    sum_ref[...] = smalls[0]
-
-    @pl.loop(1, smalls.shape[0])
+    dp_smalls.finish()
+    small_rows = sum_ref.shape[0]
+    sum_ref[...] = smalls[:small_rows, :]
+
+    @pl.loop(1, 2 * line.line)
     def _(at):
-        sum_ref[...] += smalls[at]
+        sum_ref[...] += smalls[pl.ds(at * small_rows, small_rows), :]
 
     shared[ring.me] = sum_ref[...]
     shared_smalls.start()
-    line.finish()
-    maps[ring.me, 0] = pack_ref[:, first_map : first_map + 2 * STATE].astype(BF16)
-    maps[ring.me, 1] = later_ref[:, first_map : first_map + 2 * STATE].astype(BF16)
-    shared_maps.start()
+    line.parts[0].finish()
+    maps[0, ring.me] = pack_ref[:, first_map : first_map + 2 * STATE].astype(BF16)
+    shared_maps[0].start()
     shared_smalls.wait()
     shared_ref[...] = (shared[0] + shared[1]) + (shared[2] + shared[3])
-    shared_maps.wait()
+    line.parts[1].finish()
     for layer in range(LAYERS):
-        maps_ref[layer] = (maps[0, layer].astype(F32) + maps[1, layer].astype(F32)) + (
-            maps[2, layer].astype(F32) + maps[3, layer].astype(F32)
+        shared_maps[layer].wait()
+        maps_ref[layer] = (maps[layer, 0].astype(F32) + maps[layer, 1].astype(F32)) + (
+            maps[layer, 2].astype(F32) + maps[layer, 3].astype(F32)
         )
     bins.wait()
 
@@ -1583,13 +1553,13 @@
         + line_scratch(count, pack_rows, total)[:2]
         + [
             pltpu.SemaphoreType.DMA((2, 5, count // 2)),
-            pltpu.VMEM((count,) + small.shape, F32),
+            pltpu.VMEM((count * small.shape[0], width), F32),
             pltpu.VMEM((4,) + small.shape, F32),
-            pltpu.VMEM((4, LAYERS, pack_rows, 2 * STATE), BF16),
+            pltpu.VMEM((LAYERS, 4, pack_rows, 2 * STATE), BF16),
             pltpu.SemaphoreType.DMA((count, 2)),
-            pltpu.SemaphoreType.DMA((count, 2)),
+            pltpu.SemaphoreType.DMA((6, count // 2)),
             pltpu.SemaphoreType.DMA((4, 2)),
-            pltpu.SemaphoreType.DMA((4, 2)),
+            pltpu.SemaphoreType.DMA((LAYERS, 4, 2)),
         ],
         compiler_params=pltpu.CompilerParams(
             vmem_limit_bytes=56 * 1024 * 1024, collective_id=3, has_side_effects=True
@@ -1621,10 +1591,11 @@
     given_tokens, given_cot = (array[packing].reshape(by_bin) for array in (tokens, cotangent))
 
     spread = spread_matrix(inner_part, heads_here)
+    last_columns = [jnp.concatenate([w_dt[0], pre_gain.T], axis=1), w_dt[1]]
     packs = []
     for layer in range(LAYERS):
         own = jnp.concatenate(
-            [w_out[layer].T, w_z[layer], w_x[layer], w_bc[layer], pad_to(w_dt[layer], dp_rows, LANES)], axis=1
+            [w_out[layer].T, w_z[layer], w_x[layer], w_bc[layer], pad_to(last_columns[layer], dp_rows, LANES)], axis=1
         )
         taps = jnp.concatenate([conv_x[layer], conv_bc[layer]], axis=1).astype(F32)
         head = jnp.stack([head_params[layer, 0], -jnp.exp(head_params[layer, 1])])
@@ -1633,22 +1604,22 @@
         )
         packs.append((own, pad_to(taps, 8, mixed), pad_to(head, 8, LANES), pad_to(wide, 8, inner_part)))
 
-    own_gains = lax.dynamic_update_slice(
-        jnp.zeros((8, dp_count * dp_rows), F32), pre_gain.astype(F32), (0, bin_index * dp_rows)
-    )
     taps_all, head_all, wide_all = (jnp.stack([pack[at] for pack in packs]) for at in (1, 2, 3))
     (
         rows_all, gate, mixed_in, conv, dt_raw, mixed_out, gained_all, states, first_before, middle, totals, scales,
         final_rows, gains, cot_columns, all_weights,
     ) = layers_forward(
-        bounds, given_tokens, jnp.stack([pack[0] for pack in packs]), own_gains, given_cot,
+        bounds, given_tokens, jnp.stack([pack[0] for pack in packs]), given_cot,
         taps_all, head_all, wide_all, spread,
     )
     grad_columns, small, later_pack, first_packs, activations_back = layers_backward(
         bounds, cot_columns, totals, scales, first_before, middle, gains, taps_all, head_all, wide_all, spread,
         all_weights, final_rows, (gate, mixed_in, conv, dt_raw, mixed_out, states, rows_all, gained_all), pos_here,
     )
-    returned, first_pack, sums, shared, maps = end_exchange(bounds, grad_columns, first_packs, small, later_pack, pos_here)
+    returned, first_pack, sums, shared, maps = end_exchange(
+        bounds, grad_columns, first_packs, small.reshape(LAYERS * 8, -1), later_pack, pos_here
+    )
+    sums, shared = sums.reshape(small.shape), shared.reshape(small.shape)
     grad_convx = sums[:, : CONV + 1, :inner_part]
     grad_convbc = shared[:, : CONV + 1, inner_part:mixed]
     shard_pre = lax.dynamic_slice_in_dim(shared[:, 5], bin_index * dp_rows, dp_rows, 1)

time: 478 us -> 469 us (0.981)
  Pallas kernels: 438 us -> 430 us
    pallas_call x1, Pallas kernels: 194 us -> 187 us  [layers_forward(): pl.pallas_call(forward_kernel, grid=(steps,), in_specs=[pl.BlockSpec(memo...]
    unnamed x55 -> x53, local copies, waits for them, and re-layouts: 13.6 us -> 12.9 us
where the time goes in v6:
time: 469 us
  Pallas kernels  430 us (92%)
  local copies, waits for them, and re-layouts  31.9 us (7%)
  other arithmetic  6.07 us (1%)
    pallas_call x1, Pallas kernels, layers_forward(): pl.pallas_call(forward_kernel, grid=(steps,), in_specs=[pl.BlockSpec(memo...  187 us
    pallas_call x1, Pallas kernels, layers_backward(): pl.pallas_call(backward_kernel, grid=(steps,), in_specs=[pl.BlockSpec(mem...  160 us
    pallas_call x1, Pallas kernels, end_exchange(): pl.pallas_call(end_kernel, in_specs=[pl.BlockSpec(memory_space=pltpu.SMEM...  82.7 us
    unnamed x53, local copies, waits for them, and re-layouts  12.9 us

profile of v6, /device:TPU:1, one launch (start us, length us, event | category | flops | bytes accessed | tf_op | source)
XLA Modules:
  0.0 468.6 jit_solution(12145796194182508124)
XLA Ops:
  0.7 0.8 compare_select_fusion.1
  1.5 0.6 scatter_custom_fusion
  2.2 0.8 slice_bitcast_fusion.2
  3.3 0.7 slice_bitcast_fusion
  4.0 0.7 pad_maximum_fusion.4
  4.6 0.8 slice_convert_fusion.1
  5.4 1.4 gather_fusion
  7.2 0.8 fusion.26
  8.0 0.8 fusion.25
  10.0 1.8 gather_fusion.2
  11.8 3.2 gather_fusion.1
  15.1 186.6 %layers_forward.1 = (bf16[4096,1024]{1,0:T(8,128)(2,1)}, bf16[4096,512]{1,0:T(8,128)(2,1)}, bf16[4096,768]{1,0:T(8,128)(2,1)}, f32[4096,768]{1,0:T(8,128)}, f32[...) custom-call(s32[2]{0:T(128)S(1)} %slice_bitcast_fusion.5.off_ref, ...), custom_call_target="tpu_custom_call" | custom-call | flops 60000002048 | bytes 60000000 | tf_op jit(solution)/shard_map/layers_forward/pallas_call | solution.py:1060
  201.7 1.0 copy-done.7
  202.6 1.0 copy-done.8
  203.6 1.0 copy-done.9
  204.6 1.0 copy-done.10
  205.6 0.8 copy-done.11
  206.4 0.6 copy-done.12
  207.0 160.3 %layers_backward.1 = (bf16[8,256,256]{2,1,0:T(8,128)(2,1)}, f32[2,8,1024]{2,1,0:T(8,128)}, f32[128,1920]{1,0:T(8,128)}, bf16[1024,1920]{1,0:T(8,128)(2,1)}, bf16[8,3,128,256]{3,2,1,0:T(8,128)(2,1)}) custom-call(s32[2]{0:T(128)} %copy-done.6, bf16[8,256,256]{2,1,0:T(8,128)(2,1)} %copy-done.10, bf16[16,64,1024]{2,1,0:T(8,128)(2,1)} %get-tuple-element.39.tot_in, ...), custom_call_target="tpu_custom_call" | custom-call | flops 60000002048 | bytes 60000000 | tf_op jit(solution)/shard_map/layers_backward/pallas_call | solution.py:1132
  367.3 3.2 gather_fusion.3
  370.6 82.7 %end_exchange.1 = (bf16[8,3,128,256]{3,2,1,0:T(8,128)(2,1)}, f32[128,1920]{1,0:T(8,128)}, f32[16,1024]{1,0:T(8,128)}, f32[16,1024]{1,0:T(8,128)}, f32[2,128,256]{2,1,0:T(8,128)}) custom-call(s32[2]{0:T(128)} %copy-done.6, bf16[2048,256]{1,0:T(8,128)(2,1)} %bitcast.102, bf16[1024,1920]{1,0:T(8,128)(2,1)} %get-tuple-element.56.packs_ref, ...), custom_call_target="tpu_custom_call" | custom-call | flops 60000002048 | bytes 60000000 | tf_op jit(solution)/shard_map/end_exchange/pallas_call | solution.py:1541
  453.3 3.4 gather_fusion.4
  456.7 0.8 slice.150
  457.5 0.7 slice.158
  458.8 0.6 copy.81
  459.5 0.6 copy.80
  460.1 0.6 copy.90
  461.4 0.7 fusion.3
  462.1 1.2 fusion.2
  463.3 1.6 copy.71
  464.9 2.0 copy.72
  466.9 1.7 copy.100
  (79 shorter events, 3.1 us)
Async XLA Ops:
  0.6 9.3 %copy-start = (bf16[24,128,256]{2,1,0:T(8,128)(2,1)S(1)}, bf16[24,128,256]{2,1,0:T(8,128)(2,1)}, u32[]{:S(2)}) copy-start(bf16[24,128,256]{2,1,0:T(8,128)(2,1)} %param.15) | copy-start | bytes 4718596
  0.7 8.7 %copy-start.15 = (bf16[2,512,128]{2,1,0:T(8,128)(2,1)S(1)}, bf16[2,512,128]{2,1,0:T(8,128)(2,1)}, u32[]{:S(2)}) copy-start(bf16[2,512,128]{2,1,0:T(8,128)(2,1)} %param.27) | copy-start | bytes 786436
  0.7 9.0 %copy-start.16 = (bf16[2,128,512]{2,1,0:T(8,128)(2,1)S(1)}, bf16[2,128,512]{2,1,0:T(8,128)(2,1)}, u32[]{:S(2)}) copy-start(bf16[2,128,512]{2,1,0:T(8,128)(2,1)} %param.19) | copy-start | bytes 786436
  5.4 4.3 copy-start.17
  7.1 7.9 %copy-start.6 = (s32[2]{0:T(128)}, s32[2]{0:T(128)S(1)}, u32[]{:S(2)}) copy-start(s32[2]{0:T(128)S(1)} %slice_bitcast_fusion.5.off_ref) | copy-start | bytes 28
  7.2 7.9 %copy-start.5 = (f32[2,8,128]{2,1,0:T(8,128)}, f32[2,8,128]{2,1,0:T(8,128)S(1)}, u32[]{:S(2)}) copy-start(f32[2,8,128]{2,1,0:T(8,128)S(1)} %pad_maximum_fusion.3.head_ref) | copy-start | bytes 24580
  8.8 0.9 copy-start.18
  8.9 6.2 %copy-start.3 = (f32[2,8,768]{2,1,0:T(8,128)}, f32[2,8,768]{2,1,0:T(8,128)S(1)}, u32[]{:S(2)}) copy-start(f32[2,8,768]{2,1,0:T(8,128)S(1)} %maximum_convert_fusion.taps_ref) | copy-start | bytes 147460
  8.9 6.1 %copy-start.4 = (f32[2,8,512]{2,1,0:T(8,128)}, f32[2,8,512]{2,1,0:T(8,128)S(1)}, u32[]{:S(2)}) copy-start(f32[2,8,512]{2,1,0:T(8,128)S(1)} %pad_maximum_fusion.2.wide_ref) | copy-start | bytes 98308
  9.4 5.7 %copy-start.2 = (bf16[256,512]{1,0:T(8,128)(2,1)}, bf16[256,512]{1,0:T(8,128)(2,1)S(1)}, u32[]{:S(2)}) copy-start(bf16[256,512]{1,0:T(8,128)(2,1)S(1)} %select_convert_fusion.spread_ref) | copy-start | bytes 786436
  201.6 1.0 copy-start.7
  202.6 1.0 copy-start.8
  203.6 1.0 copy-start.9
  204.6 1.0 copy-start.10
  205.6 0.8 copy-start.11
  206.4 0.6 copy-start.12
  453.3 3.4 copy-start.19
  453.3 8.2 %copy-start.13 = (f32[128,1920]{1,0:T(8,128)S(1)}, f32[128,1920]{1,0:T(8,128)}, u32[]{:S(2)}) copy-start(f32[128,1920]{1,0:T(8,128)} %get-tuple-element.58.later_ref) | copy-start | bytes 2949124
  453.3 8.2 %copy-start.14 = (f32[128,1920]{1,0:T(8,128)S(1)}, f32[128,1920]{1,0:T(8,128)}, u32[]{:S(2)}) copy-start(f32[128,1920]{1,0:T(8,128)} %get-tuple-element.61) | copy-start | bytes 2949124
  462.1 6.5 %copy-start.1 = (bf16[24,128,256]{2,1,0:T(8,128)(2,1)S(1)}, bf16[24,128,256]{2,1,0:T(8,128)(2,1)}, u32[]{:S(2)}) copy-start(bf16[24,128,256]{2,1,0:T(8,128)(2,1)} %param.15) | copy-start | bytes 4718596

commit v7 on v6

--- a/solution.py
+++ b/solution.py
@@ -1260,10 +1260,10 @@
         )
 
     def right(self, place, own=False):
-        return self.copy(0, place, (self.high + 1) * 2 + self.low, own)
+        return self.copy(0, place, (self.high + 1) % self.line * 2 + self.low, own)
 
     def left(self, place, own=False):
-        return self.copy(1, place, (self.high - 1) * 2 + self.low, own)
+        return self.copy(1, place, (self.high + self.line - 1) % self.line * 2 + self.low, own)
 
     def pair(self, place, own=False):
         return self.copy(2, place, self.high * 2 + 1 - self.low, own)
@@ -1372,7 +1372,7 @@
 
     def onward(self, place, right):
         slot = place + 1 if right else place
-        other = (self.high + 1 if right else self.high - 1) * 2 + self.low
+        other = (self.high + (1 if right else self.line - 1)) % self.line * 2 + self.low
         return pltpu.make_async_remote_copy(
             src_ref=self.pair_buf.at[place], dst_ref=self.arrivals.at[slot],
             send_sem=self.sems.at[2, place], recv_sem=self.sems.at[3 if right else 4, place],

time: 469 us -> 469 us (level)
  no operation moved by 1% of the time
where the time goes in v7:
time: 469 us
  Pallas kernels  430 us (92%)
  local copies, waits for them, and re-layouts  31.9 us (7%)
  other arithmetic  6.07 us (1%)
    pallas_call x1, Pallas kernels, layers_forward(): pl.pallas_call(forward_kernel, grid=(steps,), in_specs=[pl.BlockSpec(memo...  187 us
    pallas_call x1, Pallas kernels, layers_backward(): pl.pallas_call(backward_kernel, grid=(steps,), in_specs=[pl.BlockSpec(mem...  160 us
    pallas_call x1, Pallas kernels, end_exchange(): pl.pallas_call(end_kernel, in_specs=[pl.BlockSpec(memory_space=pltpu.SMEM...  82.7 us
    unnamed x53, local copies, waits for them, and re-layouts  12.9 us

profile of v7, /device:TPU:1, one launch (start us, length us, event | category | flops | bytes accessed | tf_op | source)
XLA Modules:
  0.0 468.6 jit_solution(526914381710118805)
XLA Ops:
  0.7 0.8 compare_select_fusion.1
  1.5 0.6 scatter_custom_fusion
  2.2 0.8 slice_bitcast_fusion.2
  3.3 0.7 slice_bitcast_fusion
  4.0 0.7 pad_maximum_fusion.4
  4.6 0.8 slice_convert_fusion.1
  5.4 1.4 gather_fusion
  7.2 0.8 fusion.26
  8.0 0.8 fusion.25
  10.0 1.8 gather_fusion.2
  11.8 3.2 gather_fusion.1
  15.1 186.6 %layers_forward.1 = (bf16[4096,1024]{1,0:T(8,128)(2,1)}, bf16[4096,512]{1,0:T(8,128)(2,1)}, bf16[4096,768]{1,0:T(8,128)(2,1)}, f32[4096,768]{1,0:T(8,128)}, f32[...) custom-call(s32[2]{0:T(128)S(1)} %slice_bitcast_fusion.5.off_ref, ...), custom_call_target="tpu_custom_call" | custom-call | flops 60000002048 | bytes 60000000 | tf_op jit(solution)/shard_map/layers_forward/pallas_call | solution.py:1060
  201.7 1.0 copy-done.7
  202.6 1.0 copy-done.8
  203.6 1.0 copy-done.9
  204.6 1.0 copy-done.10
  205.6 0.8 copy-done.11
  206.4 0.6 copy-done.12
  207.0 160.2 %layers_backward.1 = (bf16[8,256,256]{2,1,0:T(8,128)(2,1)}, f32[2,8,1024]{2,1,0:T(8,128)}, f32[128,1920]{1,0:T(8,128)}, bf16[1024,1920]{1,0:T(8,128)(2,1)}, bf16[8,3,128,256]{3,2,1,0:T(8,128)(2,1)}) custom-call(s32[2]{0:T(128)} %copy-done.6, bf16[8,256,256]{2,1,0:T(8,128)(2,1)} %copy-done.10, bf16[16,64,1024]{2,1,0:T(8,128)(2,1)} %get-tuple-element.39.tot_in, ...), custom_call_target="tpu_custom_call" | custom-call | flops 60000002048 | bytes 60000000 | tf_op jit(solution)/shard_map/layers_backward/pallas_call | solution.py:1132
  367.3 3.2 gather_fusion.3
  370.5 82.7 %end_exchange.1 = (bf16[8,3,128,256]{3,2,1,0:T(8,128)(2,1)}, f32[128,1920]{1,0:T(8,128)}, f32[16,1024]{1,0:T(8,128)}, f32[16,1024]{1,0:T(8,128)}, f32[2,128,256]{2,1,0:T(8,128)}) custom-call(s32[2]{0:T(128)} %copy-done.6, bf16[2048,256]{1,0:T(8,128)(2,1)} %bitcast.102, bf16[1024,1920]{1,0:T(8,128)(2,1)} %get-tuple-element.56.packs_ref, ...), custom_call_target="tpu_custom_call" | custom-call | flops 60000002048 | bytes 60000000 | tf_op jit(solution)/shard_map/end_exchange/pallas_call | solution.py:1541
  453.3 3.4 gather_fusion.4
  456.7 0.8 slice.150
  457.5 0.7 slice.158
  458.8 0.6 copy.81
  459.4 0.6 copy.80
  460.1 0.6 copy.90
  461.4 0.7 fusion.3
  462.1 1.2 fusion.2
  463.3 1.6 copy.71
  464.9 2.0 copy.72
  466.9 1.7 copy.100
  (79 shorter events, 3.1 us)
Async XLA Ops:
  0.6 9.3 %copy-start = (bf16[24,128,256]{2,1,0:T(8,128)(2,1)S(1)}, bf16[24,128,256]{2,1,0:T(8,128)(2,1)}, u32[]{:S(2)}) copy-start(bf16[24,128,256]{2,1,0:T(8,128)(2,1)} %param.15) | copy-start | bytes 4718596
  0.7 8.7 %copy-start.15 = (bf16[2,512,128]{2,1,0:T(8,128)(2,1)S(1)}, bf16[2,512,128]{2,1,0:T(8,128)(2,1)}, u32[]{:S(2)}) copy-start(bf16[2,512,128]{2,1,0:T(8,128)(2,1)} %param.27) | copy-start | bytes 786436
  0.7 9.0 %copy-start.16 = (bf16[2,128,512]{2,1,0:T(8,128)(2,1)S(1)}, bf16[2,128,512]{2,1,0:T(8,128)(2,1)}, u32[]{:S(2)}) copy-start(bf16[2,128,512]{2,1,0:T(8,128)(2,1)} %param.19) | copy-start | bytes 786436
  5.4 4.3 copy-start.17
  7.1 7.9 %copy-start.6 = (s32[2]{0:T(128)}, s32[2]{0:T(128)S(1)}, u32[]{:S(2)}) copy-start(s32[2]{0:T(128)S(1)} %slice_bitcast_fusion.5.off_ref) | copy-start | bytes 28
  7.2 7.9 %copy-start.5 = (f32[2,8,128]{2,1,0:T(8,128)}, f32[2,8,128]{2,1,0:T(8,128)S(1)}, u32[]{:S(2)}) copy-start(f32[2,8,128]{2,1,0:T(8,128)S(1)} %pad_maximum_fusion.3.head_ref) | copy-start | bytes 24580
  8.8 0.9 copy-start.18
  8.9 6.2 %copy-start.3 = (f32[2,8,768]{2,1,0:T(8,128)}, f32[2,8,768]{2,1,0:T(8,128)S(1)}, u32[]{:S(2)}) copy-start(f32[2,8,768]{2,1,0:T(8,128)S(1)} %maximum_convert_fusion.taps_ref) | copy-start | bytes 147460
  8.9 6.1 %copy-start.4 = (f32[2,8,512]{2,1,0:T(8,128)}, f32[2,8,512]{2,1,0:T(8,128)S(1)}, u32[]{:S(2)}) copy-start(f32[2,8,512]{2,1,0:T(8,128)S(1)} %pad_maximum_fusion.2.wide_ref) | copy-start | bytes 98308
  9.4 5.7 %copy-start.2 = (bf16[256,512]{1,0:T(8,128)(2,1)}, bf16[256,512]{1,0:T(8,128)(2,1)S(1)}, u32[]{:S(2)}) copy-start(bf16[256,512]{1,0:T(8,128)(2,1)S(1)} %select_convert_fusion.spread_ref) | copy-start | bytes 786436
  201.7 1.0 copy-start.7
  202.6 1.0 copy-start.8
  203.6 1.0 copy-start.9
  204.6 1.0 copy-start.10
  205.6 0.8 copy-start.11
  206.4 0.6 copy-start.12
  453.2 3.4 copy-start.19
  453.3 8.2 %copy-start.13 = (f32[128,1920]{1,0:T(8,128)S(1)}, f32[128,1920]{1,0:T(8,128)}, u32[]{:S(2)}) copy-start(f32[128,1920]{1,0:T(8,128)} %get-tuple-element.58.later_ref) | copy-start | bytes 2949124
  453.3 8.2 %copy-start.14 = (f32[128,1920]{1,0:T(8,128)S(1)}, f32[128,1920]{1,0:T(8,128)}, u32[]{:S(2)}) copy-start(f32[128,1920]{1,0:T(8,128)} %get-tuple-element.61) | copy-start | bytes 2949124
  462.1 6.5 %copy-start.1 = (bf16[24,128,256]{2,1,0:T(8,128)(2,1)S(1)}, bf16[24,128,256]{2,1,0:T(8,128)(2,1)}, u32[]{:S(2)}) copy-start(bf16[24,128,256]{2,1,0:T(8,128)(2,1)} %param.15) | copy-start | bytes 4718596
